TPU v7x, 32 devices: a whole 2x2x4 slice. The times are simulated.
32 devices in a mesh: blk: 8 (over z, y), rep: 4 (over x, core).
Axes of the slice: x: 2, y: 2, z: 4, core: 2. Of those that a mesh axis runs over, the one named last changes fastest.
Arguments:
- tiles: bfloat16 [8, 32, 128, 128], P('blk', 'rep'), may hold values from -6 to 6
- tile_rows: int32 [8, 32], P('blk', 'rep'), may hold values from 0 to 15
- tile_cols: int32 [8, 32], P('blk', 'rep'), may hold values from 0 to 63
- start_right: float32 [65536, 64], P(('blk', 'rep')), may hold values from -6 to 6
Outputs:
- left_vectors: float32 [16384, 64], P('blk')
- right_vectors: float32 [65536, 64], P(('blk', 'rep'))
All inputs are finite; a program needn't handle non-finite values.
Results may differ from a plain program's by a relative error of at most 0.022.
Values may be sent and summed in bfloat16 or wider, within the bound.
No kernel may reach another device: no remote copies, remote signals or barrier semaphores. Data moves between devices by JAX's collectives and lax.ppermute only.
A program may use at most 64 MiB of HBM per device.

v0:
```python
import math

import jax
import jax.numpy as jnp
from jax import lax
from jax.sharding import PartitionSpec as P

ITERS = 2
ROW_TILES = 16


def gram_of(matrix):
    return jnp.dot(
        matrix.T, matrix, precision=lax.Precision.HIGHEST, preferred_element_type=jnp.float32
    )


def normalize(matrix, gram_matrix):
    factor = jnp.linalg.cholesky(gram_matrix)
    return jax.scipy.linalg.solve_triangular(factor, matrix.T, lower=True).T


def local(tiles, tile_rows, tile_cols, start_right):
    cycle_size = lax.axis_size("blk")
    group_size = lax.axis_size("rep")
    tile_size = tiles.shape[-1]
    block_width = start_right.shape[1]
    share_count = start_right.shape[0]
    flat_tiles = tiles.reshape(-1, tile_size, tile_size)
    local_rows = tile_rows.reshape(-1)
    local_cols = tile_cols.reshape(-1)
    slot_count = local_cols.shape[0] // cycle_size
    piece_tiles = share_count * group_size // tile_size
    total_rows = ROW_TILES * tile_size * cycle_size
    total_cols = piece_tiles * tile_size * cycle_size
    requested = lax.all_to_all(
        local_cols.reshape(cycle_size, slot_count), "blk", split_axis=0, concat_axis=0, tiled=True
    ).reshape(-1)
    right_share = start_right
    right_piece = start_right
    left = jnp.zeros((ROW_TILES * tile_size, block_width), jnp.float32)
    for iteration in range(ITERS):
        if iteration == 0:
            narrow_piece = lax.all_gather(
                start_right.astype(jnp.bfloat16), "rep", axis=0, tiled=True
            )
        else:
            narrow_piece = right_piece.astype(jnp.bfloat16)
        outgoing = narrow_piece.reshape(piece_tiles, tile_size, block_width)[requested]
        chosen = lax.all_to_all(
            outgoing.reshape(cycle_size, slot_count, tile_size, block_width),
            "blk",
            split_axis=0,
            concat_axis=0,
            tiled=True,
        ).reshape(-1, tile_size, block_width)
        products = jnp.einsum(
            "tab,tbk->tak", flat_tiles, chosen, preferred_element_type=jnp.float32
        )
        partial_value = (
            jnp.zeros((ROW_TILES, tile_size, block_width), jnp.float32)
            .at[local_rows]
            .add(products)
            .reshape(-1, block_width)
        )
        left_raw = lax.psum(partial_value.astype(jnp.bfloat16), "rep").astype(jnp.float32)
        gram_left = lax.psum(gram_of(left_raw), "blk")
        left = normalize(left_raw, gram_left)
        left_narrow = left.astype(jnp.bfloat16).reshape(ROW_TILES, tile_size, block_width)
        picked = left_narrow[local_rows]
        transposed = jnp.einsum(
            "tab,tak->tbk", flat_tiles, picked, preferred_element_type=jnp.float32
        )
        returned = (
            lax.all_to_all(
                transposed.reshape(cycle_size, slot_count, tile_size, block_width).astype(
                    jnp.bfloat16
                ),
                "blk",
                split_axis=0,
                concat_axis=0,
                tiled=True,
            )
            .astype(jnp.float32)
            .reshape(-1, tile_size, block_width)
        )
        column_term = (
            jnp.zeros((piece_tiles, tile_size, block_width), jnp.float32)
            .at[requested]
            .add(returned)
            .reshape(-1, block_width)
        )
        right_raw = lax.psum(column_term.astype(jnp.bfloat16), "rep").astype(jnp.float32)
        gram_right = lax.psum(gram_of(right_raw), "blk")
        right_piece = normalize(right_raw, gram_right)
        right_share = lax.dynamic_slice_in_dim(
            right_piece, lax.axis_index("rep") * share_count, share_count, 0
        )
    return (left * math.sqrt(total_rows), right_share * math.sqrt(total_cols))


def solution(mesh):
    in_specs = (
        P("blk", "rep", None, None),
        P("blk", "rep"),
        P("blk", "rep"),
        P(("blk", "rep"), None),
    )
    out_specs = (P("blk", None), P(("blk", "rep"), None))
    return jax.shard_map(local, mesh=mesh, in_specs=in_specs, out_specs=out_specs, check_vma=False)
```

profile of v0, /device:TPU:0, one launch (start us, length us, event | category | flops | bytes accessed | tf_op | source)
XLA Modules:
  0.0 429.5 jit_solution(8003843160552063038)
XLA Ops:
  9.8 13.5 %all_to_all.32 = s32[8,1,1]{2,1,0:T(1,128)S(1)} all-to-all(s32[8,1,1]{2,1,0:T(1,128)S(1)} %copy.66), channel_id=1, replica_groups=mesh['blk'=8,'rep'=4] {'blk'}, dimensions={0} | all-to-all | bytes 64 | tf_op jit(solution)/shard_map/all_to_all | solution.py:36
  23.6 6.0 %all-gather.2.cloned.1.call-done = bf16[8192,64]{0,1:T(8,128)(2,1)} async-done(((bf16[2048,64]{0,1:T(8,128)(2,1)}), bf16[8192,64]{0,1:T(8,128)(2,1)}) %all-gather.2.cloned.1.call-update) | async-done | bytes 1048592 | tf_op jit(solution)/shard_map/all_gather | solution.py:44
  32.4 5.5 %all-to-all-start.1 = ((bf16[8,1,128,64]{2,3,1,0:T(8,128)(2,1)}), bf16[8,1,128,64]{2,3,1,0:T(8,128)(2,1)S(1)}, u32[]{:S(2)}, u32[]{:S(2)}) async-start(bf16[8,1,128,64]{2,3,1,0:T(8,128)(2,1)} %bitcast.5), calls=%async_computation.1 | async-start | bytes 262144 | tf_op jit(solution)/shard_map/all_to_all | solution.py:50
  37.9 7.3 %all-to-all-done.1 = bf16[8,1,128,64]{2,3,1,0:T(8,128)(2,1)S(1)} async-done(((bf16[8,1,128,64]{2,3,1,0:T(8,128)(2,1)}), bf16[8,1,128,64]{2,3,1,0:T(8,128)(2,1)S(1)}, u32[]{:S(2)}, u32[]{:S(2)}) %all-to-all-start.1) | async-done | bytes 131104 | tf_op jit(solution)/shard_map/all_to_all | solution.py:50
  47.3 29.3 %all-reduce.5.cloned.1.call-done = bf16[2048,64]{0,1:T(8,128)(2,1)} async-done(((bf16[2048,64]{0,1:T(8,128)(2,1)}), bf16[2048,64]{0,1:T(8,128)(2,1)}) %all-reduce.5.cloned.1.call-update) | async-done | bytes 262160 | tf_op jit(solution)/shard_map/psum | solution.py:66
  77.8 37.1 %psum.57 = f32[64,64]{0,1:T(8,128)S(1)} all-reduce(f32[64,64]{0,1:T(8,128)S(1)} %fusion.44), channel_id=1, replica_groups=mesh['blk'=8,'rep'=4] {'blk'}, use_global_device_ids=true, to_apply=%region_2.0 | all-reduce | flops 4096 | bytes 32768 | tf_op jit(solution)/shard_map/psum | solution.py:67
  115.0 5.8 %cholesky.74 = f32[64,64]{1,0:T(8,128)S(1)} custom-call(f32[64,64]{1,0:T(8,128)S(1)} %fusion.33), custom_call_target="Cholesky" | custom-call | tf_op jit(solution)/shard_map/jit(cholesky)/cholesky | solution.py:19
  122.2 4.9 %custom-call.10 = f32[1,64,64]{1,2,0:T(8,128)S(1)} custom-call(f32[1,64,64]{2,1,0:T(8,128)S(1)} %fusion.22), custom_call_target="InvertDiagBlocksLowerTriangular" | custom-call | tf_op jit(solution)/shard_map/jit(_solve_triangular)/triangular_solve | solution.py:20
  129.5 9.7 %all_to_all.33 = bf16[8,1,128,64]{2,3,1,0:T(8,128)(2,1)S(1)} all-to-all(bf16[8,1,128,64]{2,3,1,0:T(8,128)(2,1)S(1)} %fusion.9), channel_id=1, replica_groups=mesh['blk'=8,'rep'=4] {'blk'}, dimensions={0} | all-to-all | bytes 262144 | tf_op jit(solution)/shard_map/all_to_all | solution.py:75
  141.7 33.0 %all-reduce.7.cloned.1.call-done = bf16[8192,64]{0,1:T(8,128)(2,1)} async-done(((bf16[8192,64]{0,1:T(8,128)(2,1)}), bf16[8192,64]{0,1:T(8,128)(2,1)}) %all-reduce.7.cloned.1.call-update) | async-done | bytes 1048592 | tf_op jit(solution)/shard_map/psum | solution.py:93
  176.8 37.1 %psum.59 = f32[64,64]{0,1:T(8,128)S(1)} all-reduce(f32[64,64]{0,1:T(8,128)S(1)} %fusion.45), channel_id=1, replica_groups=mesh['blk'=8,'rep'=4] {'blk'}, use_global_device_ids=true, to_apply=%region_7.10 | all-reduce | flops 4096 | bytes 32768 | tf_op jit(solution)/shard_map/psum | solution.py:94
  213.9 5.8 %cholesky.85 = f32[64,64]{1,0:T(8,128)S(1)} custom-call(f32[64,64]{1,0:T(8,128)S(1)} %fusion.31), custom_call_target="Cholesky" | custom-call | tf_op jit(solution)/shard_map/jit(cholesky)/cholesky | solution.py:19
  221.1 4.9 %custom-call.11 = f32[1,64,64]{1,2,0:T(8,128)S(1)} custom-call(f32[1,64,64]{2,1,0:T(8,128)S(1)} %fusion.23), custom_call_target="InvertDiagBlocksLowerTriangular" | custom-call | tf_op jit(solution)/shard_map/jit(_solve_triangular)/triangular_solve | solution.py:20
  228.8 9.7 %all_to_all.34 = bf16[8,1,128,64]{2,3,1,0:T(8,128)(2,1)S(1)} all-to-all(bf16[8,1,128,64]{2,3,1,0:T(8,128)(2,1)S(1)} %bitcast.164), channel_id=1, replica_groups=mesh['blk'=8,'rep'=4] {'blk'}, dimensions={0} | all-to-all | bytes 262144 | tf_op jit(solution)/shard_map/all_to_all | solution.py:50
  240.6 29.3 %all-reduce.9.cloned.1.call-done = bf16[2048,64]{0,1:T(8,128)(2,1)} async-done(((bf16[2048,64]{0,1:T(8,128)(2,1)}), bf16[2048,64]{0,1:T(8,128)(2,1)}) %all-reduce.9.cloned.1.call-update) | async-done | bytes 262160 | tf_op jit(solution)/shard_map/psum | solution.py:66
  271.2 37.1 %psum.61 = f32[64,64]{0,1:T(8,128)S(1)} all-reduce(f32[64,64]{0,1:T(8,128)S(1)} %fusion.46), channel_id=1, replica_groups=mesh['blk'=8,'rep'=4] {'blk'}, use_global_device_ids=true, to_apply=%region_10.0 | all-reduce | flops 4096 | bytes 32768 | tf_op jit(solution)/shard_map/psum | solution.py:67
  308.4 5.8 %cholesky.96 = f32[64,64]{1,0:T(8,128)S(1)} custom-call(f32[64,64]{1,0:T(8,128)S(1)} %fusion.29), custom_call_target="Cholesky" | custom-call | tf_op jit(solution)/shard_map/jit(cholesky)/cholesky | solution.py:19
  315.6 4.9 %custom-call.12 = f32[1,64,64]{1,2,0:T(8,128)S(1)} custom-call(f32[1,64,64]{2,1,0:T(8,128)S(1)} %fusion.24), custom_call_target="InvertDiagBlocksLowerTriangular" | custom-call | tf_op jit(solution)/shard_map/jit(_solve_triangular)/triangular_solve | solution.py:20
  320.5 2.4 convert_bitcast_fusion.2
  323.7 9.7 %all_to_all.35 = bf16[8,1,128,64]{2,3,1,0:T(8,128)(2,1)S(1)} all-to-all(bf16[8,1,128,64]{2,3,1,0:T(8,128)(2,1)S(1)} %fusion.10), channel_id=1, replica_groups=mesh['blk'=8,'rep'=4] {'blk'}, dimensions={0} | all-to-all | bytes 262144 | tf_op jit(solution)/shard_map/all_to_all | solution.py:75
  335.8 33.1 %all-reduce.11.cloned.1.call-done = bf16[8192,64]{0,1:T(8,128)(2,1)} async-done(((bf16[8192,64]{0,1:T(8,128)(2,1)}), bf16[8192,64]{0,1:T(8,128)(2,1)}) %all-reduce.11.cloned.1.call-update) | async-done | bytes 1048592 | tf_op jit(solution)/shard_map/psum | solution.py:93
  371.0 37.1 %psum.63 = f32[64,64]{0,1:T(8,128)S(1)} all-reduce(f32[64,64]{0,1:T(8,128)S(1)} %fusion.47), channel_id=1, replica_groups=mesh['blk'=8,'rep'=4] {'blk'}, use_global_device_ids=true, to_apply=%region_13.17 | all-reduce | flops 4096 | bytes 32768 | tf_op jit(solution)/shard_map/psum | solution.py:94
  408.1 5.8 %cholesky.107 = f32[64,64]{1,0:T(8,128)S(1)} custom-call(f32[64,64]{1,0:T(8,128)S(1)} %fusion.27), custom_call_target="Cholesky" | custom-call | tf_op jit(solution)/shard_map/jit(cholesky)/cholesky | solution.py:19
  415.3 4.9 %custom-call.13 = f32[1,64,64]{1,2,0:T(8,128)S(1)} custom-call(f32[1,64,64]{2,1,0:T(8,128)S(1)} %fusion.25), custom_call_target="InvertDiagBlocksLowerTriangular" | custom-call | tf_op jit(solution)/shard_map/jit(_solve_triangular)/triangular_solve | solution.py:20
  (79 shorter events, 35.3 us)
Async XLA Ops:
  7.2 38.1 %copy-start = (bf16[1,8,128,128]{3,2,1,0:T(8,128)(2,1)S(1)}, bf16[1,8,128,128]{3,2,1,0:T(8,128)(2,1)}, u32[]{:S(2)}) copy-start(bf16[1,8,128,128]{3,2,1,0:T(8,128)(2,1)} %param.9) | copy-start | bytes 786436
  7.2 30.7 %copy-start.3 = (s32[1,8]{1,0:T(1,128)S(1)}, s32[1,8]{1,0:T(1,128)}, u32[]{:S(2)}) copy-start(s32[1,8]{1,0:T(1,128)} %param.10) | copy-start | bytes 100
  7.2 22.4 %all-gather.2.cloned.1.call-start = ((), (), s32[]{:S(2)}) async-start(), calls=%async_computation.5 | async-start | bytes 1310720 | tf_op jit(solution)/shard_map/all_gather | solution.py:44
  32.4 12.9 %all-to-all-start.1 = ((bf16[8,1,128,64]{2,3,1,0:T(8,128)(2,1)}), bf16[8,1,128,64]{2,3,1,0:T(8,128)(2,1)S(1)}, u32[]{:S(2)}, u32[]{:S(2)}) async-start(bf16[8,1,128,64]{2,3,1,0:T(8,128)(2,1)} %bitcast.5), calls=%async_computation.1 | async-start | bytes 262144 | tf_op jit(solution)/shard_map/all_to_all | solution.py:50
  37.9 38.7 %all-reduce.5.cloned.1.call-start = ((), (), s32[]{:S(2)}) async-start(), calls=%async_computation.6 | async-start | bytes 524288 | tf_op jit(solution)/shard_map/psum | solution.py:66
  47.3 127.5 %all-reduce.7.cloned.1.call-start = ((), (), s32[]{:S(2)}) async-start(), calls=%async_computation.7 | async-start | bytes 2097152 | tf_op jit(solution)/shard_map/psum | solution.py:93
  141.6 128.3 %all-reduce.9.cloned.1.call-start = ((), (), s32[]{:S(2)}) async-start(), calls=%async_computation.8 | async-start | bytes 524288 | tf_op jit(solution)/shard_map/psum | solution.py:66
  174.7 51.3 %copy-start.2 = (bf16[8192,64]{0,1:T(8,128)(2,1)S(1)}, bf16[8192,64]{0,1:T(8,128)(2,1)}, u32[]{:S(2)}) copy-start(bf16[8192,64]{0,1:T(8,128)(2,1)} %all-reduce.7.cloned.1.call-done) | copy-start | bytes 3145732
  240.5 128.4 %all-reduce.11.cloned.1.call-start = ((), (), s32[]{:S(2)}) async-start(), calls=%async_computation.9 | async-start | bytes 2097152 | tf_op jit(solution)/shard_map/psum | solution.py:93
  368.9 51.3 %copy-start.1 = (bf16[8192,64]{0,1:T(8,128)(2,1)S(1)}, bf16[8192,64]{0,1:T(8,128)(2,1)}, u32[]{:S(2)}) copy-start(bf16[8192,64]{0,1:T(8,128)(2,1)} %all-reduce.11.cloned.1.call-done) | copy-start | bytes 3145732
Sparse Core Ops, SparseCore 0:
  10.2 19.4 all-gather.1
  47.4 29.1 all-reduce.4
  141.8 32.9 all-reduce.6
  240.7 29.2 all-reduce.8
  335.9 32.9 all-reduce.10
where the time goes:
time: 430 us
  blocking collectives  191 us (44%)
  waiting for transfers between devices  138 us (32%)
  other arithmetic  58.6 us (14%)
  matrix products  15.2 us (4%)
  between operations  14.1 us (3%)
  local copies, waits for them, and re-layouts  6.53 us (2%)
  starting transfers between devices  5.73 us (1%)
    psum x2, blocking collectives, local(): gram_left = lax.psum(gram_of(left_raw), 'blk')  74.2 us
    psum x2, blocking collectives, local(): gram_right = lax.psum(gram_of(right_raw), 'blk')  74.2 us
    psum x2, waiting for transfers between devices, local(): lax.psum(column_term.astype(jnp.bfloat16), 'rep').astype(jnp.float32)  66.1 us
    psum x2, waiting for transfers between devices, local(): lax.psum(partial_value.astype(jnp.bfloat16), 'rep').astype(jnp.float32)  58.6 us
    another operation x12, other arithmetic, normalize(): factor = jnp.linalg.cholesky(gram_matrix)  26.1 us
    another operation x8, other arithmetic, normalize(): return jax.scipy.linalg.solve_triangular(factor, matrix.T, lower=True).T  22.2 us
    all_to_all x2, blocking collectives, local(): lax.all_to_all(transposed.reshape(cycle_size, slot_count, tile_size, bloc...  19.5 us
    all_to_all x1, blocking collectives, local(): lax.all_to_all(local_cols.reshape(cycle_size, slot_count), 'blk', split_a...  13.5 us
  transfers between devices with their start and end apart: 6, of which 6 were waited for; matrix products, arithmetic and copies ran while one was open for 0% of the time, Pallas kernels for 0%

commit v1 on v0

v1 whole, which is shorter than its diff:
```python
import functools
import math

import jax
import jax.numpy as jnp
from jax import lax
from jax.experimental import pallas as pl
from jax.experimental.pallas import tpu as pltpu
from jax.sharding import PartitionSpec as P

ITERS = 2
ROW_TILES = 16
F32 = jnp.float32
BF16 = jnp.bfloat16
VMEM_BYTES = 48 * 1024 * 1024
NT = (((1,), (1,)), ((), ()))
NN = (((1,), (0,)), ((), ()))


def dot(a, b, dims):
    return lax.dot_general(a, b, dims, preferred_element_type=F32)


def split3(value):
    high = value.astype(BF16)
    rest = value - high.astype(F32)
    middle = rest.astype(BF16)
    low = (rest - middle.astype(F32)).astype(BF16)
    return high, middle, low


def gram_of(value):
    width = value.shape[0]
    high, middle, low = split3(value)
    parts = jnp.concatenate([high, middle, low], axis=0)
    full = dot(parts, parts, NT)

    def block(i, j):
        return full[i * width : (i + 1) * width, j * width : (j + 1) * width]

    small = block(1, 1) + block(0, 2) + block(2, 0)
    return block(0, 0) + (block(0, 1) + block(1, 0) + small)


def eliminate(work):
    size = work.shape[0]
    for k in range(size // 8):
        at = size + 8 * k
        panel = work[8 * k : 8 * k + 8, :]
        shape = panel.shape
        cols = [jnp.broadcast_to(panel[:, at + s : at + s + 1], shape) for s in range(8)]
        d = {(i, s): jnp.broadcast_to(cols[s][i : i + 1, :], shape) for s in range(8) for i in range(s, 8)}
        rows = [jnp.broadcast_to(panel[s : s + 1, :], shape) for s in range(8)]
        inverse = [None] * 8
        lower = {}
        for s in range(8):
            inverse[s] = 1.0 / d[s, s]
            for i in range(s + 1, 8):
                lower[i, s] = d[i, s] * inverse[s]
            for i in range(s + 1, 8):
                for j in range(s + 1, i + 1):
                    d[i, j] = d[i, j] - lower[i, s] * d[j, s]
                rows[i] = rows[i] - lower[i, s] * rows[s]
        solved = [None] * 8
        for s in reversed(range(8)):
            solved[s] = rows[s] * inverse[s]
            for i in range(s + 1, 8):
                solved[s] = solved[s] - lower[i, s] * solved[i]
        for i in range(k + 1, size // 8):
            rest = work[8 * i : 8 * i + 8, :]
            updated = rest
            for s in range(8):
                updated = updated - jnp.broadcast_to(rest[:, at + s : at + s + 1], shape) * solved[s]
            work[8 * i : 8 * i + 8, :] = updated
        for s in range(8):
            work[8 * k + s : 8 * k + s + 1, :] = (rows[s] * lax.rsqrt(d[s, s]))[0:1, :]


def put_identity(work):
    size = work.shape[0]
    row = lax.broadcasted_iota(jnp.int32, (size, size), 0)
    column = lax.broadcasted_iota(jnp.int32, (size, size), 1)
    work[:, 0:size] = jnp.where(row == column, 1.0, 0.0).astype(F32)


def pack_half_gram(gram_half):
    high, middle, low = split3(gram_half)
    half = gram_half.shape[0] // 2
    return jnp.concatenate(
        [
            jnp.concatenate([high, middle], axis=1),
            jnp.concatenate([low[0:half], low[half:]], axis=1),
        ],
        axis=0,
    )


def unpack_half_gram(ref, at, width):
    half = width // 2
    total = jnp.zeros((half, width), F32)
    top = jnp.zeros((half, 2 * width), F32)
    bottom = jnp.zeros((half // 2, 2 * width), F32)
    for b in range(ref.shape[0]):
        top = top + ref[b, at : at + half, :].astype(F32)
        bottom = bottom + ref[b, at + half : at + half + half // 2, :].astype(F32)
    total = top[:, 0:width] + top[:, width:]
    return total + jnp.concatenate([bottom[:, 0:width], bottom[:, width:]], axis=0)


def factor(work, own_ref, other_ref, core, at, width):
    half = width // 2
    put_identity(work)
    work[pl.ds(pl.multiple_of(core * half, half), half), width : 2 * width] = unpack_half_gram(own_ref, at, width)
    work[pl.ds(pl.multiple_of((1 - core) * half, half), half), width : 2 * width] = unpack_half_gram(
        other_ref, at, width
    )
    eliminate(work)
    return work[:, 0:width]


def normalise_tile(scale_parts, tile):
    width = tile.shape[0]
    both = dot(scale_parts, tile, NN)
    return (both[0:width] + both[width:]).astype(BF16)


def two_parts(scale):
    high = scale.astype(BF16)
    return jnp.concatenate([high, (scale - high.astype(F32)).astype(BF16)], axis=0)


def choose_kernel(cols_ref, place_ref, own_ref, near_ref, out_ref):
    rep = place_ref[0]
    core = lax.rem(rep, 2)
    tile = own_ref.shape[2] // place_share(own_ref)
    per_share = own_ref.shape[2] // tile
    blocks = out_ref.shape[0]
    width = own_ref.shape[1]
    for b in range(blocks):
        for x in range(2):
            col = cols_ref[b, x * 2 + core]
            share = lax.div(col, per_share)
            at = pl.multiple_of(lax.rem(col, per_share) * tile, tile)
            away = lax.bitwise_xor(share, rep)
            same_core = lax.rem(away, 2) == 0
            far = lax.div(away, 2)
            mine = own_ref[far, :, pl.ds(at, tile)]
            theirs = near_ref[far, :, pl.ds(at, tile)]
            out_ref[b, x * width : (x + 1) * width, :] = jnp.where(same_core, mine, theirs)


def place_share(ref):
    return ref.shape[2] // 128


def left_kernel(first, rows_ref, place_ref, tiles_ref, own_ref, other_ref, out_ref, raw_ref, work):
    core = lax.rem(place_ref[0], 2)
    pieces = own_ref.shape[0]
    width = raw_ref.shape[0]
    tile = tiles_ref.shape[-1]
    if not first:
        scale = two_parts(factor(work, own_ref, other_ref, core, 2 * width, width))
    raw_ref[...] = jnp.zeros_like(raw_ref)
    for source, at_core in ((own_ref, core), (other_ref, 1 - core)):
        for x in range(2):
            rep = x * 2 + at_core

            def add(p, source=source, x=x, rep=rep):
                chosen = source[p, x * width : (x + 1) * width, :]
                if not first:
                    chosen = normalise_tile(scale, chosen)
                product = dot(chosen, tiles_ref[rep, p], NT)
                at = pl.multiple_of(rows_ref[rep, p] * tile, tile)
                raw_ref[:, pl.ds(at, tile)] += product

            each(pieces, add)
    gram = gram_of(raw_ref[...])
    half = width // 2
    work[:, width : 2 * width] = gram
    packed = pack_half_gram(work[pl.ds(pl.multiple_of(core * half, half), half), width : 2 * width])

    def send(p):
        for x in range(2):
            at = pl.multiple_of(rows_ref[x * 2 + core, p] * tile, tile)
            out_ref[p, x * width : (x + 1) * width, :] = raw_ref[:, pl.ds(at, tile)].astype(BF16)
        out_ref[p, 2 * width :, :] = packed

    each(pieces, send)


def each(count, body):
    if count <= 8:
        for i in range(count):
            body(i)
    else:
        lax.fori_loop(0, count // 8, lambda o, c: [body(o * 8 + i) for i in range(8)] and c, 0)


def right_kernel(last, cols_ref, fresh_ref, place_ref, tiles_ref, own_ref, other_ref, out_ref, *rest):
    if last:
        share_ref, scale_ref, raw, stacked, work = rest
    else:
        raw, stacked, work = rest
    core = lax.rem(place_ref[0], 2)
    blocks = own_ref.shape[0]
    width = raw.shape[1]
    tile = raw.shape[2]
    full_scale = factor(work, own_ref, other_ref, core, 2 * width, width)
    if last:
        scale_ref[...] = full_scale
    scale = two_parts(full_scale)
    raw[...] = jnp.zeros_like(raw)
    for source, at_core in ((own_ref, core), (other_ref, 1 - core)):
        for x in range(2):
            rep = x * 2 + at_core

            def add(b, source=source, x=x, rep=rep):
                chosen = normalise_tile(scale, source[b, x * width : (x + 1) * width, :])
                raw[cols_ref[b, rep]] += dot(chosen, tiles_ref[rep, b, 0:tile, :], NN)

            each(blocks, add)
    gram = jnp.zeros((width, width), F32)
    half = width // 2

    def take(b, base):
        for rep in range(4):
            value = raw[cols_ref[b, rep]] * fresh_ref[b, rep].astype(F32)
            at = (b * 4 + rep - base) * tile
            if not isinstance(at, int):
                at = pl.multiple_of(at, tile)
            high, middle, low = split3(value)
            stacked[0:width, pl.ds(at, tile)] = high
            stacked[width : 2 * width, pl.ds(at, tile)] = middle
            stacked[2 * width :, pl.ds(at, tile)] = low

    def add_gram(base):
        for b in range(8):
            take(base + b, base * 4)
        parts = stacked[...]
        full = dot(parts, parts, NT)

        def block(i, j):
            return full[i * width : (i + 1) * width, j * width : (j + 1) * width]

        small = block(1, 1) + block(0, 2) + block(2, 0)
        return block(0, 0) + (block(0, 1) + block(1, 0) + small)

    if blocks == 8:
        gram = add_gram(0)
    else:
        gram = lax.fori_loop(0, blocks // 8, lambda o, g: g + add_gram(o * 8), gram)
    if last:
        both = jnp.concatenate([gram[0:half], gram[half:]], axis=1)

        def send(b):
            out_ref[b] = both

        each(blocks, send)
        shares = share_ref.shape[1] // tile
        for i in range(shares):
            share_ref[:, i * tile : (i + 1) * tile] = raw[place_ref[0] * shares + i]
        return
    work[:, width : 2 * width] = gram
    packed = pack_half_gram(work[pl.ds(pl.multiple_of(core * half, half), half), width : 2 * width])

    def send(b):
        for x in range(2):
            out_ref[b, x * width : (x + 1) * width, :] = raw[cols_ref[b, x * 2 + core]].astype(BF16)
        out_ref[b, 2 * width :, :] = packed

    each(blocks, send)


def finish_kernel(left_factor, right_factor, gram_ref, scale_ref, left_ref, share_ref, left_out, right_out, work):
    width = left_ref.shape[0]
    half = width // 2
    total = gram_ref[0]
    for b in range(1, gram_ref.shape[0]):
        total = total + gram_ref[b]
    put_identity(work)
    work[0:half, width : 2 * width] = total[:, 0:width]
    work[half:, width : 2 * width] = total[:, width:]
    eliminate(work)
    right_out[...] = lax.dot_general(
        work[:, 0:width] * right_factor,
        share_ref[...],
        NN,
        precision=lax.Precision.HIGHEST,
        preferred_element_type=F32,
    )
    left_out[...] = lax.dot_general(
        scale_ref[...] * left_factor,
        left_ref[...],
        NN,
        precision=lax.Precision.HIGHEST,
        preferred_element_type=F32,
    )


SMEM = pl.BlockSpec(memory_space=pltpu.SMEM)
VMEM = pl.BlockSpec(memory_space=pltpu.VMEM)


def call(kernel, outs, smem, vmem, scratch=()):
    return pl.pallas_call(
        kernel,
        out_shape=outs,
        in_specs=[SMEM] * len(smem) + [VMEM] * len(vmem),
        out_specs=[VMEM] * len(outs),
        scratch_shapes=list(scratch),
        compiler_params=pltpu.CompilerParams(vmem_limit_bytes=VMEM_BYTES),
    )(*smem, *vmem)


def local(tiles, tile_rows, tile_cols, start_right):
    blocks = lax.axis_size("blk")
    group = lax.axis_size("rep")
    rep = lax.axis_index("rep").astype(jnp.int32)
    tile = tiles.shape[-1]
    share, width = start_right.shape
    flat_tiles = tiles.reshape(-1, tile, tile)
    total_rows = ROW_TILES * tile * blocks
    piece_tiles = share * group // tile
    total_cols = share * group * blocks
    place = rep.reshape(1)
    packed_rows = 2 * width + 3 * width // 4

    def across(value):
        return lax.all_to_all(value, "blk", split_axis=0, concat_axis=0, tiled=True)

    def swap_core(value):
        return lax.ppermute(value, "rep", [(i, i ^ 1) for i in range(group)])

    def swap_x(value):
        return lax.ppermute(value, "rep", [(i, i ^ 2) for i in range(group)])

    shape = jax.ShapeDtypeStruct
    work = pltpu.VMEM((width, 2 * width), F32)

    places = lax.all_gather(jnp.concatenate([tile_rows, tile_cols], axis=1).reshape(2, -1), "rep", axis=0)
    rows_all = places[:, 0, :]
    cols_all = places[:, 1, :]
    start = start_right.T.astype(BF16)
    start_own = jnp.stack([start, swap_x(start)])
    start_near = swap_core(start_own)
    row_tiles = lax.all_gather(flat_tiles, "rep", axis=0)

    asked = jnp.zeros((blocks, 16, tile), BF16).at[:, 0, 0:group].set(cols_all.T.astype(BF16))
    moved = across(jnp.concatenate([flat_tiles, asked], axis=1))
    cols_here = moved[:, tile, 0:group].astype(jnp.int32)
    column_tiles = lax.all_gather(moved, "rep", axis=0)
    flat_cols = cols_here.reshape(-1)
    count = flat_cols.shape[0]
    earlier = jnp.arange(count)[None, :] < jnp.arange(count)[:, None]
    seen = jnp.any((flat_cols[None, :] == flat_cols[:, None]) & earlier, axis=1)
    fresh = jnp.where(seen, 0, 1).astype(jnp.int32).reshape(blocks, group)

    (chosen,) = call(
        choose_kernel,
        [shape((blocks, 2 * width, tile), BF16)],
        [cols_here, place],
        [start_own, start_near],
    )
    for iteration in range(ITERS):
        first, last = iteration == 0, iteration == ITERS - 1
        chosen = across(chosen)
        picked, left_raw = call(
            functools.partial(left_kernel, first),
            [shape((blocks, packed_rows, tile), BF16), shape((width, ROW_TILES * tile), F32)],
            [rows_all, place],
            [row_tiles, chosen, swap_core(chosen)],
            [work],
        )
        picked = across(picked)
        outs = [shape((blocks, packed_rows, tile), BF16)]
        if last:
            outs = [
                shape((blocks, width // 2, 2 * width), F32),
                shape((width, share), F32),
                shape((width, width), F32),
            ]
        results = call(
            functools.partial(right_kernel, last),
            outs,
            [cols_here, fresh, place],
            [column_tiles, picked, swap_core(picked)],
            [
                pltpu.VMEM((piece_tiles, width, tile), F32),
                pltpu.VMEM((3 * width, 8 * group * tile), BF16),
                work,
            ],
        )
        chosen = results[0]
    gram, right_raw, left_scale = results
    left, right = call(
        functools.partial(finish_kernel, math.sqrt(total_rows), math.sqrt(total_cols)),
        [shape(left_raw.shape, F32), shape(right_raw.shape, F32)],
        [],
        [across(gram), left_scale, left_raw, right_raw],
        [work],
    )
    return (left.T, right.T)


def solution(mesh):
    in_specs = (
        P("blk", "rep", None, None),
        P("blk", "rep"),
        P("blk", "rep"),
        P(("blk", "rep"), None),
    )
    out_specs = (P("blk", None), P(("blk", "rep"), None))
    return jax.shard_map(local, mesh=mesh, in_specs=in_specs, out_specs=out_specs, check_vma=False)
```

time: 430 us -> 144 us (0.33)
  blocking collectives: 191 us -> 61.8 us
  waiting for transfers between devices: 138 us -> 25 us
  other arithmetic: 58.6 us -> 2.91 us
  Pallas kernels: 0 us -> 23.6 us
  matrix products: 15.2 us -> 0 us
  starting transfers between devices: 5.73 us -> 12.9 us
    psum x4 -> x0, blocking collectives: 148 us -> none  [the longest x2 74.2 us: local(): gram_left = lax.psum(gram_of(left_raw), 'blk')]
    psum x4 -> x0, waiting for transfers between devices: 125 us -> none  [the longest x2 66.1 us: local(): lax.psum(column_term.astype(jnp.bfloat16), 'rep').astype(jnp.float32)]
    another operation x20 -> x2, other arithmetic: 48.3 us -> 1.14 us  [local(): start_own = jnp.stack([start, swap_x(start)])]
    pallas_call x0 -> x6, Pallas kernels: none -> 23.6 us  [call(): pl.pallas_call(kernel, out_shape=outs, in_specs=[SMEM] * len(smem) + [VME...]
    all_to_all x4, blocking collectives: 42.7 us -> 54.8 us  [across(): return lax.all_to_all(value, 'blk', split_axis=0, concat_axis=0, tiled=True)]
    all_to_all x1 -> x2, waiting for transfers between devices: 7.31 us -> 18.2 us  [across(): return lax.all_to_all(value, 'blk', split_axis=0, concat_axis=0, tiled=True)]
    another operation x4 -> x0, matrix products: 7.73 us -> none  [normalize(): return jax.scipy.linalg.solve_triangular(factor, matrix.T, lower=True).T]
    dot_general x8 -> x0, matrix products: 7.49 us -> none  [the longest x4 6.57 us: gram_of(): jnp.dot(matrix.T, matrix, precision=lax.Precision.HIGHEST, preferred_elem...]
  transfers between devices with their start and end apart: 6 -> 10, of which waited for: 6 -> 6; matrix products, arithmetic and copies ran while one was open for 0% -> 2% of each run, Pallas kernels for 0% -> 3%
where the time goes in v1:
time: 144 us; the launch traced here: 143 us
  blocking collectives  61.8 us (43%)
  waiting for transfers between devices  25 us (17%)
  Pallas kernels  23.6 us (16%)
  between operations  14.2 us (10%)
  starting transfers between devices  12.9 us (9%)
  local copies, waits for them, and re-layouts  2.91 us (2%)
  other arithmetic  2.91 us (2%)
    all_to_all x4, blocking collectives, across(): return lax.all_to_all(value, 'blk', split_axis=0, concat_axis=0, tiled=True)  54.8 us
    pallas_call x6, Pallas kernels, call(): pl.pallas_call(kernel, out_shape=outs, in_specs=[SMEM] * len(smem) + [VME...  23.6 us
    all_to_all x2, waiting for transfers between devices, across(): return lax.all_to_all(value, 'blk', split_axis=0, concat_axis=0, tiled=True)  18.2 us
    all_to_all x2, starting transfers between devices, across(): return lax.all_to_all(value, 'blk', split_axis=0, concat_axis=0, tiled=True)  9.72 us
    all_gather x1, blocking collectives, local(): lax.all_gather(jnp.concatenate([tile_rows, tile_cols], axis=1).reshape(2,...  7.01 us
    ppermute x5, waiting for transfers between devices, swap_core(): return lax.ppermute(value, 'rep', [(i, i ^ 1) for i in range(group)])  5.46 us
    ppermute x1, starting transfers between devices, swap_x(): return lax.ppermute(value, 'rep', [(i, i ^ 2) for i in range(group)])  3 us
  transfers between devices with their start and end apart: 10, of which 6 were waited for; matrix products, arithmetic and copies ran while one was open for 2% of the time, Pallas kernels for 3%

profile of v1, /device:TPU:0, one launch (start us, length us, event | category | flops | bytes accessed | tf_op | source)
XLA Modules:
  0.0 143.3 jit_solution(7175096146022982971)
XLA Ops:
  7.9 1.1 convert_bitcast_fusion
  9.0 3.0 %collective-permute-start = (bf16[64,2048]{1,0:T(8,128)(2,1)S(1)}, bf16[64,2048]{1,0:T(8,128)(2,1)S(1)}, u32[]{:S(2)}, u32[]{:S(2)}) collective-permute-start(bf16[64,2048]{1,0:T(8,128)(2,1)S(1)} %get-tuple-element.31), channel_id=1, source_target_pairs={{0,2},{1,3},{2,0},{3,1},{4,6},{5,7},{6,4},{7,5},{8,10},{9,11},{10,... | collective-permute-start | bytes 786440 | tf_op jit(solution)/shard_map/ppermute | solution.py:335
  12.2 7.0 %all_gather.12 = s32[4,2,8]{2,1,0:T(2,128)S(1)} all-gather(s32[1,2,8]{2,1,0:T(2,128)S(1)} %all_gather_reshape.3), channel_id=1, replica_groups=mesh['blk'=8,'rep'=4] {'rep'}, dimensions={0}, use_global_device_ids=true | all-gather | bytes 320 | tf_op jit(solution)/shard_map/all_gather | solution.py:340
  19.3 0.7 fusion.1
  20.1 6.1 %all-to-all-start = ((bf16[8,144,128]{2,1,0:T(8,128)(2,1)}), bf16[8,144,128]{2,1,0:T(8,128)(2,1)S(1)}, u32[]{:S(2)}, u32[]{:S(2)}) async-start(bf16[8,144,128]{2,1,0:T(8,128)(2,1)} %fusion.1), calls=%async_computation | async-start | bytes 589824 | tf_op jit(solution)/shard_map/all_to_all | solution.py:329
  26.3 9.9 %all-to-all-done = bf16[8,144,128]{2,1,0:T(8,128)(2,1)S(1)} async-done(((bf16[8,144,128]{2,1,0:T(8,128)(2,1)}), bf16[8,144,128]{2,1,0:T(8,128)(2,1)S(1)}, u32[]{:S(2)}, u32[]{:S(2)}) %all-to-all-start) | async-done | bytes 294944 | tf_op jit(solution)/shard_map/all_to_all | solution.py:329
  36.2 1.5 %shard_map.59 = bf16[8,128,128]{2,1,0:T(8,128)(2,1)} custom-call(s32[8,4]{1,0:T(8,128)S(1)} %bitcast.22, s32[1]{0:T(128)} %bitcast.4.place_ref, bf16[2,64,2048]{2,1,0:T(8,128)(2,1)S(1)} %pad_maximum_fusion.own_ref, bf16[2,64,2048]{2,1,0:T(8,128)(2,1)S(1)} %collective-permute-done.1.near_ref), custom_call_target="tpu_custom_call" | custom-call | tf_op jit(solution)/shard_map/pallas_call | solution.py:305
  37.7 3.6 %all-to-all-start.1 = ((bf16[8,128,128]{2,1,0:T(8,128)(2,1)}), bf16[8,128,128]{2,1,0:T(8,128)(2,1)S(1)}, u32[]{:S(2)}, u32[]{:S(2)}) async-start(bf16[8,128,128]{2,1,0:T(8,128)(2,1)} %shard_map.59), calls=%async_computation.1 | async-start | bytes 524288 | tf_op jit(solution)/shard_map/all_to_all | solution.py:329
  42.1 8.3 %all-to-all-done.1.own_ref = bf16[8,128,128]{2,1,0:T(8,128)(2,1)S(1)} async-done(((bf16[8,128,128]{2,1,0:T(8,128)(2,1)}), bf16[8,128,128]{2,1,0:T(8,128)(2,1)S(1)}, u32[]{:S(2)}, u32[]{:S(2)}) %all-to-all-start.1) | async-done | bytes 262176 | tf_op jit(solution)/shard_map/all_to_all | solution.py:329
  50.4 1.5 %collective-permute-done.2.other_ref = bf16[8,128,128]{2,1,0:T(8,128)(2,1)S(1)} collective-permute-done((bf16[8,128,128]{2,1,0:T(8,128)(2,1)S(1)}, bf16[8,128,128]{2,1,0:T(8,128)(2,1)S(1)}, u32[]{:S(2)}, u32[]{:S(2)}) %collective-permute-start.2) | collective-permute-done | bytes 262176 | tf_op jit(solution)/shard_map/ppermute | solution.py:332
  51.9 1.3 copy-done.2
  53.2 2.3 %shard_map.60 = (bf16[8,176,128]{2,1,0:T(8,128)(2,1)S(1)}, f32[64,2048]{1,0:T(8,128)}) custom-call(s32[4,8]{1,0:T(4,128)S(1)} %bitcast.25, s32[1]{0:T(128)} %bitcast.4.place_ref, bf16[4,8,128,128]{3,2,1,0:T(8,128)(2,1)S(1)} %copy-done.2, bf16[8,128,128]{2,1,0:T(8,128)(2,1)S(1)} %all-to-all-done.1.own_ref, ...), custom_call_target="tpu_custom_call" | custom-call | tf_op jit(solution)/shard_map/pallas_call | solution.py:305
  55.5 15.1 %all_to_all.30.own_ref = bf16[8,176,128]{2,1,0:T(8,128)(2,1)S(1)} all-to-all(bf16[8,176,128]{2,1,0:T(8,128)(2,1)S(1)} %get-tuple-element.22), channel_id=1, replica_groups=mesh['blk'=8,'rep'=4] {'blk'}, dimensions={0} | all-to-all | bytes 720896 | tf_op jit(solution)/shard_map/all_to_all | solution.py:329
  70.6 0.7 fusion.4
  72.2 1.3 copy-done
  73.5 4.9 %shard_map.61 = bf16[8,176,128]{2,1,0:T(8,128)(2,1)S(1)} custom-call(s32[8,4]{1,0:T(8,128)S(1)} %bitcast.23, s32[8,4]{1,0:T(8,128)S(1)} %select_n.9.fresh_ref, s32[1]{0:T(128)} %bitcast.4.place_ref, bf16[4,8,144,128]{3,2,1,0:T(8,128)(2,1)S(1)} %bitcast.20, bf16[8,176,128]{2,1,0:T(8,128)(2,1)S(1)} %all_to_all.30.own_ref, ...), custom_call_target="tpu_custom_call" | custom-call | tf_op jit(solution)/shard_map/pallas_call | solution.py:305
  78.4 14.7 %all_to_all.31.own_ref = bf16[8,176,128]{2,1,0:T(8,128)(2,1)S(1)} all-to-all(bf16[8,176,128]{2,1,0:T(8,128)(2,1)S(1)} %shard_map.61), channel_id=1, replica_groups=mesh['blk'=8,'rep'=4] {'blk'}, dimensions={0} | all-to-all | bytes 720896 | tf_op jit(solution)/shard_map/all_to_all | solution.py:329
  93.1 1.7 %collective-permute-done.4.other_ref = bf16[8,176,128]{2,1,0:T(8,128)(2,1)S(1)} collective-permute-done((bf16[8,176,128]{2,1,0:T(8,128)(2,1)S(1)}, bf16[8,176,128]{2,1,0:T(8,128)(2,1)S(1)}, u32[]{:S(2)}, u32[]{:S(2)}) %collective-permute-start.4) | collective-permute-done | bytes 360480 | tf_op jit(solution)/shard_map/ppermute | solution.py:332
  94.8 6.1 %shard_map.62 = (bf16[8,176,128]{2,1,0:T(8,128)(2,1)S(1)}, f32[64,2048]{1,0:T(8,128)S(1)}) custom-call(s32[4,8]{1,0:T(4,128)S(1)} %bitcast.26, s32[1]{0:T(128)} %bitcast.4.place_ref, bf16[4,8,128,128]{3,2,1,0:T(8,128)(2,1)S(1)} %copy-done.3, bf16[8,176,128]{2,1,0:T(8,128)(2,1)S(1)} %all_to_all.31.own_ref, ...), custom_call_target="tpu_custom_call" | custom-call | tf_op jit(solution)/shard_map/pallas_call | solution.py:305
  101.0 14.7 %all_to_all.32.own_ref = bf16[8,176,128]{2,1,0:T(8,128)(2,1)S(1)} all-to-all(bf16[8,176,128]{2,1,0:T(8,128)(2,1)S(1)} %get-tuple-element.23), channel_id=1, replica_groups=mesh['blk'=8,'rep'=4] {'blk'}, dimensions={0} | all-to-all | bytes 720896 | tf_op jit(solution)/shard_map/all_to_all | solution.py:329
  115.7 1.7 %collective-permute-done.5.other_ref = bf16[8,176,128]{2,1,0:T(8,128)(2,1)S(1)} collective-permute-done((bf16[8,176,128]{2,1,0:T(8,128)(2,1)S(1)}, bf16[8,176,128]{2,1,0:T(8,128)(2,1)S(1)}, u32[]{:S(2)}, u32[]{:S(2)}) %collective-permute-start.5) | collective-permute-done | bytes 360480 | tf_op jit(solution)/shard_map/ppermute | solution.py:332
  117.4 4.8 %shard_map.63 = (f32[8,32,128]{2,1,0:T(8,128)S(1)}, f32[64,2048]{1,0:T(8,128)S(1)}, f32[64,64]{1,0:T(8,128)S(1)}) custom-call(s32[8,4]{1,0:T(8,128)S(1)} %bitcast.24, s32[8,4]{1,0:T(8,128)S(1)} %select_n.9.fresh_ref, s32[1]{0:T(128)} %bitcast.4.place_ref, bf16[4,8,144,128]{3,2,1,0:T(8,128)(2,1)S(1)} %bitcast.21, ...), custom_call_target="tpu_custom_call" | custom-call | tf_op jit(solution)/shard_map/pallas_call | solution.py:305
  122.2 10.3 %all_to_all.33.gram_ref = f32[8,32,128]{2,1,0:T(8,128)S(1)} all-to-all(f32[8,32,128]{2,1,0:T(8,128)S(1)} %get-tuple-element.24), channel_id=1, replica_groups=mesh['blk'=8,'rep'=4] {'blk'}, dimensions={0} | all-to-all | bytes 262144 | tf_op jit(solution)/shard_map/all_to_all | solution.py:329
  132.5 4.0 %shard_map.64 = (f32[64,2048]{1,0:T(8,128)}, f32[64,2048]{1,0:T(8,128)}) custom-call(f32[8,32,128]{2,1,0:T(8,128)S(1)} %all_to_all.33.gram_ref, f32[64,64]{1,0:T(8,128)S(1)} %get-tuple-element.25.scale_ref, f32[64,2048]{1,0:T(8,128)S(1)} %get-tuple-element.26.left_ref, f32[64,2048]{1,0:T(8,128)S(1)} %get-tuple-element.27.share_ref), custom_call_target="tpu_custom_call" | custom-call | tf_op jit(solution)/shard_map/pallas_call | solution.py:305
  (39 shorter events, 2.9 us)
Async XLA Ops:
  7.2 12.2 %copy-start.5 = (bf16[1,8,128,128]{3,2,1,0:T(8,128)(2,1)S(1)}, bf16[1,8,128,128]{3,2,1,0:T(8,128)(2,1)}, u32[]{:S(2)}) copy-start(bf16[1,8,128,128]{3,2,1,0:T(8,128)(2,1)} %param.6) | copy-start | bytes 786436
  7.2 4.9 %copy-start.6 = (s32[1,8]{1,0:T(1,128)S(1)}, s32[1,8]{1,0:T(1,128)}, u32[]{:S(2)}) copy-start(s32[1,8]{1,0:T(1,128)} %param.8) | copy-start | bytes 100
  7.2 4.9 %copy-start.7 = (s32[1,8]{1,0:T(1,128)S(1)}, s32[1,8]{1,0:T(1,128)}, u32[]{:S(2)}) copy-start(s32[1,8]{1,0:T(1,128)} %param.7) | copy-start | bytes 100
  7.2 44.7 %all-gather.4.cloned.1.call-start = ((), (), s32[]{:S(2)}) async-start(), calls=%async_computation.6 | async-start | bytes 1310720 | tf_op jit(solution)/shard_map/all_gather | solution.py:346
  9.0 17.1 %collective-permute-start = (bf16[64,2048]{1,0:T(8,128)(2,1)S(1)}, bf16[64,2048]{1,0:T(8,128)(2,1)S(1)}, u32[]{:S(2)}, u32[]{:S(2)}) collective-permute-start(bf16[64,2048]{1,0:T(8,128)(2,1)S(1)} %get-tuple-element.31), channel_id=1, source_target_pairs={{0,2},{1,3},{2,0},{3,1},{4,6},{5,7},{6,4},{7,5},{8,10},{9,11},{10,... | collective-permute-start | bytes 786440 | tf_op jit(solution)/shard_map/ppermute | solution.py:335
  20.1 16.1 %all-to-all-start = ((bf16[8,144,128]{2,1,0:T(8,128)(2,1)}), bf16[8,144,128]{2,1,0:T(8,128)(2,1)S(1)}, u32[]{:S(2)}, u32[]{:S(2)}) async-start(bf16[8,144,128]{2,1,0:T(8,128)(2,1)} %fusion.1), calls=%async_computation | async-start | bytes 589824 | tf_op jit(solution)/shard_map/all_to_all | solution.py:329
  26.2 10.0 %collective-permute-start.1 = (bf16[2,64,2048]{2,1,0:T(8,128)(2,1)S(1)}, bf16[2,64,2048]{2,1,0:T(8,128)(2,1)S(1)}, u32[]{:S(2)}, u32[]{:S(2)}) collective-permute-start(bf16[2,64,2048]{2,1,0:T(8,128)(2,1)S(1)} %pad_maximum_fusion.own_ref), channel_id=1, source_target_pairs={{0,1},{1,0},{2,3},{3,2},{4,5},{5,4},{6,7},{7,6},{8,9},{9,8},{10,11... | collective-permute-start | bytes 1572872 | tf_op jit(solution)/shard_map/ppermute | solution.py:332
  36.2 5.2 %copy-start.4 = (bf16[8,144,128]{2,1,0:T(8,128)(2,1)}, bf16[8,144,128]{2,1,0:T(8,128)(2,1)S(1)}, u32[]{:S(2)}) copy-start(bf16[8,144,128]{2,1,0:T(8,128)(2,1)S(1)} %all-to-all-done) | copy-start | bytes 884740
  37.7 12.7 %all-to-all-start.1 = ((bf16[8,128,128]{2,1,0:T(8,128)(2,1)}), bf16[8,128,128]{2,1,0:T(8,128)(2,1)S(1)}, u32[]{:S(2)}, u32[]{:S(2)}) async-start(bf16[8,128,128]{2,1,0:T(8,128)(2,1)} %shard_map.59), calls=%async_computation.1 | async-start | bytes 524288 | tf_op jit(solution)/shard_map/all_to_all | solution.py:329
  41.3 30.3 %all-gather.6.cloned.1.call-start = ((), (), s32[]{:S(2)}) async-start(), calls=%async_computation.7 | async-start | bytes 1474560 | tf_op jit(solution)/shard_map/all_gather | solution.py:351
  50.4 1.5 %collective-permute-start.2 = (bf16[8,128,128]{2,1,0:T(8,128)(2,1)S(1)}, bf16[8,128,128]{2,1,0:T(8,128)(2,1)S(1)}, u32[]{:S(2)}, u32[]{:S(2)}) collective-permute-start(bf16[8,128,128]{2,1,0:T(8,128)(2,1)S(1)} %all-to-all-done.1.own_ref), channel_id=1, source_target_pairs={{0,1},{1,0},{2,3},{3,2},{4,5},{5,4},{6,7},{7,6},{8,9},{9,8},{10,11... | collective-permute-start | bytes 786440 | tf_op jit(solution)/shard_map/ppermute | solution.py:332
  51.9 1.3 copy-start.2
  70.6 1.7 %collective-permute-start.3 = (bf16[8,176,128]{2,1,0:T(8,128)(2,1)S(1)}, bf16[8,176,128]{2,1,0:T(8,128)(2,1)S(1)}, u32[]{:S(2)}, u32[]{:S(2)}) collective-permute-start(bf16[8,176,128]{2,1,0:T(8,128)(2,1)S(1)} %all_to_all.30.own_ref), channel_id=1, source_target_pairs={{0,1},{1,0},{2,3},{3,2},{4,5},{5,4},{6,7},{7,6},{8,9},{9,8},{10,11... | collective-permute-start | bytes 1081352 | tf_op jit(solution)/shard_map/ppermute | solution.py:332
  72.2 1.3 copy-start
  73.5 21.3 %copy-start.3 = (bf16[4,8,128,128]{3,2,1,0:T(8,128)(2,1)S(1)}, bf16[4,8,128,128]{3,2,1,0:T(8,128)(2,1)}, u32[]{:S(2)}) copy-start(bf16[4,8,128,128]{3,2,1,0:T(8,128)(2,1)} %all-gather.4.cloned.1.call-done.tiles_ref) | copy-start | bytes 3145732
  93.1 24.2 %copy-start.1 = (bf16[32,144,128]{2,1,0:T(8,128)(2,1)S(1)}, bf16[32,144,128]{2,1,0:T(8,128)(2,1)}, u32[]{:S(2)}) copy-start(bf16[32,144,128]{2,1,0:T(8,128)(2,1)} %all-gather.6.cloned.1.call-done) | copy-start | bytes 3538948
  93.1 1.7 %collective-permute-start.4 = (bf16[8,176,128]{2,1,0:T(8,128)(2,1)S(1)}, bf16[8,176,128]{2,1,0:T(8,128)(2,1)S(1)}, u32[]{:S(2)}, u32[]{:S(2)}) collective-permute-start(bf16[8,176,128]{2,1,0:T(8,128)(2,1)S(1)} %all_to_all.31.own_ref), channel_id=1, source_target_pairs={{0,1},{1,0},{2,3},{3,2},{4,5},{5,4},{6,7},{7,6},{8,9},{9,8},{10,11... | collective-permute-start | bytes 1081352 | tf_op jit(solution)/shard_map/ppermute | solution.py:332
  115.7 1.7 %collective-permute-start.5 = (bf16[8,176,128]{2,1,0:T(8,128)(2,1)S(1)}, bf16[8,176,128]{2,1,0:T(8,128)(2,1)S(1)}, u32[]{:S(2)}, u32[]{:S(2)}) collective-permute-start(bf16[8,176,128]{2,1,0:T(8,128)(2,1)S(1)} %all_to_all.32.own_ref), channel_id=1, source_target_pairs={{0,1},{1,0},{2,3},{3,2},{4,5},{5,4},{6,7},{7,6},{8,9},{9,8},{10,11... | collective-permute-start | bytes 1081352 | tf_op jit(solution)/shard_map/ppermute | solution.py:332
Sparse Core Ops, SparseCore 0:
  9.6 19.4 all-gather.3
  44.3 18.8 all-gather.5

commit v2 on v1

v2 whole, which is shorter than its diff:
```python
import functools
import math

import jax
import jax.numpy as jnp
from jax import lax
from jax.experimental import pallas as pl
from jax.experimental.pallas import tpu as pltpu
from jax.sharding import PartitionSpec as P

ITERS = 2
ROW_TILES = 16
F32 = jnp.float32
BF16 = jnp.bfloat16
VMEM_BYTES = 48 * 1024 * 1024
NT = (((1,), (1,)), ((), ()))
NN = (((1,), (0,)), ((), ()))


def dot(a, b, dims):
    return lax.dot_general(a, b, dims, preferred_element_type=F32)


def exact_dot(a, b):
    return lax.dot_general(a, b, NN, precision=lax.Precision.HIGHEST, preferred_element_type=F32)


def two_parts(value):
    high = value.astype(BF16)
    return high, (value - high.astype(F32)).astype(BF16)


def eliminate(work):
    size = work.shape[0]
    for k in range(size // 8):
        at = size + 8 * k
        panel = work[8 * k : 8 * k + 8, :]
        shape = panel.shape
        cols = [jnp.broadcast_to(panel[:, at + s : at + s + 1], shape) for s in range(8)]
        d = {(i, s): jnp.broadcast_to(cols[s][i : i + 1, :], shape) for s in range(8) for i in range(s, 8)}
        rows = [jnp.broadcast_to(panel[s : s + 1, :], shape) for s in range(8)]
        inverse = [None] * 8
        lower = {}
        for s in range(8):
            inverse[s] = 1.0 / d[s, s]
            for i in range(s + 1, 8):
                lower[i, s] = d[i, s] * inverse[s]
            for i in range(s + 1, 8):
                for j in range(s + 1, i + 1):
                    d[i, j] = d[i, j] - lower[i, s] * d[j, s]
                rows[i] = rows[i] - lower[i, s] * rows[s]
        solved = [None] * 8
        for s in reversed(range(8)):
            solved[s] = rows[s] * inverse[s]
            for i in range(s + 1, 8):
                solved[s] = solved[s] - lower[i, s] * solved[i]
        for i in range(k + 1, size // 8):
            rest = work[8 * i : 8 * i + 8, :]
            updated = rest
            for s in range(8):
                updated = updated - jnp.broadcast_to(rest[:, at + s : at + s + 1], shape) * solved[s]
            work[8 * i : 8 * i + 8, :] = updated
        for s in range(8):
            work[8 * k + s : 8 * k + s + 1, :] = (rows[s] * lax.rsqrt(d[s, s]))[0:1, :]
        yield


def run(steps):
    for _ in steps:
        pass


def put_identity(work):
    size = work.shape[0]
    row = lax.broadcasted_iota(jnp.int32, work.shape, 0)
    column = lax.broadcasted_iota(jnp.int32, work.shape, 1)
    work[...] = jnp.where(row == column, 1.0, 0.0).astype(F32)


def gather_gram(work, own_ref, other_ref, core):
    size = work.shape[0]
    half = size // 2
    put_identity(work)
    for source, at_core in ((own_ref, core), (other_ref, 1 - core)):
        total = jnp.zeros((half, 2 * size), F32)
        for b in range(source.shape[0]):
            total = total + source[b, 2 * size :, :].astype(F32)
        total = total + pltpu.roll(total, size, 1)
        at = pl.multiple_of(at_core * half, half)
        work[pl.ds(at, half), size:] = total[:, size:]


def gram_of_parts(parts):
    width = parts.shape[0] // 2
    full = dot(parts, parts, NT)
    full = full[0:width] + full[width:]
    return full + pltpu.roll(full, width, 1)


def apply_scale(scale_parts, value):
    high, low = two_parts(value)
    scale_high, scale_low = scale_parts
    return dot(
        jnp.concatenate([scale_high, scale_high, scale_low], axis=1),
        jnp.concatenate([high, low, high], axis=0),
        NN,
    )


def each(count, body, step=8):
    if count <= step:
        for i in range(count):
            body(i)
    else:

        def several(o, carry):
            for i in range(step):
                body(o * step + i)
            return carry

        lax.fori_loop(0, count // step, several, 0)


def beside(steps, tasks, count):
    if count > 8:
        run(steps)
        for task in tasks:
            each(count, task)
        return
    tasks = [functools.partial(task, i) for task in tasks for i in range(count)]
    panels = 8
    for n in range(panels):
        next(steps, None)
        for task in tasks[len(tasks) * n // panels : len(tasks) * (n + 1) // panels]:
            task()
    run(steps)


def choose_kernel(cols_ref, place_ref, own_ref, near_ref, out_ref):
    rep = place_ref[0]
    core = lax.rem(rep, 2)
    tile = out_ref.shape[2]
    per_share = own_ref.shape[2] // tile
    width = own_ref.shape[1]

    def choose(b):
        for x in range(2):
            col = cols_ref[b, x * 2 + core]
            share = lax.div(col, per_share)
            at = pl.multiple_of(lax.rem(col, per_share) * tile, tile)
            away = lax.bitwise_xor(share, rep)
            same_core = lax.rem(away, 2) == 0
            far = lax.div(away, 2)
            mine = own_ref[far, :, pl.ds(at, tile)]
            theirs = near_ref[far, :, pl.ds(at, tile)]
            out_ref[b, x * width : (x + 1) * width, :] = jnp.where(same_core, mine, theirs)

    each(out_ref.shape[0], choose)


def left_kernel(first, last, rows_ref, place_ref, tiles_hbm, own_ref, other_ref, out_ref, *rest):
    if last:
        raw_ref, *rest = rest
    total, stacked, packed, work, tiles, sems = rest
    core = lax.rem(place_ref[0], 2)
    pieces, _, tile = own_ref.shape
    width = total.shape[0]
    half = width // 2
    copies = [pltpu.make_async_copy(tiles_hbm.at[r], tiles.at[r], sems.at[r]) for r in range(4)]
    for copy in copies:
        copy.start()
    if not first:
        gather_gram(work, own_ref, other_ref, core)
    steps = eliminate(work) if not first else iter(())
    total[...] = jnp.zeros_like(total)

    tasks = []
    for x in range(2):
        for source, at_core in ((own_ref, core), (other_ref, 1 - core)):

            def add(p, source=source, x=x, rep=x * 2 + at_core):
                product = dot(source[p, x * width : (x + 1) * width, :], tiles[rep, p], NT)
                at = pl.multiple_of(rows_ref[rep, p] * tile, tile)
                total[:, pl.ds(at, tile)] += product

            tasks.append(add)
    next(steps, None)
    for copy in copies:
        copy.wait()
    beside(steps, tasks, pieces)
    value = total[...]
    if not first:
        value = apply_scale(two_parts(work[:, 0:width]), value)
    if last:
        raw_ref[...] = value
    high, low = two_parts(value)
    stacked[0:width, :] = high
    stacked[width:, :] = low
    pack_gram(gram_of_parts(stacked[...]), packed)
    mine = packed[pl.ds(pl.multiple_of(core * half, half), half), :]

    def send(p):
        for x in range(2):
            at = pl.multiple_of(rows_ref[x * 2 + core, p] * tile, tile)
            out_ref[p, x * width : (x + 1) * width, :] = stacked[0:width, pl.ds(at, tile)]
        out_ref[p, 2 * width :, :] = mine

    each(pieces, send)


def pack_gram(gram_twice, packed):
    high, low = two_parts(gram_twice)
    lane = lax.broadcasted_iota(jnp.int32, gram_twice.shape, 1)
    packed[...] = jnp.where(lane < gram_twice.shape[0], high.astype(F32), low.astype(F32)).astype(BF16)


def right_kernel(last, slots_ref, cols_ref, place_ref, tiles_hbm, own_ref, other_ref, out_ref, *rest):
    if last:
        share_ref, scale_ref, *rest = rest
    total, stacked, packed, work, tiles, sems = rest
    core = lax.rem(place_ref[0], 2)
    blocks, _, tile = own_ref.shape
    width = total.shape[0]
    half = width // 2
    quarter = tile // 4
    copies = [
        pltpu.make_async_copy(
            tiles_hbm.at[q, :, pl.ds(0, quarter), :], tiles.at[:, pl.ds(q * quarter, quarter), :], sems.at[q]
        )
        for q in range(4)
    ]
    for copy in copies:
        copy.start()
    gather_gram(work, own_ref, other_ref, core)
    steps = eliminate(work)
    total[...] = jnp.zeros_like(total)

    tasks = []
    for x in range(2):
        for source, at_core in ((own_ref, core), (other_ref, 1 - core)):

            def add(b, source=source, x=x, rep=x * 2 + at_core):
                product = dot(source[b, x * width : (x + 1) * width, :], tiles[b * 4 + rep], NN)
                at = pl.multiple_of(slots_ref[b, rep] * tile, tile)
                total[:, pl.ds(at, tile)] += product

            tasks.append(add)
    next(steps, None)
    for copy in copies:
        copy.wait()
    beside(steps, tasks, blocks)
    scale = work[:, 0:width]
    scale_parts = two_parts(scale)
    chunk = 8 * tile

    def apply(o):
        at = o * chunk if isinstance(o, int) else pl.multiple_of(o * chunk, chunk)
        high, low = two_parts(apply_scale(scale_parts, total[:, pl.ds(at, chunk)]))
        stacked[0:width, pl.ds(at, chunk)] = high
        stacked[width:, pl.ds(at, chunk)] = low

    each(total.shape[1] // chunk, apply)
    gram = gram_of_parts(stacked[...])
    if last:
        scale_ref[...] = scale
        both = jnp.concatenate([gram[0:half, 0:width], gram[half:, 0:width]], axis=1)

        def send(b):
            out_ref[b] = both

        each(blocks, send)
        shares = share_ref.shape[1] // tile
        share_ref[...] = jnp.zeros_like(share_ref)

        def keep(b):
            for rep in range(4):
                col = cols_ref[b, rep]

                @pl.when(lax.div(col, shares) == place_ref[0])
                def _():
                    to = pl.multiple_of(lax.rem(col, shares) * tile, tile)
                    at = pl.multiple_of(slots_ref[b, rep] * tile, tile)
                    share_ref[:, pl.ds(to, tile)] = total[:, pl.ds(at, tile)]

        each(blocks, keep)
        return
    pack_gram(gram, packed)
    mine = packed[pl.ds(pl.multiple_of(core * half, half), half), :]

    def send(b):
        for x in range(2):
            at = pl.multiple_of(slots_ref[b, x * 2 + core] * tile, tile)
            out_ref[b, x * width : (x + 1) * width, :] = stacked[0:width, pl.ds(at, tile)]
        out_ref[b, 2 * width :, :] = mine

    each(blocks, send)


def finish_left(factor, scale_ref, left_ref, left_out):
    left_out[...] = exact_dot(scale_ref[...] * factor, left_ref[...])


def finish_right(factor, gram_ref, scale_ref, share_ref, right_out, work):
    width = share_ref.shape[0]
    half = width // 2
    total = gram_ref[0]
    for b in range(1, gram_ref.shape[0]):
        total = total + gram_ref[b]
    put_identity(work)
    work[0:half, width:] = total[:, 0:width]
    work[half:, width:] = total[:, width:]
    run(eliminate(work))
    right_out[...] = exact_dot(exact_dot(work[:, 0:width], scale_ref[...]) * factor, share_ref[...])


SMEM = pl.BlockSpec(memory_space=pltpu.SMEM)
VMEM = pl.BlockSpec(memory_space=pltpu.VMEM)
ANY = pl.BlockSpec(memory_space=pl.ANY)


def call(kernel, outs, smem, held, vmem, scratch=()):
    return pl.pallas_call(
        kernel,
        out_shape=outs,
        in_specs=[SMEM] * len(smem) + [ANY] * len(held) + [VMEM] * len(vmem),
        out_specs=[VMEM] * len(outs),
        scratch_shapes=list(scratch),
        compiler_params=pltpu.CompilerParams(vmem_limit_bytes=VMEM_BYTES),
    )(*smem, *held, *vmem)


def local(tiles, tile_rows, tile_cols, start_right):
    blocks = lax.axis_size("blk")
    group = lax.axis_size("rep")
    block = lax.axis_index("blk")
    rep = lax.axis_index("rep").astype(jnp.int32)
    tile = tiles.shape[-1]
    share, width = start_right.shape
    flat_tiles = tiles.reshape(-1, tile, tile)
    held = flat_tiles.shape[0]
    quarter = tile // group
    total_rows = ROW_TILES * tile * blocks
    total_cols = share * group * blocks
    count = blocks * group
    place = rep.reshape(1)
    packed_rows = 2 * width + width // 2
    shape = jax.ShapeDtypeStruct

    def across(value):
        return lax.all_to_all(value, "blk", split_axis=0, concat_axis=0, tiled=True)

    def swap_core(value):
        return lax.ppermute(value, "rep", [(i, i ^ 1) for i in range(group)])

    def swap_x(value):
        return lax.ppermute(value, "rep", [(i, i ^ 2) for i in range(group)])

    start = start_right.T.astype(BF16)
    start_own = jnp.stack([start, swap_x(start)])
    start_near = swap_core(start_own)
    row_tiles = lax.all_gather(flat_tiles, "rep", axis=0)

    places = jnp.concatenate([tile_rows, tile_cols], axis=1).astype(BF16)
    places = jnp.pad(places, ((0, 7), (0, tile - 2 * held)))
    moved = jnp.concatenate(
        [flat_tiles.reshape(count, quarter, tile), jnp.broadcast_to(places, (count, 8, tile))], axis=1
    )
    moved = lax.all_to_all(moved, ("blk", "rep"), split_axis=0, concat_axis=0, tiled=True)
    places = moved[:, quarter, 0 : 2 * held].reshape(blocks, group, 2 * held).astype(jnp.int32)
    rows_all = lax.dynamic_index_in_dim(places, block, 0, keepdims=False)[:, 0:held]
    cols_here = lax.dynamic_index_in_dim(places, held + block, 2, keepdims=False)
    column_tiles = lax.all_gather(moved, "rep", axis=0)
    flat_cols = cols_here.reshape(-1)
    slots = jnp.argmax(flat_cols[:, None] == flat_cols[None, :], axis=1).astype(jnp.int32).reshape(blocks, group)

    (chosen,) = call(
        choose_kernel,
        [shape((blocks, 2 * width, tile), BF16)],
        [cols_here, place],
        [],
        [start_own, start_near],
    )
    packed = pltpu.VMEM((width, 2 * width), BF16)
    work = pltpu.VMEM((width, 2 * width), F32)
    sems = pltpu.SemaphoreType.DMA((4,))
    for iteration in range(ITERS):
        first, last = iteration == 0, iteration == ITERS - 1
        chosen = across(chosen)
        outs = [shape((blocks, packed_rows, tile), BF16)]
        if last:
            outs.append(shape((width, ROW_TILES * tile), F32))
        results = call(
            functools.partial(left_kernel, first, last),
            outs,
            [rows_all, place],
            [row_tiles],
            [chosen, swap_core(chosen)],
            [
                pltpu.VMEM((width, ROW_TILES * tile), F32),
                pltpu.VMEM((2 * width, ROW_TILES * tile), BF16),
                packed,
                work,
                pltpu.VMEM(row_tiles.shape, BF16),
                sems,
            ],
        )
        picked = across(results[0])
        left_raw = results[-1]
        outs = [shape((blocks, packed_rows, tile), BF16)]
        if last:
            outs = [
                shape((blocks, width // 2, 2 * width), F32),
                shape((width, share), F32),
                shape((width, width), F32),
            ]
        results = call(
            functools.partial(right_kernel, last),
            outs,
            [slots, cols_here, place],
            [column_tiles],
            [picked, swap_core(picked)],
            [
                pltpu.VMEM((width, count * tile), F32),
                pltpu.VMEM((2 * width, count * tile), BF16),
                packed,
                work,
                pltpu.VMEM((count, tile, tile), BF16),
                sems,
            ],
        )
        chosen = results[0]
    gram, right_raw, left_scale = results
    (left,) = call(
        functools.partial(finish_left, math.sqrt(total_rows)),
        [shape(left_raw.shape, F32)],
        [],
        [],
        [left_scale, left_raw],
    )
    (right,) = call(
        functools.partial(finish_right, math.sqrt(total_cols)),
        [shape(right_raw.shape, F32)],
        [],
        [],
        [across(gram), left_scale, right_raw],
        [work],
    )
    return (left.T, right.T)


def solution(mesh):
    in_specs = (
        P("blk", "rep", None, None),
        P("blk", "rep"),
        P("blk", "rep"),
        P(("blk", "rep"), None),
    )
    out_specs = (P("blk", None), P(("blk", "rep"), None))
    return jax.shard_map(local, mesh=mesh, in_specs=in_specs, out_specs=out_specs, check_vma=False)
```

time: 144 us -> 133 us (0.924)
  blocking collectives: 61.8 us -> 54 us
  Pallas kernels: 23.6 us -> 20.8 us
    all_to_all x2 -> x1, waiting for transfers between devices: 18.2 us -> 6.17 us  [across(): return lax.all_to_all(value, 'blk', split_axis=0, concat_axis=0, tiled=True)]
    all_to_all x0 -> x1, waiting for transfers between devices: none -> 11.4 us  [local(): lax.all_to_all(moved, ('blk', 'rep'), split_axis=0, concat_axis=0, tiled=...]
    all_gather x1 -> x0, blocking collectives: 7.01 us -> none  [local(): lax.all_gather(jnp.concatenate([tile_rows, tile_cols], axis=1).reshape(2,...]
    all_to_all x2 -> x1, starting transfers between devices: 9.72 us -> 3.38 us  [across(): return lax.all_to_all(value, 'blk', split_axis=0, concat_axis=0, tiled=True)]
    all_to_all x0 -> x1, starting transfers between devices: none -> 4.92 us  [local(): lax.all_to_all(moved, ('blk', 'rep'), split_axis=0, concat_axis=0, tiled=...]
    pallas_call x6 -> x7, Pallas kernels: 23.6 us -> 20.8 us  [call(): pl.pallas_call(kernel, out_shape=outs, in_specs=[SMEM] * len(smem) + [ANY...]
    unnamed x18 -> x16, local copies, waits for them, and re-layouts: 2.67 us -> 3.29 us
  transfers between devices with their start and end apart: 10 -> 10, of which waited for: 6 -> 7; matrix products, arithmetic and copies ran while one was open for 2% -> 3% of each run, Pallas kernels for 3% -> 3%
where the time goes in v2:
time: 133 us; the launch traced here: 132 us
  blocking collectives  54 us (41%)
  waiting for transfers between devices  24.2 us (18%)
  Pallas kernels  20.8 us (16%)
  between operations  14.2 us (11%)
  starting transfers between devices  11.5 us (9%)
  local copies, waits for them, and re-layouts  3.93 us (3%)
  other arithmetic  3.55 us (3%)
    all_to_all x4, blocking collectives, across(): return lax.all_to_all(value, 'blk', split_axis=0, concat_axis=0, tiled=True)  54 us
    pallas_call x7, Pallas kernels, call(): pl.pallas_call(kernel, out_shape=outs, in_specs=[SMEM] * len(smem) + [ANY...  20.8 us
    all_to_all x1, waiting for transfers between devices, local(): lax.all_to_all(moved, ('blk', 'rep'), split_axis=0, concat_axis=0, tiled=...  11.4 us
    all_to_all x1, waiting for transfers between devices, across(): return lax.all_to_all(value, 'blk', split_axis=0, concat_axis=0, tiled=True)  6.17 us
    ppermute x5, waiting for transfers between devices, swap_core(): return lax.ppermute(value, 'rep', [(i, i ^ 1) for i in range(group)])  5.55 us
    all_to_all x1, starting transfers between devices, local(): lax.all_to_all(moved, ('blk', 'rep'), split_axis=0, concat_axis=0, tiled=...  4.92 us
    all_to_all x1, starting transfers between devices, across(): return lax.all_to_all(value, 'blk', split_axis=0, concat_axis=0, tiled=True)  3.38 us
    unnamed x16, local copies, waits for them, and re-layouts  3.29 us
  transfers between devices with their start and end apart: 10, of which 7 were waited for; matrix products, arithmetic and copies ran while one was open for 3% of the time, Pallas kernels for 3%

profile of v2, /device:TPU:0, one launch (start us, length us, event | category | flops | bytes accessed | tf_op | source)
XLA Modules:
  0.0 132.2 jit_solution(17855223099889354273)
XLA Ops:
  7.9 1.1 convert_bitcast_fusion
  9.0 3.0 %collective-permute-start = (bf16[64,2048]{1,0:T(8,128)(2,1)S(1)}, bf16[64,2048]{1,0:T(8,128)(2,1)S(1)}, u32[]{:S(2)}, u32[]{:S(2)}) collective-permute-start(bf16[64,2048]{1,0:T(8,128)(2,1)S(1)} %get-tuple-element.17), channel_id=1, source_target_pairs={{0,2},{1,3},{2,0},{3,1},{4,6},{5,7},{6,4},{7,5},{8,10},{9,11},{10,... | collective-permute-start | bytes 786440 | tf_op jit(solution)/shard_map/ppermute | solution.py:356
  12.9 4.9 %all-to-all-start = ((bf16[32,40,128]{2,1,0:T(8,128)(2,1)}), bf16[32,40,128]{2,1,0:T(8,128)(2,1)S(1)}, u32[]{:S(2)}, u32[]{:S(2)}) async-start(bf16[32,40,128]{2,1,0:T(8,128)(2,1)} %pad_maximum_fusion.1), calls=%async_computation | async-start | bytes 655360 | tf_op jit(solution)/shard_map/all_to_all | solution.py:368
  18.5 11.4 %all-to-all-done = bf16[32,40,128]{2,1,0:T(8,128)(2,1)S(1)} async-done(((bf16[32,40,128]{2,1,0:T(8,128)(2,1)}), bf16[32,40,128]{2,1,0:T(8,128)(2,1)S(1)}, u32[]{:S(2)}, u32[]{:S(2)}) %all-to-all-start) | async-done | bytes 327712 | tf_op jit(solution)/shard_map/all_to_all | solution.py:368
  30.6 0.9 slice_convert_fusion
  31.9 0.8 shard_map.59
  32.7 11.4 %all_to_all.30.own_ref = bf16[8,128,128]{2,1,0:T(8,128)(2,1)S(1)} all-to-all(bf16[8,128,128]{2,1,0:T(8,128)(2,1)S(1)} %shard_map.59), channel_id=1, replica_groups=mesh['blk'=8,'rep'=4] {'blk'}, dimensions={0} | all-to-all | bytes 524288 | tf_op jit(solution)/shard_map/all_to_all | solution.py:350
  44.2 1.5 %collective-permute-done.2.other_ref = bf16[8,128,128]{2,1,0:T(8,128)(2,1)S(1)} collective-permute-done((bf16[8,128,128]{2,1,0:T(8,128)(2,1)S(1)}, bf16[8,128,128]{2,1,0:T(8,128)(2,1)S(1)}, u32[]{:S(2)}, u32[]{:S(2)}) %collective-permute-start.2) | collective-permute-done | bytes 262176 | tf_op jit(solution)/shard_map/ppermute | solution.py:353
  45.7 1.2 copy-done.2
  46.9 2.2 %shard_map.60 = bf16[8,160,128]{2,1,0:T(8,128)(2,1)S(1)} custom-call(s32[4,8]{1,0:T(4,128)S(1)} %bitcast.18, s32[1]{0:T(128)} %bitcast.3.place_ref, bf16[4,8,128,128]{3,2,1,0:T(8,128)(2,1)S(1)} %copy-done.2, bf16[8,128,128]{2,1,0:T(8,128)(2,1)S(1)} %all_to_all.30.own_ref, bf16[8,128,128]{2,1,0:T(8,128)(2,1)S(1)} %collective-permute-done.2.other_ref), custom_call_target="tpu_custom_call" | custom-call | tf_op jit(solution)/shard_map/pallas_call | solution.py:322
  49.1 14.6 %all_to_all.31.own_ref = bf16[8,160,128]{2,1,0:T(8,128)(2,1)S(1)} all-to-all(bf16[8,160,128]{2,1,0:T(8,128)(2,1)S(1)} %shard_map.60), channel_id=1, replica_groups=mesh['blk'=8,'rep'=4] {'blk'}, dimensions={0} | all-to-all | bytes 655360 | tf_op jit(solution)/shard_map/all_to_all | solution.py:350
  64.5 0.8 collective-permute-done.3.other_ref
  65.3 1.3 copy-done
  66.6 4.0 %shard_map.61 = bf16[8,160,128]{2,1,0:T(8,128)(2,1)S(1)} custom-call(s32[8,4]{1,0:T(8,128)S(1)} %reshape.44.slots_ref, s32[8,4]{1,0:T(8,128)S(1)} %copy.21.cols_ref, s32[1]{0:T(128)} %bitcast.3.place_ref, bf16[4,32,40,128]{3,2,1,0:T(8,128)(2,1)S(1)} %bitcast.16, bf16[8,160,128]{2,1,0:T(8,128)(2,1)S(1)} %all_to_all.31.own_ref, ...), custom_call_target="tpu_custom_call" | custom-call | tf_op jit(solution)/shard_map/pallas_call | solution.py:322
  70.6 14.0 %all_to_all.32.own_ref = bf16[8,160,128]{2,1,0:T(8,128)(2,1)S(1)} all-to-all(bf16[8,160,128]{2,1,0:T(8,128)(2,1)S(1)} %shard_map.61), channel_id=1, replica_groups=mesh['blk'=8,'rep'=4] {'blk'}, dimensions={0} | all-to-all | bytes 655360 | tf_op jit(solution)/shard_map/all_to_all | solution.py:350
  84.6 1.6 %collective-permute-done.4.other_ref = bf16[8,160,128]{2,1,0:T(8,128)(2,1)S(1)} collective-permute-done((bf16[8,160,128]{2,1,0:T(8,128)(2,1)S(1)}, bf16[8,160,128]{2,1,0:T(8,128)(2,1)S(1)}, u32[]{:S(2)}, u32[]{:S(2)}) %collective-permute-start.4) | collective-permute-done | bytes 327712 | tf_op jit(solution)/shard_map/ppermute | solution.py:353
  86.3 3.8 %shard_map.62 = (bf16[8,160,128]{2,1,0:T(8,128)(2,1)S(1)}, f32[64,2048]{1,0:T(8,128)S(1)}) custom-call(s32[4,8]{1,0:T(4,128)S(1)} %bitcast.19, s32[1]{0:T(128)} %bitcast.3.place_ref, bf16[4,8,128,128]{3,2,1,0:T(8,128)(2,1)S(1)} %copy-done.3, bf16[8,160,128]{2,1,0:T(8,128)(2,1)S(1)} %all_to_all.32.own_ref, ...), custom_call_target="tpu_custom_call" | custom-call | tf_op jit(solution)/shard_map/pallas_call | solution.py:322
  90.0 14.0 %all_to_all.33.own_ref = bf16[8,160,128]{2,1,0:T(8,128)(2,1)S(1)} all-to-all(bf16[8,160,128]{2,1,0:T(8,128)(2,1)S(1)} %get-tuple-element.9), channel_id=1, replica_groups=mesh['blk'=8,'rep'=4] {'blk'}, dimensions={0} | all-to-all | bytes 655360 | tf_op jit(solution)/shard_map/all_to_all | solution.py:350
  104.1 1.6 %collective-permute-done.5.other_ref = bf16[8,160,128]{2,1,0:T(8,128)(2,1)S(1)} collective-permute-done((bf16[8,160,128]{2,1,0:T(8,128)(2,1)S(1)}, bf16[8,160,128]{2,1,0:T(8,128)(2,1)S(1)}, u32[]{:S(2)}, u32[]{:S(2)}) %collective-permute-start.5) | collective-permute-done | bytes 327712 | tf_op jit(solution)/shard_map/ppermute | solution.py:353
  105.7 5.0 %shard_map.63 = (f32[8,32,128]{2,1,0:T(8,128)}, f32[64,2048]{1,0:T(8,128)S(1)}, f32[64,64]{1,0:T(8,128)S(1)}) custom-call(s32[8,4]{1,0:T(8,128)S(1)} %reshape.44.slots_ref, s32[8,4]{1,0:T(8,128)S(1)} %copy.21.cols_ref, s32[1]{0:T(128)} %bitcast.3.place_ref, bf16[4,32,40,128]{3,2,1,0:T(8,128)(2,1)S(1)} %bitcast.17, ...), custom_call_target="tpu_custom_call" | custom-call | tf_op jit(solution)/shard_map/pallas_call | solution.py:322
  110.7 3.4 %all-to-all-start.5 = ((f32[8,32,128]{2,1,0:T(8,128)}), f32[8,32,128]{2,1,0:T(8,128)S(1)}, u32[]{:S(2)}, u32[]{:S(2)}) async-start(f32[8,32,128]{2,1,0:T(8,128)} %get-tuple-element.12), calls=%async_computation.5 | async-start | bytes 262144 | tf_op jit(solution)/shard_map/all_to_all | solution.py:350
  114.1 1.4 %shard_map.64 = f32[64,2048]{1,0:T(8,128)} custom-call(f32[64,64]{1,0:T(8,128)S(1)} %get-tuple-element.10.scale_ref, f32[64,2048]{1,0:T(8,128)S(1)} %get-tuple-element.11.left_ref), custom_call_target="tpu_custom_call" | custom-call | tf_op jit(solution)/shard_map/pallas_call | solution.py:322
  115.4 6.2 %all-to-all-done.5.gram_ref = f32[8,32,128]{2,1,0:T(8,128)S(1)} async-done(((f32[8,32,128]{2,1,0:T(8,128)}), f32[8,32,128]{2,1,0:T(8,128)S(1)}, u32[]{:S(2)}, u32[]{:S(2)}) %all-to-all-start.5) | async-done | bytes 131104 | tf_op jit(solution)/shard_map/all_to_all | solution.py:350
  121.6 3.8 %shard_map.65 = f32[64,2048]{1,0:T(8,128)} custom-call(f32[8,32,128]{2,1,0:T(8,128)S(1)} %all-to-all-done.5.gram_ref, f32[64,64]{1,0:T(8,128)S(1)} %get-tuple-element.10.scale_ref, f32[64,2048]{1,0:T(8,128)S(1)} %get-tuple-element.13.share_ref), custom_call_target="tpu_custom_call" | custom-call | tf_op jit(solution)/shard_map/pallas_call | solution.py:322
  (40 shorter events, 4.3 us)
Async XLA Ops:
  7.2 5.0 %copy-start.5 = (bf16[1,8,128,128]{3,2,1,0:T(8,128)(2,1)S(1)}, bf16[1,8,128,128]{3,2,1,0:T(8,128)(2,1)}, u32[]{:S(2)}) copy-start(bf16[1,8,128,128]{3,2,1,0:T(8,128)(2,1)} %param.4) | copy-start | bytes 786436
  7.2 4.9 %copy-start.6 = (s32[1,8]{1,0:T(1,128)S(1)}, s32[1,8]{1,0:T(1,128)}, u32[]{:S(2)}) copy-start(s32[1,8]{1,0:T(1,128)} %param.5) | copy-start | bytes 100
  7.2 4.9 %copy-start.7 = (s32[1,8]{1,0:T(1,128)S(1)}, s32[1,8]{1,0:T(1,128)}, u32[]{:S(2)}) copy-start(s32[1,8]{1,0:T(1,128)} %param.6) | copy-start | bytes 100
  7.2 38.5 %all-gather.4.cloned.1.call-start = ((), (), s32[]{:S(2)}) async-start(), calls=%async_computation.6 | async-start | bytes 1310720 | tf_op jit(solution)/shard_map/all_gather | solution.py:361
  9.0 9.3 %collective-permute-start = (bf16[64,2048]{1,0:T(8,128)(2,1)S(1)}, bf16[64,2048]{1,0:T(8,128)(2,1)S(1)}, u32[]{:S(2)}, u32[]{:S(2)}) collective-permute-start(bf16[64,2048]{1,0:T(8,128)(2,1)S(1)} %get-tuple-element.17), channel_id=1, source_target_pairs={{0,2},{1,3},{2,0},{3,1},{4,6},{5,7},{6,4},{7,5},{8,10},{9,11},{10,... | collective-permute-start | bytes 786440 | tf_op jit(solution)/shard_map/ppermute | solution.py:356
  12.9 16.9 %all-to-all-start = ((bf16[32,40,128]{2,1,0:T(8,128)(2,1)}), bf16[32,40,128]{2,1,0:T(8,128)(2,1)S(1)}, u32[]{:S(2)}, u32[]{:S(2)}) async-start(bf16[32,40,128]{2,1,0:T(8,128)(2,1)} %pad_maximum_fusion.1), calls=%async_computation | async-start | bytes 655360 | tf_op jit(solution)/shard_map/all_to_all | solution.py:368
  17.8 47.5 %all-gather.6.cloned.1.call-start = ((), (), s32[]{:S(2)}) async-start(), calls=%async_computation.7 | async-start | bytes 1638400 | tf_op jit(solution)/shard_map/all_gather | solution.py:372
  18.4 13.5 %collective-permute-start.1 = (bf16[2,64,2048]{2,1,0:T(8,128)(2,1)S(1)}, bf16[2,64,2048]{2,1,0:T(8,128)(2,1)S(1)}, u32[]{:S(2)}, u32[]{:S(2)}) collective-permute-start(bf16[2,64,2048]{2,1,0:T(8,128)(2,1)S(1)} %pad_maximum_fusion.own_ref), channel_id=1, source_target_pairs={{0,1},{1,0},{2,3},{3,2},{4,5},{5,4},{6,7},{7,6},{8,9},{9,8},{10,11... | collective-permute-start | bytes 1572872 | tf_op jit(solution)/shard_map/ppermute | solution.py:353
  29.8 0.7 copy-start.4
  44.2 1.5 %collective-permute-start.2 = (bf16[8,128,128]{2,1,0:T(8,128)(2,1)S(1)}, bf16[8,128,128]{2,1,0:T(8,128)(2,1)S(1)}, u32[]{:S(2)}, u32[]{:S(2)}) collective-permute-start(bf16[8,128,128]{2,1,0:T(8,128)(2,1)S(1)} %all_to_all.30.own_ref), channel_id=1, source_target_pairs={{0,1},{1,0},{2,3},{3,2},{4,5},{5,4},{6,7},{7,6},{8,9},{9,8},{10,11... | collective-permute-start | bytes 786440 | tf_op jit(solution)/shard_map/ppermute | solution.py:353
  45.7 1.2 copy-start.2
  63.7 1.6 %collective-permute-start.3 = (bf16[8,160,128]{2,1,0:T(8,128)(2,1)S(1)}, bf16[8,160,128]{2,1,0:T(8,128)(2,1)S(1)}, u32[]{:S(2)}, u32[]{:S(2)}) collective-permute-start(bf16[8,160,128]{2,1,0:T(8,128)(2,1)S(1)} %all_to_all.31.own_ref), channel_id=1, source_target_pairs={{0,1},{1,0},{2,3},{3,2},{4,5},{5,4},{6,7},{7,6},{8,9},{9,8},{10,11... | collective-permute-start | bytes 983048 | tf_op jit(solution)/shard_map/ppermute | solution.py:353
  65.3 1.3 copy-start
  66.6 19.6 %copy-start.3 = (bf16[4,8,128,128]{3,2,1,0:T(8,128)(2,1)S(1)}, bf16[4,8,128,128]{3,2,1,0:T(8,128)(2,1)}, u32[]{:S(2)}) copy-start(bf16[4,8,128,128]{3,2,1,0:T(8,128)(2,1)} %all-gather.4.cloned.1.call-done.tiles_hbm) | copy-start | bytes 3145732
  84.6 21.1 %copy-start.1 = (bf16[128,40,128]{2,1,0:T(8,128)(2,1)S(1)}, bf16[128,40,128]{2,1,0:T(8,128)(2,1)}, u32[]{:S(2)}) copy-start(bf16[128,40,128]{2,1,0:T(8,128)(2,1)} %all-gather.6.cloned.1.call-done) | copy-start | bytes 3932164
  84.6 1.6 %collective-permute-start.4 = (bf16[8,160,128]{2,1,0:T(8,128)(2,1)S(1)}, bf16[8,160,128]{2,1,0:T(8,128)(2,1)S(1)}, u32[]{:S(2)}, u32[]{:S(2)}) collective-permute-start(bf16[8,160,128]{2,1,0:T(8,128)(2,1)S(1)} %all_to_all.32.own_ref), channel_id=1, source_target_pairs={{0,1},{1,0},{2,3},{3,2},{4,5},{5,4},{6,7},{7,6},{8,9},{9,8},{10,11... | collective-permute-start | bytes 983048 | tf_op jit(solution)/shard_map/ppermute | solution.py:353
  104.1 1.6 %collective-permute-start.5 = (bf16[8,160,128]{2,1,0:T(8,128)(2,1)S(1)}, bf16[8,160,128]{2,1,0:T(8,128)(2,1)S(1)}, u32[]{:S(2)}, u32[]{:S(2)}) collective-permute-start(bf16[8,160,128]{2,1,0:T(8,128)(2,1)S(1)} %all_to_all.33.own_ref), channel_id=1, source_target_pairs={{0,1},{1,0},{2,3},{3,2},{4,5},{5,4},{6,7},{7,6},{8,9},{9,8},{10,11... | collective-permute-start | bytes 983048 | tf_op jit(solution)/shard_map/ppermute | solution.py:353
  110.7 10.9 %all-to-all-start.5 = ((f32[8,32,128]{2,1,0:T(8,128)}), f32[8,32,128]{2,1,0:T(8,128)S(1)}, u32[]{:S(2)}, u32[]{:S(2)}) async-start(f32[8,32,128]{2,1,0:T(8,128)} %get-tuple-element.12), calls=%async_computation.5 | async-start | bytes 262144 | tf_op jit(solution)/shard_map/all_to_all | solution.py:350
Sparse Core Ops, SparseCore 0:
  9.6 21.9 all-gather.3
  33.7 17.9 all-gather.5

commit v3 on v2

v3 whole, which is shorter than its diff:
```python
import functools
import math

import jax
import jax.numpy as jnp
from jax import lax
from jax.experimental import pallas as pl
from jax.experimental.pallas import tpu as pltpu
from jax.sharding import PartitionSpec as P

ITERS = 2
ROW_TILES = 16
F32 = jnp.float32
BF16 = jnp.bfloat16
VMEM_BYTES = 48 * 1024 * 1024
NT = (((1,), (1,)), ((), ()))
NN = (((1,), (0,)), ((), ()))


def dot(a, b, dims):
    return lax.dot_general(a, b, dims, preferred_element_type=F32)


def exact_dot(a, b):
    return lax.dot_general(a, b, NN, precision=lax.Precision.HIGHEST, preferred_element_type=F32)


def two_parts(value):
    high = value.astype(BF16)
    return high, (value - high.astype(F32)).astype(BF16)


def eliminate(work, spread):
    size = work.shape[0]
    for k in range(size // 8):
        at = size + 8 * k
        panel = work[8 * k : 8 * k + 8, :]
        shape = panel.shape
        for s in range(8):
            spread[k % 2, s] = jnp.broadcast_to(panel[:, at + s : at + s + 1], shape)
        d = {(i, s): jnp.broadcast_to(spread[k % 2, s, i : i + 1, :], shape) for s in range(8) for i in range(s, 8)}
        rows = [jnp.broadcast_to(work[8 * k + s : 8 * k + s + 1, :], shape) for s in range(8)]
        inverse = [None] * 8
        lower = {}
        for s in range(8):
            inverse[s] = 1.0 / d[s, s]
            for i in range(s + 1, 8):
                lower[i, s] = d[i, s] * inverse[s]
            for i in range(s + 1, 8):
                for j in range(s + 1, i + 1):
                    d[i, j] = d[i, j] - lower[i, s] * d[j, s]
                rows[i] = rows[i] - lower[i, s] * rows[s]
        for s in range(8):
            work[8 * k + s : 8 * k + s + 1, :] = (rows[s] * lax.rsqrt(d[s, s]))[0:1, :]
        solved = [rows[s] * inverse[s] for s in range(8)]
        below = [work[at : at + 8, :] for at in range(8 * k + 8, size, 8)]
        updated = list(below)
        for s in reversed(range(8)):
            for i in range(s):
                solved[i] = solved[i] - lower[s, i] * solved[s]
            for i, old in enumerate(below):
                updated[i] = updated[i] - jnp.broadcast_to(old[:, at + s : at + s + 1], shape) * solved[s]
        for i, new in enumerate(updated):
            work[8 * (k + 1 + i) : 8 * (k + 2 + i), :] = new
        yield


def run(steps):
    for _ in steps:
        pass


def put_identity(work):
    size = work.shape[0]
    row = lax.broadcasted_iota(jnp.int32, work.shape, 0)
    column = lax.broadcasted_iota(jnp.int32, work.shape, 1)
    work[...] = jnp.where(row == column, 1.0, 0.0).astype(F32)


def gather_gram(work, own_ref, other_ref, core):
    size = work.shape[0]
    half = size // 2
    put_identity(work)
    for source, at_core in ((own_ref, core), (other_ref, 1 - core)):
        total = jnp.zeros((half, 2 * size), F32)
        for b in range(source.shape[0]):
            total = total + source[b, 2 * size :, :].astype(F32)
        total = total + pltpu.roll(total, size, 1)
        at = pl.multiple_of(at_core * half, half)
        work[pl.ds(at, half), size:] = total[:, size:]


def gram_of_parts(parts):
    width = parts.shape[0] // 2
    full = dot(parts, parts, NT)
    full = full[0:width] + full[width:]
    return full + pltpu.roll(full, width, 1)


def apply_scale(scale_parts, value):
    high, low = two_parts(value)
    scale_high, scale_low = scale_parts
    return dot(
        jnp.concatenate([scale_high, scale_high, scale_low], axis=1),
        jnp.concatenate([high, low, high], axis=0),
        NN,
    )


def each(count, body, step=8):
    if count <= step:
        for i in range(count):
            body(i)
    else:

        def several(o, carry):
            for i in range(step):
                body(o * step + i)
            return carry

        lax.fori_loop(0, count // step, several, 0)


def beside(steps, tasks, count):
    if count > 8:
        run(steps)
        for task in tasks:
            each(count, task)
        return
    panels = 8
    done = 0
    for n in range(1, panels + 1):
        next(steps, None)
        while done < len(tasks) * count * n // panels:
            tasks[done // count](done % count)
            done += 1
    run(steps)


def pack_kernel(rows_hbm, cols_hbm, tiles_hbm, start_hbm, out_ref, start_out, rows_ref, cols_ref, tiles_ref, start_ref, sems):
    pairs = ((rows_hbm, rows_ref), (cols_hbm, cols_ref), (start_hbm, start_ref), (tiles_hbm, tiles_ref))
    copies = [pltpu.make_async_copy(source, to, sems.at[n]) for n, (source, to) in enumerate(pairs)]
    for copy in copies:
        copy.start()
    count, quarter, tile = tiles_ref.shape
    held = rows_ref.shape[1]
    lane = lax.broadcasted_iota(jnp.int32, (8, tile), 1)
    places = jnp.zeros((8, tile), jnp.int32)
    copies[0].wait()
    copies[1].wait()
    for j in range(held):
        places = jnp.where(lane == j, rows_ref[0, j], jnp.where(lane == held + j, cols_ref[0, j], places))
    places = places.astype(F32).astype(BF16)
    copies[2].wait()
    start_out[...] = start_ref[...].astype(BF16)
    copies[3].wait()

    def pack(i):
        out_ref[i] = jnp.concatenate([tiles_ref[i], places], axis=0)

    each(count, pack, 32)


def fetch_kernel(source, out_ref, sems):
    copies = [
        pltpu.make_async_copy(
            source.at[i, pl.ds(0, out_ref.shape[1]), pl.ds(0, out_ref.shape[2]), :], out_ref.at[i], sems.at[i]
        )
        for i in range(out_ref.shape[0])
    ]
    for copy in copies:
        copy.start()
    for copy in copies:
        copy.wait()


def choose_kernel(place_ref, moved_ref, own_ref, near_ref, out_ref, places_ref):
    rep, block = place_ref[0], place_ref[1]
    core = lax.rem(rep, 2)
    blocks, _, tile = out_ref.shape
    width, share = own_ref.shape[1:]
    per_share = share // tile
    lane = lax.broadcasted_iota(jnp.int32, (8, tile), 1)

    def choose(b):
        for r in range(4):
            entry = moved_ref[b * 4 + r]
            entry = entry[entry.shape[0] - 8 :, :].astype(F32)
            places_ref[b * 4 + r] = entry.astype(jnp.int32)
        for x in range(2):
            entry = moved_ref[b * 4 + x * 2 + core]
            entry = entry[entry.shape[0] - 8 :, :].astype(F32)
            col = jnp.max(jnp.where(lane == blocks + block, entry, 0.0)).astype(jnp.int32)
            at = pl.multiple_of(lax.rem(col, per_share) * tile, tile)
            away = lax.bitwise_xor(lax.div(col, per_share), rep)
            far = lax.div(away, 2)
            mine = own_ref[far, :, pl.ds(at, tile)]
            theirs = near_ref[far, :, pl.ds(at, tile)]
            out_ref[b, x * width : (x + 1) * width, :] = jnp.where(lax.rem(away, 2) == 0, mine, theirs)

    each(blocks, choose)


def find_slots(cols_ref, slots_ref, first_at):
    blocks, group = cols_ref.shape

    def note(o):
        b = blocks - 1 - o
        for r in reversed(range(group)):
            first_at[cols_ref[b, r]] = b * group + r

    def look(b):
        for r in range(group):
            slots_ref[b, r] = first_at[cols_ref[b, r]]

    each(blocks, note)
    each(blocks, look)


def left_kernel(first, last, rows_ref, place_ref, tiles_ref, own_ref, other_ref, out_ref, *rest):
    if last:
        raw_ref, *rest = rest
    total, stacked, packed, work, spread = rest
    core = lax.rem(place_ref[0], 2)
    pieces, _, tile = own_ref.shape
    width = total.shape[0]
    half = width // 2
    if not first:
        gather_gram(work, own_ref, other_ref, core)
    steps = eliminate(work, spread) if not first else iter(())
    total[...] = jnp.zeros_like(total)

    tasks = []
    for x in range(2):
        for source, at_core in ((own_ref, core), (other_ref, 1 - core)):

            def add(p, source=source, x=x, rep=x * 2 + at_core):
                product = dot(source[p, x * width : (x + 1) * width, :], tiles_ref[rep, p], NT)
                at = pl.multiple_of(rows_ref[rep, p] * tile, tile)
                total[:, pl.ds(at, tile)] += product

            tasks.append(add)
    beside(steps, tasks, pieces)
    value = total[...]
    if not first:
        value = apply_scale(two_parts(work[:, 0:width]), value)
    if last:
        raw_ref[...] = value
    high, low = two_parts(value)
    stacked[0:width, :] = high
    stacked[width:, :] = low
    pack_gram(gram_of_parts(stacked[...]), packed)
    mine = packed[pl.ds(pl.multiple_of(core * half, half), half), :]

    def send(p):
        for x in range(2):
            at = pl.multiple_of(rows_ref[x * 2 + core, p] * tile, tile)
            out_ref[p, x * width : (x + 1) * width, :] = stacked[0:width, pl.ds(at, tile)]
        out_ref[p, 2 * width :, :] = mine

    each(pieces, send)


def pack_gram(gram_twice, packed):
    high, low = two_parts(gram_twice)
    lane = lax.broadcasted_iota(jnp.int32, gram_twice.shape, 1)
    packed[...] = jnp.where(lane < gram_twice.shape[0], high.astype(F32), low.astype(F32)).astype(BF16)


def right_kernel(last, cols_ref, place_ref, tiles_ref, own_ref, other_ref, out_ref, *rest):
    if last:
        total, scale_ref, *rest = rest
    else:
        total, *rest = rest
    stacked, packed, work, spread, slots_ref, first_at = rest
    find_slots(cols_ref, slots_ref, first_at)
    core = lax.rem(place_ref[0], 2)
    blocks, _, tile = own_ref.shape
    width = total.shape[0]
    half = width // 2
    def stored(b, r):
        return jnp.concatenate([tiles_ref[q, b, r] for q in range(4)], axis=0)

    gather_gram(work, own_ref, other_ref, core)
    steps = eliminate(work, spread)
    total[...] = jnp.zeros_like(total)

    tasks = []
    for x in range(2):
        for source, at_core in ((own_ref, core), (other_ref, 1 - core)):

            def add(b, source=source, x=x, rep=x * 2 + at_core):
                product = dot(source[b, x * width : (x + 1) * width, :], stored(b, rep), NN)
                at = pl.multiple_of(slots_ref[b, rep] * tile, tile)
                total[:, pl.ds(at, tile)] += product

            tasks.append(add)
    beside(steps, tasks, blocks)
    scale = work[:, 0:width]
    scale_parts = two_parts(scale)
    chunk = 8 * tile

    def apply(o):
        at = o * chunk if isinstance(o, int) else pl.multiple_of(o * chunk, chunk)
        high, low = two_parts(apply_scale(scale_parts, total[:, pl.ds(at, chunk)]))
        stacked[0:width, pl.ds(at, chunk)] = high
        stacked[width:, pl.ds(at, chunk)] = low

    each(total.shape[1] // chunk, apply)
    gram = gram_of_parts(stacked[...])
    if last:
        scale_ref[...] = scale
        both = jnp.concatenate([gram[0:half, 0:width], gram[half:, 0:width]], axis=1)

        def send(b):
            out_ref[b] = both

        each(blocks, send)
        return
    pack_gram(gram, packed)
    mine = packed[pl.ds(pl.multiple_of(core * half, half), half), :]

    def send(b):
        for x in range(2):
            at = pl.multiple_of(slots_ref[b, x * 2 + core] * tile, tile)
            out_ref[b, x * width : (x + 1) * width, :] = stacked[0:width, pl.ds(at, tile)]
        out_ref[b, 2 * width :, :] = mine

    each(blocks, send)


def three_parts(value):
    high, low = two_parts(value)
    rest = value - high.astype(F32)
    return high, low, (rest - low.astype(F32)).astype(BF16)


def between_kernel(
    factor, cols_ref, place_ref, scale_ref, left_ref, total_ref, left_out, parts_ref, share, slots_ref, first_at
):
    width, tile = share.shape[0], total_ref.shape[1] // (slots_ref.shape[0] * 4)
    shares = share.shape[1] // tile
    find_slots(cols_ref, slots_ref, first_at)
    share[...] = jnp.zeros_like(share)

    def keep(b):
        for rep in range(4):
            col = cols_ref[b, rep]

            @pl.when(lax.div(col, shares) == place_ref[0])
            def _():
                to = pl.multiple_of(lax.rem(col, shares) * tile, tile)
                at = pl.multiple_of(slots_ref[b, rep] * tile, tile)
                share[:, pl.ds(to, tile)] = total_ref[:, pl.ds(at, tile)]

    each(slots_ref.shape[0], keep)
    high, middle, low = three_parts(share[...])
    for n, part in enumerate((high, middle, high, low, high, middle)):
        parts_ref[n * width : (n + 1) * width, :] = part
    left_out[...] = exact_dot(scale_ref[...] * factor, left_ref[...])


def finish_kernel(factor, gram_ref, scale_ref, parts_ref, right_hbm, work, spread, right, sems):
    width = scale_ref.shape[0]
    half = width // 2
    total = gram_ref[0]
    for b in range(1, gram_ref.shape[0]):
        total = total + gram_ref[b]
    put_identity(work)
    work[0:half, width:] = total[:, 0:width]
    work[half:, width:] = total[:, width:]
    run(eliminate(work, spread))
    high, middle, low = three_parts(exact_dot(work[:, 0:width], scale_ref[...]) * factor)
    scale = jnp.concatenate([high, high, middle, high, low, middle], axis=1)
    chunk = right.shape[1] // 4
    copies = []
    for n in range(4):
        at = pl.ds(n * chunk, chunk)
        right[:, at] = dot(scale, parts_ref[:, at], NN)
        copies.append(pltpu.make_async_copy(right.at[:, at], right_hbm.at[:, at], sems.at[n]))
        copies[-1].start()
    for copy in copies:
        copy.wait()


SMEM = pl.BlockSpec(memory_space=pltpu.SMEM)
VMEM = pl.BlockSpec(memory_space=pltpu.VMEM)
HBM = pl.BlockSpec(memory_space=pltpu.HBM)


def call(kernel, outs, smem, held, vmem, scratch=(), out_specs=None):
    return pl.pallas_call(
        kernel,
        out_shape=outs,
        in_specs=[SMEM] * len(smem) + [HBM] * len(held) + [VMEM] * len(vmem),
        out_specs=out_specs or [VMEM] * len(outs),
        scratch_shapes=list(scratch),
        compiler_params=pltpu.CompilerParams(vmem_limit_bytes=VMEM_BYTES),
    )(*smem, *[pltpu.with_memory_space_constraint(value, pltpu.HBM) for value in held], *vmem)


def local(tiles, tile_rows, tile_cols, start_right):
    blocks = lax.axis_size("blk")
    group = lax.axis_size("rep")
    block = lax.axis_index("blk")
    rep = lax.axis_index("rep").astype(jnp.int32)
    tile = tiles.shape[-1]
    share, width = start_right.shape
    flat_tiles = tiles.reshape(-1, tile, tile)
    held = flat_tiles.shape[0]
    quarter = tile // group
    total_rows = ROW_TILES * tile * blocks
    total_cols = share * group * blocks
    count = blocks * group
    place = jnp.stack([rep, block.astype(jnp.int32)])
    packed_rows = 2 * width + width // 2
    shape = jax.ShapeDtypeStruct

    def across(value):
        return lax.all_to_all(value, "blk", split_axis=0, concat_axis=0, tiled=True)

    def swap_x(value):
        return lax.ppermute(value, "rep", [(i, i ^ 2) for i in range(group)])

    def swap_core(value):
        return lax.ppermute(value, "rep", [(i, i ^ 1) for i in range(group)])

    moved, start = call(
        pack_kernel,
        [shape((count, quarter + 8, tile), BF16), shape((width, share), BF16)],
        [],
        [tile_rows, tile_cols, flat_tiles.reshape(count, quarter, tile), start_right.T],
        [],
        [
            pltpu.SMEM(tile_rows.shape, jnp.int32),
            pltpu.SMEM(tile_cols.shape, jnp.int32),
            pltpu.VMEM((count, quarter, tile), BF16),
            pltpu.VMEM((width, share), F32),
            pltpu.SemaphoreType.DMA((4,)),
        ],
    )
    start_own = jnp.stack([start, swap_x(start)])
    start_near = swap_core(start_own)
    flat_tiles, start = lax.optimization_barrier((flat_tiles, start))
    row_tiles = lax.all_gather(flat_tiles, "rep", axis=0)
    moved = lax.all_to_all(moved, ("blk", "rep"), split_axis=0, concat_axis=0, tiled=True)
    chosen, places = call(
        choose_kernel,
        [shape((blocks, 2 * width, tile), BF16), shape((count, 8, tile), jnp.int32)],
        [place],
        [],
        [moved, start_own, start_near],
    )
    places = places[:, 0, 0 : 2 * held].reshape(blocks, group, 2 * held)
    rows_all = lax.dynamic_index_in_dim(places, block, 0, keepdims=False)[:, 0:held]
    cols_here = lax.dynamic_index_in_dim(places, held + block, 2, keepdims=False)

    def fetch(value, rows):
        parts = value.shape[0]
        (value,) = call(
            fetch_kernel,
            [shape((*value.shape[:2], rows, value.shape[3]), BF16)],
            [],
            [value],
            [],
            [pltpu.SemaphoreType.DMA((parts,))],
        )
        return value

    packed = pltpu.VMEM((width, 2 * width), BF16)
    work = pltpu.VMEM((width, 2 * width), F32)
    spread = pltpu.VMEM((2, 8, 8, 2 * width), F32)
    slot_scratch = [pltpu.SMEM((blocks, group), jnp.int32), pltpu.SMEM((share * group // tile,), jnp.int32)]
    for iteration in range(ITERS):
        first, last = iteration == 0, iteration == ITERS - 1
        chosen = across(chosen)
        if first:
            chosen, moved, row_tiles = lax.optimization_barrier((chosen, moved, row_tiles))
            row_tiles = fetch(row_tiles.reshape(2 * group, -1, tile, tile), tile).reshape(row_tiles.shape)
            column_tiles = lax.all_gather(moved, "rep", axis=0)
        outs = [shape((blocks, packed_rows, tile), BF16)]
        if last:
            outs.append(shape((width, ROW_TILES * tile), F32))
        results = call(
            functools.partial(left_kernel, first, last),
            outs,
            [rows_all, place],
            [],
            [row_tiles, chosen, swap_core(chosen)],
            [
                pltpu.VMEM((width, ROW_TILES * tile), F32),
                pltpu.VMEM((2 * width, ROW_TILES * tile), BF16),
                packed,
                work,
                spread,
            ],
        )
        picked = across(results[0])
        left_raw = results[-1]
        if first:
            picked, column_tiles = lax.optimization_barrier((picked, column_tiles))
            column_tiles = column_tiles.reshape(2 * group, count // 2, -1, tile)
            column_tiles = fetch(column_tiles, quarter).reshape(group, blocks, group, quarter, tile)
        outs = [shape((blocks, packed_rows, tile), BF16)]
        if last:
            outs = [
                shape((blocks, width // 2, 2 * width), F32),
                shape((width, count * tile), F32),
                shape((width, width), F32),
            ]
        results = call(
            functools.partial(right_kernel, last),
            outs,
            [cols_here, place],
            [],
            [column_tiles, picked, swap_core(picked)],
            ([] if last else [pltpu.VMEM((width, count * tile), F32)])
            + [
                pltpu.VMEM((2 * width, count * tile), BF16),
                packed,
                work,
                spread,
            ]
            + slot_scratch,
        )
        chosen = results[0]
    gram, right_total, left_scale = results
    left, parts = call(
        functools.partial(between_kernel, math.sqrt(total_rows)),
        [shape(left_raw.shape, F32), shape((6 * width, share), BF16)],
        [cols_here, place],
        [],
        [left_scale, left_raw, right_total],
        [pltpu.VMEM((width, share), F32)] + slot_scratch,
    )
    (right,) = call(
        functools.partial(finish_kernel, math.sqrt(total_cols)),
        [shape((width, share), F32)],
        [],
        [],
        [across(gram), left_scale, parts],
        [work, spread, pltpu.VMEM((width, share), F32), pltpu.SemaphoreType.DMA((4,))],
        [HBM],
    )
    return (left.T, right.T)


def solution(mesh):
    in_specs = (
        P("blk", "rep", None, None),
        P("blk", "rep"),
        P("blk", "rep"),
        P(("blk", "rep"), None),
    )
    out_specs = (P("blk", None), P(("blk", "rep"), None))
    return jax.shard_map(local, mesh=mesh, in_specs=in_specs, out_specs=out_specs, check_vma=False)
```

time: 133 us -> 126 us (0.947)
  waiting for transfers between devices: 24.2 us -> 20 us
  local copies, waits for them, and re-layouts: 3.93 us -> 0.29 us
  other arithmetic: 3.55 us -> 0.13 us
  Pallas kernels: 20.8 us -> 23.3 us
  blocking collectives: 54 us -> 55.8 us
    unnamed x16 -> x2, local copies, waits for them, and re-layouts: 3.29 us -> 0.01 us
    pallas_call x7 -> x10, Pallas kernels: 20.8 us -> 23.3 us  [call(): pl.pallas_call(kernel, out_shape=outs, in_specs=[SMEM] * len(smem) + [HBM...]
    ppermute x5, waiting for transfers between devices: 5.55 us -> 3.38 us  [swap_core(): return lax.ppermute(value, 'rep', [(i, i ^ 1) for i in range(group)])]
    all_to_all x4, blocking collectives: 54 us -> 55.8 us  [across(): return lax.all_to_all(value, 'blk', split_axis=0, concat_axis=0, tiled=True)]
  transfers between devices with their start and end apart: 10 -> 10, of which waited for: 7 -> 6; matrix products, arithmetic and copies ran while one was open for 3% -> 0% of each run, Pallas kernels for 3% -> 7%
where the time goes in v3:
time: 126 us; the launch traced here: 125 us
  blocking collectives  55.8 us (44%)
  Pallas kernels  23.3 us (18%)
  waiting for transfers between devices  20 us (16%)
  between operations  14.2 us (11%)
  starting transfers between devices  11.5 us (9%)
    all_to_all x4, blocking collectives, across(): return lax.all_to_all(value, 'blk', split_axis=0, concat_axis=0, tiled=True)  55.8 us
    pallas_call x10, Pallas kernels, call(): pl.pallas_call(kernel, out_shape=outs, in_specs=[SMEM] * len(smem) + [HBM...  23.3 us
    all_to_all x1, waiting for transfers between devices, local(): lax.all_to_all(moved, ('blk', 'rep'), split_axis=0, concat_axis=0, tiled=...  10.4 us
    all_to_all x1, starting transfers between devices, local(): lax.all_to_all(moved, ('blk', 'rep'), split_axis=0, concat_axis=0, tiled=...  4.92 us
    all_to_all x1, waiting for transfers between devices, across(): return lax.all_to_all(value, 'blk', split_axis=0, concat_axis=0, tiled=True)  4.87 us
    ppermute x5, waiting for transfers between devices, swap_core(): return lax.ppermute(value, 'rep', [(i, i ^ 1) for i in range(group)])  3.38 us
    all_to_all x1, starting transfers between devices, across(): return lax.all_to_all(value, 'blk', split_axis=0, concat_axis=0, tiled=True)  3.37 us
    ppermute x1, starting transfers between devices, swap_x(): return lax.ppermute(value, 'rep', [(i, i ^ 2) for i in range(group)])  3 us
  transfers between devices with their start and end apart: 10, of which 6 were waited for; matrix products, arithmetic and copies ran while one was open for 0% of the time, Pallas kernels for 7%

profile of v3, /device:TPU:0, one launch (start us, length us, event | category | flops | bytes accessed | tf_op | source)
XLA Modules:
  0.0 125.2 jit_solution(99313641851942444)
XLA Ops:
  7.2 1.9 %shard_map.59 = (bf16[32,40,128]{2,1,0:T(8,128)(2,1)}, bf16[64,2048]{1,0:T(8,128)(2,1)S(1)}) custom-call(s32[1,8]{1,0:T(1,128)} %rows_hbm.1, s32[1,8]{1,0:T(1,128)} %cols_hbm.1, bf16[32,32,128]{2,1,0:T(8,128)(2,1)} %bitcast.29, f32[64,2048]{1,0:T(8,128)} %bitcast.32), custom_call_target="tpu_custom_call" | custom-call | tf_op jit(solution)/shard_map/pallas_call | solution.py:392
  9.2 3.0 %collective-permute-start = (bf16[64,2048]{1,0:T(8,128)(2,1)S(1)}, bf16[64,2048]{1,0:T(8,128)(2,1)S(1)}, u32[]{:S(2)}, u32[]{:S(2)}) collective-permute-start(bf16[64,2048]{1,0:T(8,128)(2,1)S(1)} %get-tuple-element.20), channel_id=1, source_target_pairs={{0,2},{1,3},{2,0},{3,1},{4,6},{5,7},{6,4},{7,5},{8,10},{9,11},{10,... | collective-permute-start | bytes 786440 | tf_op jit(solution)/shard_map/ppermute | solution.py:423
  12.2 4.9 %all-to-all-start = ((bf16[32,40,128]{2,1,0:T(8,128)(2,1)}), bf16[32,40,128]{2,1,0:T(8,128)(2,1)S(1)}, u32[]{:S(2)}, u32[]{:S(2)}) async-start(bf16[32,40,128]{2,1,0:T(8,128)(2,1)} %get-tuple-element.19), calls=%async_computation | async-start | bytes 655360 | tf_op jit(solution)/shard_map/all_to_all | solution.py:446
  17.1 1.3 %collective-permute-done = bf16[64,2048]{1,0:T(8,128)(2,1)S(1)} collective-permute-done((bf16[64,2048]{1,0:T(8,128)(2,1)S(1)}, bf16[64,2048]{1,0:T(8,128)(2,1)S(1)}, u32[]{:S(2)}, u32[]{:S(2)}) %collective-permute-start) | collective-permute-done | bytes 262176 | tf_op jit(solution)/shard_map/ppermute | solution.py:423
  18.7 10.4 %all-to-all-done.moved_ref = bf16[32,40,128]{2,1,0:T(8,128)(2,1)S(1)} async-done(((bf16[32,40,128]{2,1,0:T(8,128)(2,1)}), bf16[32,40,128]{2,1,0:T(8,128)(2,1)S(1)}, u32[]{:S(2)}, u32[]{:S(2)}) %all-to-all-start) | async-done | bytes 327712 | tf_op jit(solution)/shard_map/all_to_all | solution.py:446
  29.1 0.8 shard_map.60
  29.9 11.4 %all_to_all.30.own_ref = bf16[8,128,128]{2,1,0:T(8,128)(2,1)S(1)} all-to-all(bf16[8,128,128]{2,1,0:T(8,128)(2,1)S(1)} %get-tuple-element.22), channel_id=1, replica_groups=mesh['blk'=8,'rep'=4] {'blk'}, dimensions={0} | all-to-all | bytes 524288 | tf_op jit(solution)/shard_map/all_to_all | solution.py:420
  41.5 1.4 %shard_map.61 = bf16[8,4,128,128]{3,2,1,0:T(8,128)(2,1)S(1)} custom-call(bf16[8,4,128,128]{3,2,1,0:T(8,128)(2,1)} %bitcast.28), custom_call_target="tpu_custom_call" | custom-call | tf_op jit(solution)/shard_map/pallas_call | solution.py:392
  42.9 0.1 collective-permute-done.2.other_ref
  43.0 2.0 %shard_map.62 = bf16[8,160,128]{2,1,0:T(8,128)(2,1)S(1)} custom-call(s32[4,8]{1,0:T(4,128)S(1)} %bitcast.25, s32[2]{0:T(128)S(1)} %pad_add_fusion.place_ref, bf16[4,8,128,128]{3,2,1,0:T(8,128)(2,1)S(1)} %bitcast.20, bf16[8,128,128]{2,1,0:T(8,128)(2,1)S(1)} %all_to_all.30.own_ref, bf16[8,128,128]{2,1,0:T(8,128)(2,1)S(1)} %collective-permute-done.2.other_ref), custom_call_target="tpu_custom_call" | custom-call | tf_op jit(solution)/shard_map/pallas_call | solution.py:392
  45.0 14.8 %all_to_all.31.own_ref = bf16[8,160,128]{2,1,0:T(8,128)(2,1)S(1)} all-to-all(bf16[8,160,128]{2,1,0:T(8,128)(2,1)S(1)} %shard_map.62), channel_id=1, replica_groups=mesh['blk'=8,'rep'=4] {'blk'}, dimensions={0} | all-to-all | bytes 655360 | tf_op jit(solution)/shard_map/all_to_all | solution.py:420
  59.9 0.1 copy.10
  60.1 1.4 %shard_map.63 = bf16[8,16,32,128]{3,2,1,0:T(8,128)(2,1)S(1)} custom-call(bf16[8,16,40,128]{3,2,1,0:T(8,128)(2,1)} %bitcast.27), custom_call_target="tpu_custom_call" | custom-call | tf_op jit(solution)/shard_map/pallas_call | solution.py:392
  61.5 3.3 %shard_map.64 = bf16[8,160,128]{2,1,0:T(8,128)(2,1)S(1)} custom-call(s32[8,4]{1,0:T(8,128)S(1)} %copy.13.cols_ref, s32[2]{0:T(128)S(1)} %pad_add_fusion.place_ref, bf16[4,8,4,32,128]{4,3,2,1,0:T(8,128)(2,1)S(1)} %bitcast.22, bf16[8,160,128]{2,1,0:T(8,128)(2,1)S(1)} %all_to_all.31.own_ref, bf16[8,160,128]{2,1,0:T(8,128)(2,1)S(1)} %collective-permute-done.3.other_ref), custom_call_target="tpu_custom_call" | custom-call | tf_op jit(solution)/shard_map/pallas_call | solution.py:392
  64.8 15.5 %all_to_all.32.own_ref = bf16[8,160,128]{2,1,0:T(8,128)(2,1)S(1)} all-to-all(bf16[8,160,128]{2,1,0:T(8,128)(2,1)S(1)} %shard_map.64), channel_id=1, replica_groups=mesh['blk'=8,'rep'=4] {'blk'}, dimensions={0} | all-to-all | bytes 655360 | tf_op jit(solution)/shard_map/all_to_all | solution.py:420
  80.3 1.6 %collective-permute-done.4.other_ref = bf16[8,160,128]{2,1,0:T(8,128)(2,1)S(1)} collective-permute-done((bf16[8,160,128]{2,1,0:T(8,128)(2,1)S(1)}, bf16[8,160,128]{2,1,0:T(8,128)(2,1)S(1)}, u32[]{:S(2)}, u32[]{:S(2)}) %collective-permute-start.4) | collective-permute-done | bytes 327712 | tf_op jit(solution)/shard_map/ppermute | solution.py:426
  81.9 3.1 %shard_map.65 = (bf16[8,160,128]{2,1,0:T(8,128)(2,1)S(1)}, f32[64,2048]{1,0:T(8,128)S(1)}) custom-call(s32[4,8]{1,0:T(4,128)S(1)} %bitcast.26, s32[2]{0:T(128)S(1)} %pad_add_fusion.place_ref, bf16[4,8,128,128]{3,2,1,0:T(8,128)(2,1)S(1)} %bitcast.21, bf16[8,160,128]{2,1,0:T(8,128)(2,1)S(1)} %all_to_all.32.own_ref, ...), custom_call_target="tpu_custom_call" | custom-call | tf_op jit(solution)/shard_map/pallas_call | solution.py:392
  85.0 14.0 %all_to_all.33.own_ref = bf16[8,160,128]{2,1,0:T(8,128)(2,1)S(1)} all-to-all(bf16[8,160,128]{2,1,0:T(8,128)(2,1)S(1)} %get-tuple-element.29), channel_id=1, replica_groups=mesh['blk'=8,'rep'=4] {'blk'}, dimensions={0} | all-to-all | bytes 655360 | tf_op jit(solution)/shard_map/all_to_all | solution.py:420
  99.0 1.6 %collective-permute-done.5.other_ref = bf16[8,160,128]{2,1,0:T(8,128)(2,1)S(1)} collective-permute-done((bf16[8,160,128]{2,1,0:T(8,128)(2,1)S(1)}, bf16[8,160,128]{2,1,0:T(8,128)(2,1)S(1)}, u32[]{:S(2)}, u32[]{:S(2)}) %collective-permute-start.5) | collective-permute-done | bytes 327712 | tf_op jit(solution)/shard_map/ppermute | solution.py:426
  100.7 3.9 %shard_map.66 = (f32[8,32,128]{2,1,0:T(8,128)}, f32[64,4096]{1,0:T(8,128)S(1)}, f32[64,64]{1,0:T(8,128)S(1)}) custom-call(s32[8,4]{1,0:T(8,128)S(1)} %copy.13.cols_ref, s32[2]{0:T(128)S(1)} %pad_add_fusion.place_ref, bf16[4,8,4,32,128]{4,3,2,1,0:T(8,128)(2,1)S(1)} %bitcast.23, bf16[8,160,128]{2,1,0:T(8,128)(2,1)S(1)} %all_to_all.33.own_ref, ...), custom_call_target="tpu_custom_call" | custom-call | tf_op jit(solution)/shard_map/pallas_call | solution.py:392
  104.6 3.4 %all-to-all-start.5 = ((f32[8,32,128]{2,1,0:T(8,128)}), f32[8,32,128]{2,1,0:T(8,128)S(1)}, u32[]{:S(2)}, u32[]{:S(2)}) async-start(f32[8,32,128]{2,1,0:T(8,128)} %get-tuple-element.34), calls=%async_computation.5 | async-start | bytes 262144 | tf_op jit(solution)/shard_map/all_to_all | solution.py:420
  108.0 2.6 %shard_map.67 = (f32[64,2048]{1,0:T(8,128)}, bf16[384,2048]{1,0:T(8,128)(2,1)S(1)}) custom-call(s32[8,4]{1,0:T(8,128)S(1)} %copy.13.cols_ref, s32[2]{0:T(128)S(1)} %pad_add_fusion.place_ref, f32[64,64]{1,0:T(8,128)S(1)} %get-tuple-element.30.scale_ref, f32[64,2048]{1,0:T(8,128)S(1)} %get-tuple-element.31.left_ref, f32[64,4096]{1,0:T(8,128)S(1)} %get-tuple-element.32.total_ref), custom_call_target="tpu_custom_call" | custom-call | tf_op jit(solution)/shard_map/pallas_call | solution.py:392
  110.6 4.9 %all-to-all-done.5.gram_ref = f32[8,32,128]{2,1,0:T(8,128)S(1)} async-done(((f32[8,32,128]{2,1,0:T(8,128)}), f32[8,32,128]{2,1,0:T(8,128)S(1)}, u32[]{:S(2)}, u32[]{:S(2)}) %all-to-all-start.5) | async-done | bytes 131104 | tf_op jit(solution)/shard_map/all_to_all | solution.py:420
  115.5 2.9 %shard_map.68 = f32[64,2048]{1,0:T(8,128)} custom-call(f32[8,32,128]{2,1,0:T(8,128)S(1)} %all-to-all-done.5.gram_ref, f32[64,64]{1,0:T(8,128)S(1)} %get-tuple-element.30.scale_ref, bf16[384,2048]{1,0:T(8,128)(2,1)S(1)} %get-tuple-element.35.parts_ref), custom_call_target="tpu_custom_call" | custom-call | tf_op jit(solution)/shard_map/pallas_call | solution.py:392
  (21 shorter events, 0.6 us)
Async XLA Ops:
  7.2 34.2 %all-gather.5.cloned.1.call-start = ((), (), s32[]{:S(2)}) async-start(), calls=%async_computation.6 | async-start | bytes 1310720 | tf_op jit(solution)/shard_map/all_gather | solution.py:445
  9.2 9.3 %collective-permute-start = (bf16[64,2048]{1,0:T(8,128)(2,1)S(1)}, bf16[64,2048]{1,0:T(8,128)(2,1)S(1)}, u32[]{:S(2)}, u32[]{:S(2)}) collective-permute-start(bf16[64,2048]{1,0:T(8,128)(2,1)S(1)} %get-tuple-element.20), channel_id=1, source_target_pairs={{0,2},{1,3},{2,0},{3,1},{4,6},{5,7},{6,4},{7,5},{8,10},{9,11},{10,... | collective-permute-start | bytes 786440 | tf_op jit(solution)/shard_map/ppermute | solution.py:423
  12.2 16.9 %all-to-all-start = ((bf16[32,40,128]{2,1,0:T(8,128)(2,1)}), bf16[32,40,128]{2,1,0:T(8,128)(2,1)S(1)}, u32[]{:S(2)}, u32[]{:S(2)}) async-start(bf16[32,40,128]{2,1,0:T(8,128)(2,1)} %get-tuple-element.19), calls=%async_computation | async-start | bytes 655360 | tf_op jit(solution)/shard_map/all_to_all | solution.py:446
  17.1 42.8 %all-gather.7.cloned.1.call-start = ((), (), s32[]{:S(2)}) async-start(), calls=%async_computation.7 | async-start | bytes 1638400 | tf_op jit(solution)/shard_map/all_gather | solution.py:480
  18.5 10.6 %collective-permute-start.1 = (bf16[2,64,2048]{2,1,0:T(8,128)(2,1)S(1)}, bf16[2,64,2048]{2,1,0:T(8,128)(2,1)S(1)}, u32[]{:S(2)}, u32[]{:S(2)}) collective-permute-start(bf16[2,64,2048]{2,1,0:T(8,128)(2,1)S(1)} %pad_maximum_fusion.own_ref), channel_id=1, source_target_pairs={{0,1},{1,0},{2,3},{3,2},{4,5},{5,4},{6,7},{7,6},{8,9},{9,8},{10,11... | collective-permute-start | bytes 1572872 | tf_op jit(solution)/shard_map/ppermute | solution.py:426
  29.1 12.3 %copy-start = (bf16[32,40,128]{2,1,0:T(8,128)(2,1)}, bf16[32,40,128]{2,1,0:T(8,128)(2,1)S(1)}, u32[]{:S(2)}) copy-start(bf16[32,40,128]{2,1,0:T(8,128)(2,1)S(1)} %all-to-all-done.moved_ref) | copy-start | bytes 983044
  41.4 1.6 %collective-permute-start.2 = (bf16[8,128,128]{2,1,0:T(8,128)(2,1)S(1)}, bf16[8,128,128]{2,1,0:T(8,128)(2,1)S(1)}, u32[]{:S(2)}, u32[]{:S(2)}) collective-permute-start(bf16[8,128,128]{2,1,0:T(8,128)(2,1)S(1)} %all_to_all.30.own_ref), channel_id=1, source_target_pairs={{0,1},{1,0},{2,3},{3,2},{4,5},{5,4},{6,7},{7,6},{8,9},{9,8},{10,11... | collective-permute-start | bytes 786440 | tf_op jit(solution)/shard_map/ppermute | solution.py:426
  59.9 1.6 %collective-permute-start.3 = (bf16[8,160,128]{2,1,0:T(8,128)(2,1)S(1)}, bf16[8,160,128]{2,1,0:T(8,128)(2,1)S(1)}, u32[]{:S(2)}, u32[]{:S(2)}) collective-permute-start(bf16[8,160,128]{2,1,0:T(8,128)(2,1)S(1)} %all_to_all.31.own_ref), channel_id=1, source_target_pairs={{0,1},{1,0},{2,3},{3,2},{4,5},{5,4},{6,7},{7,6},{8,9},{9,8},{10,11... | collective-permute-start | bytes 983048 | tf_op jit(solution)/shard_map/ppermute | solution.py:426
  80.3 1.6 %collective-permute-start.4 = (bf16[8,160,128]{2,1,0:T(8,128)(2,1)S(1)}, bf16[8,160,128]{2,1,0:T(8,128)(2,1)S(1)}, u32[]{:S(2)}, u32[]{:S(2)}) collective-permute-start(bf16[8,160,128]{2,1,0:T(8,128)(2,1)S(1)} %all_to_all.32.own_ref), channel_id=1, source_target_pairs={{0,1},{1,0},{2,3},{3,2},{4,5},{5,4},{6,7},{7,6},{8,9},{9,8},{10,11... | collective-permute-start | bytes 983048 | tf_op jit(solution)/shard_map/ppermute | solution.py:426
  99.0 1.6 %collective-permute-start.5 = (bf16[8,160,128]{2,1,0:T(8,128)(2,1)S(1)}, bf16[8,160,128]{2,1,0:T(8,128)(2,1)S(1)}, u32[]{:S(2)}, u32[]{:S(2)}) collective-permute-start(bf16[8,160,128]{2,1,0:T(8,128)(2,1)S(1)} %all_to_all.33.own_ref), channel_id=1, source_target_pairs={{0,1},{1,0},{2,3},{3,2},{4,5},{5,4},{6,7},{7,6},{8,9},{9,8},{10,11... | collective-permute-start | bytes 983048 | tf_op jit(solution)/shard_map/ppermute | solution.py:426
  104.6 10.9 %all-to-all-start.5 = ((f32[8,32,128]{2,1,0:T(8,128)}), f32[8,32,128]{2,1,0:T(8,128)S(1)}, u32[]{:S(2)}, u32[]{:S(2)}) async-start(f32[8,32,128]{2,1,0:T(8,128)} %get-tuple-element.34), calls=%async_computation.5 | async-start | bytes 262144 | tf_op jit(solution)/shard_map/all_to_all | solution.py:420
Sparse Core Ops, SparseCore 0:
  9.6 21.6 all-gather.4
  41.5 16.8 all-gather.6

commit v4 on v3

--- a/solution.py
+++ b/solution.py
@@ -161,19 +161,6 @@
     each(count, pack, 32)
 
 
-def fetch_kernel(source, out_ref, sems):
-    copies = [
-        pltpu.make_async_copy(
-            source.at[i, pl.ds(0, out_ref.shape[1]), pl.ds(0, out_ref.shape[2]), :], out_ref.at[i], sems.at[i]
-        )
-        for i in range(out_ref.shape[0])
-    ]
-    for copy in copies:
-        copy.start()
-    for copy in copies:
-        copy.wait()
-
-
 def choose_kernel(place_ref, moved_ref, own_ref, near_ref, out_ref, places_ref):
     rep, block = place_ref[0], place_ref[1]
     core = lax.rem(rep, 2)
@@ -217,7 +204,7 @@
     each(blocks, look)
 
 
-def left_kernel(first, last, rows_ref, place_ref, tiles_ref, own_ref, other_ref, out_ref, *rest):
+def left_kernel(first, last, rows_ref, place_ref, tiles_own, tiles_near, own_ref, other_ref, out_ref, *rest):
     if last:
         raw_ref, *rest = rest
     total, stacked, packed, work, spread = rest
@@ -231,11 +218,13 @@
     total[...] = jnp.zeros_like(total)
 
     tasks = []
-    for x in range(2):
-        for source, at_core in ((own_ref, core), (other_ref, 1 - core)):
-
-            def add(p, source=source, x=x, rep=x * 2 + at_core):
-                product = dot(source[p, x * width : (x + 1) * width, :], tiles_ref[rep, p], NT)
+    for far in range(2):
+        for source, stored, near in ((own_ref, tiles_own, 0), (other_ref, tiles_near, 1)):
+            rep = lax.bitwise_xor(place_ref[0], 2 * far + near)
+
+            def add(p, source=source, stored=stored, far=far, rep=rep):
+                chosen = source[p, pl.ds(pl.multiple_of(lax.div(rep, 2) * width, width), width), :]
+                product = dot(chosen, stored[far, p], NT)
                 at = pl.multiple_of(rows_ref[rep, p] * tile, tile)
                 total[:, pl.ds(at, tile)] += product
 
@@ -267,19 +256,24 @@
     packed[...] = jnp.where(lane < gram_twice.shape[0], high.astype(F32), low.astype(F32)).astype(BF16)
 
 
-def right_kernel(last, cols_ref, place_ref, tiles_ref, own_ref, other_ref, out_ref, *rest):
+def right_kernel(last, cols_ref, place_ref, tiles_own, tiles_near, own_ref, other_ref, out_ref, *rest):
     if last:
         total, scale_ref, *rest = rest
     else:
         total, *rest = rest
-    stacked, packed, work, spread, slots_ref, first_at = rest
+    stacked, packed, work, spread, quarters, slots_ref, first_at = rest
     find_slots(cols_ref, slots_ref, first_at)
     core = lax.rem(place_ref[0], 2)
     blocks, _, tile = own_ref.shape
     width = total.shape[0]
     half = width // 2
+    quarter = quarters.shape[2]
+    for far in range(2):
+        for near, source in enumerate((tiles_own, tiles_near)):
+            quarters[lax.bitwise_xor(place_ref[0], 2 * far + near)] = source[far, :, 0:quarter, :]
+
     def stored(b, r):
-        return jnp.concatenate([tiles_ref[q, b, r] for q in range(4)], axis=0)
+        return jnp.concatenate([quarters[q, b * 4 + r] for q in range(4)], axis=0)
 
     gather_gram(work, own_ref, other_ref, core)
     steps = eliminate(work, spread)
@@ -441,8 +435,8 @@
     )
     start_own = jnp.stack([start, swap_x(start)])
     start_near = swap_core(start_own)
-    flat_tiles, start = lax.optimization_barrier((flat_tiles, start))
-    row_tiles = lax.all_gather(flat_tiles, "rep", axis=0)
+    tiles_own = jnp.stack([flat_tiles, swap_x(flat_tiles)])
+    tiles_near = swap_core(tiles_own)
     moved = lax.all_to_all(moved, ("blk", "rep"), split_axis=0, concat_axis=0, tiled=True)
     chosen, places = call(
         choose_kernel,
@@ -451,21 +445,11 @@
         [],
         [moved, start_own, start_near],
     )
+    columns_own = jnp.stack([moved, swap_x(moved)])
+    columns_near = swap_core(columns_own)
     places = places[:, 0, 0 : 2 * held].reshape(blocks, group, 2 * held)
     rows_all = lax.dynamic_index_in_dim(places, block, 0, keepdims=False)[:, 0:held]
     cols_here = lax.dynamic_index_in_dim(places, held + block, 2, keepdims=False)
-
-    def fetch(value, rows):
-        parts = value.shape[0]
-        (value,) = call(
-            fetch_kernel,
-            [shape((*value.shape[:2], rows, value.shape[3]), BF16)],
-            [],
-            [value],
-            [],
-            [pltpu.SemaphoreType.DMA((parts,))],
-        )
-        return value
 
     packed = pltpu.VMEM((width, 2 * width), BF16)
     work = pltpu.VMEM((width, 2 * width), F32)
@@ -474,10 +458,6 @@
     for iteration in range(ITERS):
         first, last = iteration == 0, iteration == ITERS - 1
         chosen = across(chosen)
-        if first:
-            chosen, moved, row_tiles = lax.optimization_barrier((chosen, moved, row_tiles))
-            row_tiles = fetch(row_tiles.reshape(2 * group, -1, tile, tile), tile).reshape(row_tiles.shape)
-            column_tiles = lax.all_gather(moved, "rep", axis=0)
         outs = [shape((blocks, packed_rows, tile), BF16)]
         if last:
             outs.append(shape((width, ROW_TILES * tile), F32))
@@ -486,7 +466,7 @@
             outs,
             [rows_all, place],
             [],
-            [row_tiles, chosen, swap_core(chosen)],
+            [tiles_own, tiles_near, chosen, swap_core(chosen)],
             [
                 pltpu.VMEM((width, ROW_TILES * tile), F32),
                 pltpu.VMEM((2 * width, ROW_TILES * tile), BF16),
@@ -497,10 +477,6 @@
         )
         picked = across(results[0])
         left_raw = results[-1]
-        if first:
-            picked, column_tiles = lax.optimization_barrier((picked, column_tiles))
-            column_tiles = column_tiles.reshape(2 * group, count // 2, -1, tile)
-            column_tiles = fetch(column_tiles, quarter).reshape(group, blocks, group, quarter, tile)
         outs = [shape((blocks, packed_rows, tile), BF16)]
         if last:
             outs = [
@@ -513,7 +489,7 @@
             outs,
             [cols_here, place],
             [],
-            [column_tiles, picked, swap_core(picked)],
+            [columns_own, columns_near, picked, swap_core(picked)],
             ([] if last else [pltpu.VMEM((width, count * tile), F32)])
             + [
                 pltpu.VMEM((2 * width, count * tile), BF16),
@@ -521,6 +497,7 @@
                 work,
                 spread,
             ]
+            + [pltpu.VMEM((group, count, quarter, tile), BF16)]
             + slot_scratch,
         )
         chosen = results[0]

time: 126 us -> 113 us (0.90)
  blocking collectives: 55.8 us -> 28.6 us
  waiting for transfers between devices: 20 us -> 39.1 us
  between operations: 14.2 us -> 0.77 us
  starting transfers between devices: 11.5 us -> 21.4 us
    all_to_all x4 -> x2, blocking collectives: 55.8 us -> 28.6 us  [across(): return lax.all_to_all(value, 'blk', split_axis=0, concat_axis=0, tiled=True)]
    all_to_all x1 -> x3, waiting for transfers between devices: 4.87 us -> 21.9 us  [across(): return lax.all_to_all(value, 'blk', split_axis=0, concat_axis=0, tiled=True)]
    all_to_all x1 -> x3, starting transfers between devices: 3.37 us -> 10.3 us  [across(): return lax.all_to_all(value, 'blk', split_axis=0, concat_axis=0, tiled=True)]
    ppermute x1 -> x3, starting transfers between devices: 3 us -> 5.94 us  [swap_x(): return lax.ppermute(value, 'rep', [(i, i ^ 2) for i in range(group)])]
    ppermute x1 -> x3, waiting for transfers between devices: 1.33 us -> 3.7 us  [swap_x(): return lax.ppermute(value, 'rep', [(i, i ^ 2) for i in range(group)])]
    all_to_all x1, waiting for transfers between devices: 10.4 us -> 8.6 us  [local(): lax.all_to_all(moved, ('blk', 'rep'), split_axis=0, concat_axis=0, tiled=...]
    ppermute x5 -> x7, waiting for transfers between devices: 3.38 us -> 4.98 us  [swap_core(): return lax.ppermute(value, 'rep', [(i, i ^ 1) for i in range(group)])]
    pallas_call x10 -> x8, Pallas kernels: 23.3 us -> 22.2 us  [call(): pl.pallas_call(kernel, out_shape=outs, in_specs=[SMEM] * len(smem) + [HBM...]
  transfers between devices with their start and end apart: 10 -> 14, of which waited for: 6 -> 10; matrix products, arithmetic and copies ran while one was open for 0% -> 0% of each run, Pallas kernels for 7% -> 6%
where the time goes in v4:
time: 113 us
  waiting for transfers between devices  39.1 us (35%)
  blocking collectives  28.6 us (25%)
  Pallas kernels  22.2 us (20%)
  starting transfers between devices  21.4 us (19%)
    all_to_all x2, blocking collectives, across(): return lax.all_to_all(value, 'blk', split_axis=0, concat_axis=0, tiled=True)  28.6 us
    pallas_call x8, Pallas kernels, call(): pl.pallas_call(kernel, out_shape=outs, in_specs=[SMEM] * len(smem) + [HBM...  22.2 us
    all_to_all x3, waiting for transfers between devices, across(): return lax.all_to_all(value, 'blk', split_axis=0, concat_axis=0, tiled=True)  21.9 us
    all_to_all x3, starting transfers between devices, across(): return lax.all_to_all(value, 'blk', split_axis=0, concat_axis=0, tiled=True)  10.3 us
    all_to_all x1, waiting for transfers between devices, local(): lax.all_to_all(moved, ('blk', 'rep'), split_axis=0, concat_axis=0, tiled=...  8.6 us
    ppermute x3, starting transfers between devices, swap_x(): return lax.ppermute(value, 'rep', [(i, i ^ 2) for i in range(group)])  5.94 us
    ppermute x7, waiting for transfers between devices, swap_core(): return lax.ppermute(value, 'rep', [(i, i ^ 1) for i in range(group)])  4.98 us
    all_to_all x1, starting transfers between devices, local(): lax.all_to_all(moved, ('blk', 'rep'), split_axis=0, concat_axis=0, tiled=...  4.92 us
  transfers between devices with their start and end apart: 14, of which 10 were waited for; matrix products, arithmetic and copies ran while one was open for 0% of the time, Pallas kernels for 6%

profile of v4, /device:TPU:0, one launch (start us, length us, event | category | flops | bytes accessed | tf_op | source)
XLA Modules:
  0.0 112.7 jit_solution(12909377276939488779)
XLA Ops:
  0.6 2.0 %shard_map.59 = (bf16[32,40,128]{2,1,0:T(8,128)(2,1)}, bf16[64,2048]{1,0:T(8,128)(2,1)S(1)}) custom-call(s32[1,8]{1,0:T(1,128)} %rows_hbm.1, s32[1,8]{1,0:T(1,128)} %cols_hbm.1, bf16[32,32,128]{2,1,0:T(8,128)(2,1)} %bitcast.21, f32[64,2048]{1,0:T(8,128)} %bitcast.24), custom_call_target="tpu_custom_call" | custom-call | tf_op jit(solution)/shard_map/pallas_call | solution.py:386
  2.6 3.0 %collective-permute-start = (bf16[64,2048]{1,0:T(8,128)(2,1)S(1)}, bf16[64,2048]{1,0:T(8,128)(2,1)S(1)}, u32[]{:S(2)}, u32[]{:S(2)}) collective-permute-start(bf16[64,2048]{1,0:T(8,128)(2,1)S(1)} %get-tuple-element.14), channel_id=1, source_target_pairs={{0,2},{1,3},{2,0},{3,1},{4,6},{5,7},{6,4},{7,5},{8,10},{9,11},{10,... | collective-permute-start | bytes 786440 | tf_op jit(solution)/shard_map/ppermute | solution.py:417
  5.6 4.9 %all-to-all-start = ((bf16[32,40,128]{2,1,0:T(8,128)(2,1)}), bf16[32,40,128]{2,1,0:T(8,128)(2,1)S(1)}, u32[]{:S(2)}, u32[]{:S(2)}) async-start(bf16[32,40,128]{2,1,0:T(8,128)(2,1)} %get-tuple-element.13), calls=%async_computation | async-start | bytes 655360 | tf_op jit(solution)/shard_map/all_to_all | solution.py:440
  10.5 1.4 %collective-permute-done = bf16[64,2048]{1,0:T(8,128)(2,1)S(1)} collective-permute-done((bf16[64,2048]{1,0:T(8,128)(2,1)S(1)}, bf16[64,2048]{1,0:T(8,128)(2,1)S(1)}, u32[]{:S(2)}, u32[]{:S(2)}) %collective-permute-start) | collective-permute-done | bytes 262176 | tf_op jit(solution)/shard_map/ppermute | solution.py:417
  12.1 1.8 %collective-permute-start.4 = (bf16[8,128,128]{2,1,0:T(8,128)(2,1)S(1)}, bf16[8,128,128]{2,1,0:T(8,128)(2,1)S(1)}, u32[]{:S(2)}, u32[]{:S(2)}) collective-permute-start(bf16[8,128,128]{2,1,0:T(8,128)(2,1)S(1)} %bitcast.22), channel_id=1, source_target_pairs={{0,2},{1,3},{2,0},{3,1},{4,6},{5,7},{6,4},{7,5},{8,10},{9,11},{10,... | collective-permute-start | bytes 786440 | tf_op jit(solution)/shard_map/ppermute | solution.py:417
  13.9 8.6 %all-to-all-done.moved_ref = bf16[32,40,128]{2,1,0:T(8,128)(2,1)S(1)} async-done(((bf16[32,40,128]{2,1,0:T(8,128)(2,1)}), bf16[32,40,128]{2,1,0:T(8,128)(2,1)S(1)}, u32[]{:S(2)}, u32[]{:S(2)}) %all-to-all-start) | async-done | bytes 327712 | tf_op jit(solution)/shard_map/all_to_all | solution.py:440
  22.5 1.5 %shard_map.60 = (bf16[8,128,128]{2,1,0:T(8,128)(2,1)}, s32[32,8,128]{2,1,0:T(8,128)S(1)}) custom-call(s32[2]{0:T(128)S(1)} %pad_add_fusion.place_ref, bf16[32,40,128]{2,1,0:T(8,128)(2,1)S(1)} %all-to-all-done.moved_ref, bf16[2,64,2048]{2,1,0:T(8,128)(2,1)S(1)} %pad_maximum_fusion.1.own_ref, bf16[2,64,2048]{2,1,0:T(8,128)(2,1)S(1)} %collective-permute-done.1.near_ref), custom_call_target="tpu_custom_call" | custom-call | tf_op jit(solution)/shard_map/pallas_call | solution.py:386
  24.1 3.4 %all-to-all-start.1 = ((bf16[8,128,128]{2,1,0:T(8,128)(2,1)}), bf16[8,128,128]{2,1,0:T(8,128)(2,1)S(1)}, u32[]{:S(2)}, u32[]{:S(2)}) async-start(bf16[8,128,128]{2,1,0:T(8,128)(2,1)} %get-tuple-element.16), calls=%async_computation.1 | async-start | bytes 524288 | tf_op jit(solution)/shard_map/all_to_all | solution.py:414
  27.6 8.8 %all-to-all-done.1.own_ref = bf16[8,128,128]{2,1,0:T(8,128)(2,1)S(1)} async-done(((bf16[8,128,128]{2,1,0:T(8,128)(2,1)}), bf16[8,128,128]{2,1,0:T(8,128)(2,1)S(1)}, u32[]{:S(2)}, u32[]{:S(2)}) %all-to-all-start.1) | async-done | bytes 262176 | tf_op jit(solution)/shard_map/all_to_all | solution.py:414
  38.0 2.7 %shard_map.61 = bf16[8,160,128]{2,1,0:T(8,128)(2,1)} custom-call(s32[4,8]{1,0:T(4,128)S(1)} %bitcast.19, s32[2]{0:T(128)S(1)} %pad_add_fusion.place_ref, bf16[2,8,128,128]{3,2,1,0:T(8,128)(2,1)S(1)} %pad_maximum_fusion.2.tiles_own, bf16[2,8,128,128]{3,2,1,0:T(8,128)(2,1)S(1)} %collective-permute-done.5.tiles_near, ...), custom_call_target="tpu_custom_call" | custom-call | tf_op jit(solution)/shard_map/pallas_call | solution.py:386
  40.7 3.6 %all-to-all-start.2 = ((bf16[8,160,128]{2,1,0:T(8,128)(2,1)}), bf16[8,160,128]{2,1,0:T(8,128)(2,1)S(1)}, u32[]{:S(2)}, u32[]{:S(2)}) async-start(bf16[8,160,128]{2,1,0:T(8,128)(2,1)} %shard_map.61), calls=%async_computation.2 | async-start | bytes 655360 | tf_op jit(solution)/shard_map/all_to_all | solution.py:414
  44.2 2.3 %collective-permute-done.2 = bf16[32,40,128]{2,1,0:T(8,128)(2,1)S(1)} collective-permute-done((bf16[32,40,128]{2,1,0:T(8,128)(2,1)S(1)}, bf16[32,40,128]{2,1,0:T(8,128)(2,1)S(1)}, u32[]{:S(2)}, u32[]{:S(2)}) %collective-permute-start.2) | collective-permute-done | bytes 327712 | tf_op jit(solution)/shard_map/ppermute | solution.py:417
  46.7 8.2 %all-to-all-done.2.own_ref = bf16[8,160,128]{2,1,0:T(8,128)(2,1)S(1)} async-done(((bf16[8,160,128]{2,1,0:T(8,128)(2,1)}), bf16[8,160,128]{2,1,0:T(8,128)(2,1)S(1)}, u32[]{:S(2)}, u32[]{:S(2)}) %all-to-all-start.2) | async-done | bytes 327712 | tf_op jit(solution)/shard_map/all_to_all | solution.py:414
  56.5 3.3 %shard_map.62 = bf16[8,160,128]{2,1,0:T(8,128)(2,1)S(1)} custom-call(s32[8,4]{1,0:T(8,128)S(1)} %copy.9.cols_ref, s32[2]{0:T(128)S(1)} %pad_add_fusion.place_ref, bf16[2,32,40,128]{3,2,1,0:T(8,128)(2,1)S(1)} %pad_maximum_fusion.tiles_own, bf16[2,32,40,128]{3,2,1,0:T(8,128)(2,1)S(1)} %collective-permute-done.3.tiles_near, ...), custom_call_target="tpu_custom_call" | custom-call | tf_op jit(solution)/shard_map/pallas_call | solution.py:386
  59.9 14.6 %all_to_all.30.own_ref = bf16[8,160,128]{2,1,0:T(8,128)(2,1)S(1)} all-to-all(bf16[8,160,128]{2,1,0:T(8,128)(2,1)S(1)} %shard_map.62), channel_id=1, replica_groups=mesh['blk'=8,'rep'=4] {'blk'}, dimensions={0} | all-to-all | bytes 655360 | tf_op jit(solution)/shard_map/all_to_all | solution.py:414
  74.5 1.6 %collective-permute-done.8.other_ref = bf16[8,160,128]{2,1,0:T(8,128)(2,1)S(1)} collective-permute-done((bf16[8,160,128]{2,1,0:T(8,128)(2,1)S(1)}, bf16[8,160,128]{2,1,0:T(8,128)(2,1)S(1)}, u32[]{:S(2)}, u32[]{:S(2)}) %collective-permute-start.8) | collective-permute-done | bytes 327712 | tf_op jit(solution)/shard_map/ppermute | solution.py:420
  76.2 3.1 %shard_map.63 = (bf16[8,160,128]{2,1,0:T(8,128)(2,1)S(1)}, f32[64,2048]{1,0:T(8,128)S(1)}) custom-call(s32[4,8]{1,0:T(4,128)S(1)} %bitcast.20, s32[2]{0:T(128)S(1)} %pad_add_fusion.place_ref, bf16[2,8,128,128]{3,2,1,0:T(8,128)(2,1)S(1)} %pad_maximum_fusion.2.tiles_own, bf16[2,8,128,128]{3,2,1,0:T(8,128)(2,1)S(1)} %collective-permute-done.5.tiles_near, ...), custom_call_target="tpu_custom_call" | custom-call | tf_op jit(solution)/shard_map/pallas_call | solution.py:386
  79.3 14.0 %all_to_all.31.own_ref = bf16[8,160,128]{2,1,0:T(8,128)(2,1)S(1)} all-to-all(bf16[8,160,128]{2,1,0:T(8,128)(2,1)S(1)} %get-tuple-element.17), channel_id=1, replica_groups=mesh['blk'=8,'rep'=4] {'blk'}, dimensions={0} | all-to-all | bytes 655360 | tf_op jit(solution)/shard_map/all_to_all | solution.py:414
  93.3 1.6 %collective-permute-done.9.other_ref = bf16[8,160,128]{2,1,0:T(8,128)(2,1)S(1)} collective-permute-done((bf16[8,160,128]{2,1,0:T(8,128)(2,1)S(1)}, bf16[8,160,128]{2,1,0:T(8,128)(2,1)S(1)}, u32[]{:S(2)}, u32[]{:S(2)}) %collective-permute-start.9) | collective-permute-done | bytes 327712 | tf_op jit(solution)/shard_map/ppermute | solution.py:420
  94.9 4.0 %shard_map.64 = (f32[8,32,128]{2,1,0:T(8,128)}, f32[64,4096]{1,0:T(8,128)S(1)}, f32[64,64]{1,0:T(8,128)S(1)}) custom-call(s32[8,4]{1,0:T(8,128)S(1)} %copy.9.cols_ref, s32[2]{0:T(128)S(1)} %pad_add_fusion.place_ref, bf16[2,32,40,128]{3,2,1,0:T(8,128)(2,1)S(1)} %pad_maximum_fusion.tiles_own, bf16[2,32,40,128]{3,2,1,0:T(8,128)(2,1)S(1)} %collective-permute-done.3.tiles_near, ...), custom_call_target="tpu_custom_call" | custom-call | tf_op jit(solution)/shard_map/pallas_call | solution.py:386
  98.9 3.4 %all-to-all-start.5 = ((f32[8,32,128]{2,1,0:T(8,128)}), f32[8,32,128]{2,1,0:T(8,128)S(1)}, u32[]{:S(2)}, u32[]{:S(2)}) async-start(f32[8,32,128]{2,1,0:T(8,128)} %get-tuple-element.22), calls=%async_computation.5 | async-start | bytes 262144 | tf_op jit(solution)/shard_map/all_to_all | solution.py:414
  102.3 2.6 %shard_map.65 = (f32[64,2048]{1,0:T(8,128)}, bf16[384,2048]{1,0:T(8,128)(2,1)S(1)}) custom-call(s32[8,4]{1,0:T(8,128)S(1)} %copy.9.cols_ref, s32[2]{0:T(128)S(1)} %pad_add_fusion.place_ref, f32[64,64]{1,0:T(8,128)S(1)} %get-tuple-element.18.scale_ref, f32[64,2048]{1,0:T(8,128)S(1)} %get-tuple-element.19.left_ref, f32[64,4096]{1,0:T(8,128)S(1)} %get-tuple-element.20.total_ref), custom_call_target="tpu_custom_call" | custom-call | tf_op jit(solution)/shard_map/pallas_call | solution.py:386
  105.0 4.9 %all-to-all-done.5.gram_ref = f32[8,32,128]{2,1,0:T(8,128)S(1)} async-done(((f32[8,32,128]{2,1,0:T(8,128)}), f32[8,32,128]{2,1,0:T(8,128)S(1)}, u32[]{:S(2)}, u32[]{:S(2)}) %all-to-all-start.5) | async-done | bytes 131104 | tf_op jit(solution)/shard_map/all_to_all | solution.py:414
  109.8 2.9 %shard_map.66 = f32[64,2048]{1,0:T(8,128)} custom-call(f32[8,32,128]{2,1,0:T(8,128)S(1)} %all-to-all-done.5.gram_ref, f32[64,64]{1,0:T(8,128)S(1)} %get-tuple-element.18.scale_ref, bf16[384,2048]{1,0:T(8,128)(2,1)S(1)} %get-tuple-element.23.parts_ref), custom_call_target="tpu_custom_call" | custom-call | tf_op jit(solution)/shard_map/pallas_call | solution.py:386
  (25 shorter events, 3.6 us)
Async XLA Ops:
  0.6 11.4 %copy-start = (bf16[1,8,128,128]{3,2,1,0:T(8,128)(2,1)S(1)}, bf16[1,8,128,128]{3,2,1,0:T(8,128)(2,1)}, u32[]{:S(2)}) copy-start(bf16[1,8,128,128]{3,2,1,0:T(8,128)(2,1)} %param.4) | copy-start | bytes 786436
  2.6 9.3 %collective-permute-start = (bf16[64,2048]{1,0:T(8,128)(2,1)S(1)}, bf16[64,2048]{1,0:T(8,128)(2,1)S(1)}, u32[]{:S(2)}, u32[]{:S(2)}) collective-permute-start(bf16[64,2048]{1,0:T(8,128)(2,1)S(1)} %get-tuple-element.14), channel_id=1, source_target_pairs={{0,2},{1,3},{2,0},{3,1},{4,6},{5,7},{6,4},{7,5},{8,10},{9,11},{10,... | collective-permute-start | bytes 786440 | tf_op jit(solution)/shard_map/ppermute | solution.py:417
  5.6 16.9 %all-to-all-start = ((bf16[32,40,128]{2,1,0:T(8,128)(2,1)}), bf16[32,40,128]{2,1,0:T(8,128)(2,1)S(1)}, u32[]{:S(2)}, u32[]{:S(2)}) async-start(bf16[32,40,128]{2,1,0:T(8,128)(2,1)} %get-tuple-element.13), calls=%async_computation | async-start | bytes 655360 | tf_op jit(solution)/shard_map/all_to_all | solution.py:440
  12.0 10.6 %collective-permute-start.1 = (bf16[2,64,2048]{2,1,0:T(8,128)(2,1)S(1)}, bf16[2,64,2048]{2,1,0:T(8,128)(2,1)S(1)}, u32[]{:S(2)}, u32[]{:S(2)}) collective-permute-start(bf16[2,64,2048]{2,1,0:T(8,128)(2,1)S(1)} %pad_maximum_fusion.1.own_ref), channel_id=1, source_target_pairs={{0,1},{1,0},{2,3},{3,2},{4,5},{5,4},{6,7},{7,6},{8,9},{9,8},{10,11... | collective-permute-start | bytes 1572872 | tf_op jit(solution)/shard_map/ppermute | solution.py:420
  12.1 15.4 %collective-permute-start.4 = (bf16[8,128,128]{2,1,0:T(8,128)(2,1)S(1)}, bf16[8,128,128]{2,1,0:T(8,128)(2,1)S(1)}, u32[]{:S(2)}, u32[]{:S(2)}) collective-permute-start(bf16[8,128,128]{2,1,0:T(8,128)(2,1)S(1)} %bitcast.22), channel_id=1, source_target_pairs={{0,2},{1,3},{2,0},{3,1},{4,6},{5,7},{6,4},{7,5},{8,10},{9,11},{10,... | collective-permute-start | bytes 786440 | tf_op jit(solution)/shard_map/ppermute | solution.py:417
  24.1 12.4 %all-to-all-start.1 = ((bf16[8,128,128]{2,1,0:T(8,128)(2,1)}), bf16[8,128,128]{2,1,0:T(8,128)(2,1)S(1)}, u32[]{:S(2)}, u32[]{:S(2)}) async-start(bf16[8,128,128]{2,1,0:T(8,128)(2,1)} %get-tuple-element.16), calls=%async_computation.1 | async-start | bytes 524288 | tf_op jit(solution)/shard_map/all_to_all | solution.py:414
  27.6 10.1 %collective-permute-start.5 = (bf16[2,8,128,128]{3,2,1,0:T(8,128)(2,1)S(1)}, bf16[2,8,128,128]{3,2,1,0:T(8,128)(2,1)S(1)}, u32[]{:S(2)}, u32[]{:S(2)}) collective-permute-start(bf16[2,8,128,128]{3,2,1,0:T(8,128)(2,1)S(1)} %pad_maximum_fusion.2.tiles_own), channel_id=1, source_target_pairs={{0,1},{1,0},{2,3},{3,2},{4,5},{5,4},{6,7},{7,6},{8,9},{9,8},{10,11... | collective-permute-start | bytes 1572872 | tf_op jit(solution)/shard_map/ppermute | solution.py:420
  36.4 1.5 %collective-permute-start.6 = (bf16[8,128,128]{2,1,0:T(8,128)(2,1)S(1)}, bf16[8,128,128]{2,1,0:T(8,128)(2,1)S(1)}, u32[]{:S(2)}, u32[]{:S(2)}) collective-permute-start(bf16[8,128,128]{2,1,0:T(8,128)(2,1)S(1)} %all-to-all-done.1.own_ref), channel_id=1, source_target_pairs={{0,1},{1,0},{2,3},{3,2},{4,5},{5,4},{6,7},{7,6},{8,9},{9,8},{10,11... | collective-permute-start | bytes 786440 | tf_op jit(solution)/shard_map/ppermute | solution.py:420
  36.4 10.1 %collective-permute-start.2 = (bf16[32,40,128]{2,1,0:T(8,128)(2,1)S(1)}, bf16[32,40,128]{2,1,0:T(8,128)(2,1)S(1)}, u32[]{:S(2)}, u32[]{:S(2)}) collective-permute-start(bf16[32,40,128]{2,1,0:T(8,128)(2,1)S(1)} %all-to-all-done.moved_ref), channel_id=1, source_target_pairs={{0,2},{1,3},{2,0},{3,1},{4,6},{5,7},{6,4},{7,5},{8,10},{9,11},{10,... | collective-permute-start | bytes 983048 | tf_op jit(solution)/shard_map/ppermute | solution.py:417
  40.7 14.2 %all-to-all-start.2 = ((bf16[8,160,128]{2,1,0:T(8,128)(2,1)}), bf16[8,160,128]{2,1,0:T(8,128)(2,1)S(1)}, u32[]{:S(2)}, u32[]{:S(2)}) async-start(bf16[8,160,128]{2,1,0:T(8,128)(2,1)} %shard_map.61), calls=%async_computation.2 | async-start | bytes 655360 | tf_op jit(solution)/shard_map/all_to_all | solution.py:414
  46.6 8.6 %collective-permute-start.3 = (bf16[2,32,40,128]{3,2,1,0:T(8,128)(2,1)S(1)}, bf16[2,32,40,128]{3,2,1,0:T(8,128)(2,1)S(1)}, u32[]{:S(2)}, u32[]{:S(2)}) collective-permute-start(bf16[2,32,40,128]{3,2,1,0:T(8,128)(2,1)S(1)} %pad_maximum_fusion.tiles_own), channel_id=1, source_target_pairs={{0,1},{1,0},{2,3},{3,2},{4,5},{5,4},{6,7},{7,6},{8,9},{9,8},{10,11... | collective-permute-start | bytes 1966088 | tf_op jit(solution)/shard_map/ppermute | solution.py:420
  54.9 1.6 %collective-permute-start.7 = (bf16[8,160,128]{2,1,0:T(8,128)(2,1)S(1)}, bf16[8,160,128]{2,1,0:T(8,128)(2,1)S(1)}, u32[]{:S(2)}, u32[]{:S(2)}) collective-permute-start(bf16[8,160,128]{2,1,0:T(8,128)(2,1)S(1)} %all-to-all-done.2.own_ref), channel_id=1, source_target_pairs={{0,1},{1,0},{2,3},{3,2},{4,5},{5,4},{6,7},{7,6},{8,9},{9,8},{10,11... | collective-permute-start | bytes 983048 | tf_op jit(solution)/shard_map/ppermute | solution.py:420
  74.5 1.6 %collective-permute-start.8 = (bf16[8,160,128]{2,1,0:T(8,128)(2,1)S(1)}, bf16[8,160,128]{2,1,0:T(8,128)(2,1)S(1)}, u32[]{:S(2)}, u32[]{:S(2)}) collective-permute-start(bf16[8,160,128]{2,1,0:T(8,128)(2,1)S(1)} %all_to_all.30.own_ref), channel_id=1, source_target_pairs={{0,1},{1,0},{2,3},{3,2},{4,5},{5,4},{6,7},{7,6},{8,9},{9,8},{10,11... | collective-permute-start | bytes 983048 | tf_op jit(solution)/shard_map/ppermute | solution.py:420
  93.3 1.6 %collective-permute-start.9 = (bf16[8,160,128]{2,1,0:T(8,128)(2,1)S(1)}, bf16[8,160,128]{2,1,0:T(8,128)(2,1)S(1)}, u32[]{:S(2)}, u32[]{:S(2)}) collective-permute-start(bf16[8,160,128]{2,1,0:T(8,128)(2,1)S(1)} %all_to_all.31.own_ref), channel_id=1, source_target_pairs={{0,1},{1,0},{2,3},{3,2},{4,5},{5,4},{6,7},{7,6},{8,9},{9,8},{10,11... | collective-permute-start | bytes 983048 | tf_op jit(solution)/shard_map/ppermute | solution.py:420
  98.9 10.9 %all-to-all-start.5 = ((f32[8,32,128]{2,1,0:T(8,128)}), f32[8,32,128]{2,1,0:T(8,128)S(1)}, u32[]{:S(2)}, u32[]{:S(2)}) async-start(f32[8,32,128]{2,1,0:T(8,128)} %get-tuple-element.22), calls=%async_computation.5 | async-start | bytes 262144 | tf_op jit(solution)/shard_map/all_to_all | solution.py:414

commit v5 on v4

--- a/solution.py
+++ b/solution.py
@@ -12,7 +12,7 @@
 ROW_TILES = 16
 F32 = jnp.float32
 BF16 = jnp.bfloat16
-VMEM_BYTES = 48 * 1024 * 1024
+MIB = 1024 * 1024
 NT = (((1,), (1,)), ((), ()))
 NN = (((1,), (0,)), ((), ()))
 
@@ -121,24 +121,48 @@
         lax.fori_loop(0, count // step, several, 0)
 
 
-def beside(steps, tasks, count):
-    if count > 8:
+def beside(steps, tasks):
+    if max(count for _, count in tasks) > 8:
         run(steps)
-        for task in tasks:
-            each(count, task)
+        for body, count in tasks:
+            each(count, body)
         return
+    tasks = [functools.partial(body, i) for body, count in tasks for i in range(count)]
     panels = 8
-    done = 0
-    for n in range(1, panels + 1):
+    for n in range(panels):
         next(steps, None)
-        while done < len(tasks) * count * n // panels:
-            tasks[done // count](done % count)
-            done += 1
+        for task in tasks[len(tasks) * n // panels : len(tasks) * (n + 1) // panels]:
+            task()
     run(steps)
 
 
-def pack_kernel(rows_hbm, cols_hbm, tiles_hbm, start_hbm, out_ref, start_out, rows_ref, cols_ref, tiles_ref, start_ref, sems):
-    pairs = ((rows_hbm, rows_ref), (cols_hbm, cols_ref), (start_hbm, start_ref), (tiles_hbm, tiles_ref))
+def lanes(index, size):
+    return pl.ds(index * size if isinstance(index, int) else pl.multiple_of(index * size, size), size)
+
+
+def add_gram(total, raw_gram, chunk):
+    def add(o):
+        raw_gram[...] += gram_of_parts(jnp.concatenate(two_parts(total[:, lanes(o, chunk)]), axis=0))
+
+    return add
+
+
+def scaled_gram(scale, raw_gram):
+    width = scale.shape[0]
+    once = exact_dot(scale, raw_gram[:, 0:width])
+    return lax.dot_general(
+        once,
+        jnp.concatenate([scale, scale], axis=0),
+        NT,
+        precision=lax.Precision.HIGHEST,
+        preferred_element_type=F32,
+    )
+
+
+def pack_kernel(
+    rows_hbm, cols_hbm, tiles_hbm, start_hbm, out_hbm, start_out, rows_ref, cols_ref, tiles_ref, start_ref, out_ref, sems
+):
+    pairs = ((rows_hbm, rows_ref), (cols_hbm, cols_ref), (tiles_hbm, tiles_ref), (start_hbm, start_ref))
     copies = [pltpu.make_async_copy(source, to, sems.at[n]) for n, (source, to) in enumerate(pairs)]
     for copy in copies:
         copy.start()
@@ -152,16 +176,19 @@
         places = jnp.where(lane == j, rows_ref[0, j], jnp.where(lane == held + j, cols_ref[0, j], places))
     places = places.astype(F32).astype(BF16)
     copies[2].wait()
-    start_out[...] = start_ref[...].astype(BF16)
-    copies[3].wait()
 
     def pack(i):
         out_ref[i] = jnp.concatenate([tiles_ref[i], places], axis=0)
 
     each(count, pack, 32)
-
-
-def choose_kernel(place_ref, moved_ref, own_ref, near_ref, out_ref, places_ref):
+    packed = pltpu.make_async_copy(out_ref, out_hbm, sems.at[4])
+    packed.start()
+    copies[3].wait()
+    start_out[...] = start_ref[...].astype(BF16)
+    packed.wait()
+
+
+def choose_kernel(place_ref, moved_ref, own_ref, near_ref, out_hbm, places_ref, out_ref, sems):
     rep, block = place_ref[0], place_ref[1]
     core = lax.rem(rep, 2)
     blocks, _, tile = out_ref.shape
@@ -184,8 +211,11 @@
             mine = own_ref[far, :, pl.ds(at, tile)]
             theirs = near_ref[far, :, pl.ds(at, tile)]
             out_ref[b, x * width : (x + 1) * width, :] = jnp.where(lax.rem(away, 2) == 0, mine, theirs)
+        pltpu.make_async_copy(out_ref.at[b], out_hbm.at[b], sems.at[b]).start()
 
     each(blocks, choose)
+    for b in range(blocks):
+        pltpu.make_async_copy(out_ref.at[b], out_hbm.at[b], sems.at[b]).wait()
 
 
 def find_slots(cols_ref, slots_ref, first_at):
@@ -207,7 +237,7 @@
 def left_kernel(first, last, rows_ref, place_ref, tiles_own, tiles_near, own_ref, other_ref, out_ref, *rest):
     if last:
         raw_ref, *rest = rest
-    total, stacked, packed, work, spread = rest
+    total, stacked, packed, work, spread, raw_gram, *sems = rest
     core = lax.rem(place_ref[0], 2)
     pieces, _, tile = own_ref.shape
     width = total.shape[0]
@@ -228,18 +258,49 @@
                 at = pl.multiple_of(rows_ref[rep, p] * tile, tile)
                 total[:, pl.ds(at, tile)] += product
 
-            tasks.append(add)
-    beside(steps, tasks, pieces)
-    value = total[...]
+            tasks.append((add, pieces))
+    chunk = 4 * tile
     if not first:
-        value = apply_scale(two_parts(work[:, 0:width]), value)
-    if last:
-        raw_ref[...] = value
-    high, low = two_parts(value)
-    stacked[0:width, :] = high
-    stacked[width:, :] = low
-    pack_gram(gram_of_parts(stacked[...]), packed)
-    mine = packed[pl.ds(pl.multiple_of(core * half, half), half), :]
+        raw_gram[...] = jnp.zeros_like(raw_gram)
+        tasks.append((add_gram(total, raw_gram, chunk), total.shape[1] // chunk))
+    beside(steps, tasks)
+    mine = pl.ds(pl.multiple_of(core * half, half), half)
+    if first:
+        stacked[...] = jnp.concatenate(two_parts(total[...]), axis=0)
+        copies = []
+        for p in range(pieces):
+            for x in range(2):
+                at = pl.multiple_of(rows_ref[x * 2 + core, p] * tile, tile)
+                copies.append(
+                    pltpu.make_async_copy(
+                        stacked.at[pl.ds(0, width), pl.ds(at, tile)],
+                        out_ref.at[p, pl.ds(x * width, width), :],
+                        sems[0].at[p, x],
+                    )
+                )
+                copies[-1].start()
+        pack_gram(gram_of_parts(stacked[...]), packed)
+        for p in range(pieces):
+            copies.append(
+                pltpu.make_async_copy(packed.at[mine, :], out_ref.at[p, pl.ds(2 * width, half), :], sems[0].at[p, 2])
+            )
+            copies[-1].start()
+        for copy in copies:
+            copy.wait()
+        return
+    scale = work[:, 0:width]
+    pack_gram(scaled_gram(scale, raw_gram), packed)
+    scale = two_parts(scale)
+
+    def apply(o):
+        at = lanes(o, chunk)
+        value = apply_scale(scale, total[:, at])
+        if last:
+            raw_ref[:, at] = value
+        stacked[0:width, at] = value.astype(BF16)
+
+    each(total.shape[1] // chunk, apply)
+    mine = packed[mine, :]
 
     def send(p):
         for x in range(2):
@@ -256,62 +317,77 @@
     packed[...] = jnp.where(lane < gram_twice.shape[0], high.astype(F32), low.astype(F32)).astype(BF16)
 
 
-def right_kernel(last, cols_ref, place_ref, tiles_own, tiles_near, own_ref, other_ref, out_ref, *rest):
-    if last:
-        total, scale_ref, *rest = rest
-    else:
-        total, *rest = rest
-    stacked, packed, work, spread, quarters, slots_ref, first_at = rest
+def slots_kernel(cols_ref, slots_ref, first_at):
+    find_slots(cols_ref, slots_ref, first_at)
+
+
+def place_quarters(place_ref, tiles_own, tiles_near, quarters):
+    quarter = quarters.shape[2]
+    for far in range(2):
+        for near, source in enumerate((tiles_own, tiles_near)):
+            quarters[lax.bitwise_xor(place_ref[0], 2 * far + near)] = source[far, :, 0:quarter, :]
+
+
+def right_tasks(place_ref, slots_ref, quarters, own_ref, other_ref, total, raw_gram):
+    core = lax.rem(place_ref[0], 2)
+    blocks, _, tile = own_ref.shape
+    width = total.shape[0]
+    total[...] = jnp.zeros_like(total)
+    raw_gram[...] = jnp.zeros_like(raw_gram)
+    tasks = []
+    for x in range(2):
+        for source, at_core in ((own_ref, core), (other_ref, 1 - core)):
+
+            def add(b, source=source, x=x, rep=x * 2 + at_core):
+                stored = jnp.concatenate([quarters[q, b * 4 + rep] for q in range(4)], axis=0)
+                product = dot(source[b, x * width : (x + 1) * width, :], stored, NN)
+                at = pl.multiple_of(slots_ref[b, rep] * tile, tile)
+                total[:, pl.ds(at, tile)] += product
+
+            tasks.append((add, blocks))
+    chunk = 8 * tile
+    tasks.append((add_gram(total, raw_gram, chunk), total.shape[1] // chunk))
+    return tasks
+
+
+def right_kernel(
+    cols_ref,
+    place_ref,
+    tiles_own,
+    tiles_near,
+    own_ref,
+    other_ref,
+    out_ref,
+    total,
+    stacked,
+    packed,
+    work,
+    spread,
+    raw_gram,
+    quarters,
+    slots_ref,
+    first_at,
+):
     find_slots(cols_ref, slots_ref, first_at)
     core = lax.rem(place_ref[0], 2)
     blocks, _, tile = own_ref.shape
     width = total.shape[0]
     half = width // 2
-    quarter = quarters.shape[2]
-    for far in range(2):
-        for near, source in enumerate((tiles_own, tiles_near)):
-            quarters[lax.bitwise_xor(place_ref[0], 2 * far + near)] = source[far, :, 0:quarter, :]
-
-    def stored(b, r):
-        return jnp.concatenate([quarters[q, b * 4 + r] for q in range(4)], axis=0)
-
+    place_quarters(place_ref, tiles_own, tiles_near, quarters)
     gather_gram(work, own_ref, other_ref, core)
-    steps = eliminate(work, spread)
-    total[...] = jnp.zeros_like(total)
-
-    tasks = []
-    for x in range(2):
-        for source, at_core in ((own_ref, core), (other_ref, 1 - core)):
-
-            def add(b, source=source, x=x, rep=x * 2 + at_core):
-                product = dot(source[b, x * width : (x + 1) * width, :], stored(b, rep), NN)
-                at = pl.multiple_of(slots_ref[b, rep] * tile, tile)
-                total[:, pl.ds(at, tile)] += product
-
-            tasks.append(add)
-    beside(steps, tasks, blocks)
+    beside(
+        eliminate(work, spread), right_tasks(place_ref, slots_ref, quarters, own_ref, other_ref, total, raw_gram)
+    )
     scale = work[:, 0:width]
+    pack_gram(scaled_gram(scale, raw_gram), packed)
     scale_parts = two_parts(scale)
     chunk = 8 * tile
 
     def apply(o):
-        at = o * chunk if isinstance(o, int) else pl.multiple_of(o * chunk, chunk)
-        high, low = two_parts(apply_scale(scale_parts, total[:, pl.ds(at, chunk)]))
-        stacked[0:width, pl.ds(at, chunk)] = high
-        stacked[width:, pl.ds(at, chunk)] = low
+        at = lanes(o, chunk)
+        stacked[0:width, at] = apply_scale(scale_parts, total[:, at]).astype(BF16)
 
     each(total.shape[1] // chunk, apply)
-    gram = gram_of_parts(stacked[...])
-    if last:
-        scale_ref[...] = scale
-        both = jnp.concatenate([gram[0:half, 0:width], gram[half:, 0:width]], axis=1)
-
-        def send(b):
-            out_ref[b] = both
-
-        each(blocks, send)
-        return
-    pack_gram(gram, packed)
     mine = packed[pl.ds(pl.multiple_of(core * half, half), half), :]
 
     def send(b):
@@ -323,18 +399,54 @@
     each(blocks, send)
 
 
-def three_parts(value):
-    high, low = two_parts(value)
-    rest = value - high.astype(F32)
-    return high, low, (rest - low.astype(F32)).astype(BF16)
+def last_right_kernel(
+    slots_ref, place_ref, tiles_own, tiles_near, own_ref, other_ref, gram_hbm, total, raw_gram, quarters, sems
+):
+    place_quarters(place_ref, tiles_own, tiles_near, quarters)
+    beside(iter(()), right_tasks(place_ref, slots_ref, quarters, own_ref, other_ref, total, raw_gram))
+    width = total.shape[0]
+    half = width // 2
+    lane = lax.broadcasted_iota(jnp.int32, (half, 2 * width), 1)
+    raw_gram[0:half, :] = jnp.where(lane < width, raw_gram[0:half, :], raw_gram[half:, :])
+    copies = [
+        pltpu.make_async_copy(raw_gram.at[pl.ds(0, half), :], gram_hbm.at[b], sems.at[b])
+        for b in range(gram_hbm.shape[0])
+    ]
+    for copy in copies:
+        copy.start()
+    for copy in copies:
+        copy.wait()
 
 
 def between_kernel(
-    factor, cols_ref, place_ref, scale_ref, left_ref, total_ref, left_out, parts_ref, share, slots_ref, first_at
+    left_factor,
+    right_factor,
+    cols_ref,
+    slots_ref,
+    place_ref,
+    tiles_own,
+    tiles_near,
+    own_ref,
+    other_ref,
+    left_ref,
+    left_out,
+    parts_ref,
+    scale_ref,
+    share,
+    work,
+    spread,
+    total_ref,
+    raw_gram,
+    quarters,
 ):
+    place_quarters(place_ref, tiles_own, tiles_near, quarters)
+    gather_gram(work, own_ref, other_ref, lax.rem(place_ref[0], 2))
+    products = right_tasks(place_ref, slots_ref, quarters, own_ref, other_ref, total_ref, raw_gram)[:-1]
+    beside(eliminate(work, spread), products)
+    scale_ref[...] = work[:, 0 : scale_ref.shape[1]]
+    left_out[...] = exact_dot(scale_ref[...] * left_factor, left_ref[...])
     width, tile = share.shape[0], total_ref.shape[1] // (slots_ref.shape[0] * 4)
     shares = share.shape[1] // tile
-    find_slots(cols_ref, slots_ref, first_at)
     share[...] = jnp.zeros_like(share)
 
     def keep(b):
@@ -348,29 +460,27 @@
                 share[:, pl.ds(to, tile)] = total_ref[:, pl.ds(at, tile)]
 
     each(slots_ref.shape[0], keep)
-    high, middle, low = three_parts(share[...])
-    for n, part in enumerate((high, middle, high, low, high, middle)):
+    for n, part in enumerate(two_parts(apply_scale(two_parts(scale_ref[...] * right_factor), share[...]))):
         parts_ref[n * width : (n + 1) * width, :] = part
-    left_out[...] = exact_dot(scale_ref[...] * factor, left_ref[...])
-
-
-def finish_kernel(factor, gram_ref, scale_ref, parts_ref, right_hbm, work, spread, right, sems):
+
+
+def finish_kernel(gram_ref, scale_ref, parts_ref, right_hbm, work, spread, right, sems):
     width = scale_ref.shape[0]
     half = width // 2
     total = gram_ref[0]
     for b in range(1, gram_ref.shape[0]):
         total = total + gram_ref[b]
+    gram = scaled_gram(scale_ref[...], jnp.concatenate([total[:, 0:width], total[:, width:]], axis=0))
     put_identity(work)
-    work[0:half, width:] = total[:, 0:width]
-    work[half:, width:] = total[:, width:]
+    work[:, width:] = gram[:, width:]
     run(eliminate(work, spread))
-    high, middle, low = three_parts(exact_dot(work[:, 0:width], scale_ref[...]) * factor)
-    scale = jnp.concatenate([high, high, middle, high, low, middle], axis=1)
+    high, low = two_parts(work[:, 0:width])
+    scale = jnp.concatenate([high, high], axis=1)
     chunk = right.shape[1] // 4
     copies = []
     for n in range(4):
         at = pl.ds(n * chunk, chunk)
-        right[:, at] = dot(scale, parts_ref[:, at], NN)
+        right[:, at] = dot(scale, parts_ref[:, at], NN) + dot(low, parts_ref[0:width, at], NN)
         copies.append(pltpu.make_async_copy(right.at[:, at], right_hbm.at[:, at], sems.at[n]))
         copies[-1].start()
     for copy in copies:
@@ -383,14 +493,15 @@
 
 
 def call(kernel, outs, smem, held, vmem, scratch=(), out_specs=None):
+    held = [pltpu.with_memory_space_constraint(value, pltpu.HBM) for value in held]
     return pl.pallas_call(
         kernel,
         out_shape=outs,
         in_specs=[SMEM] * len(smem) + [HBM] * len(held) + [VMEM] * len(vmem),
         out_specs=out_specs or [VMEM] * len(outs),
         scratch_shapes=list(scratch),
-        compiler_params=pltpu.CompilerParams(vmem_limit_bytes=VMEM_BYTES),
-    )(*smem, *[pltpu.with_memory_space_constraint(value, pltpu.HBM) for value in held], *vmem)
+        compiler_params=pltpu.CompilerParams(vmem_limit_bytes=min(48, lax.axis_size("blk") + 8) * MIB),
+    )(*smem, *held, *vmem)
 
 
 def local(tiles, tile_rows, tile_cols, start_right):
@@ -430,13 +541,13 @@
             pltpu.SMEM(tile_cols.shape, jnp.int32),
             pltpu.VMEM((count, quarter, tile), BF16),
             pltpu.VMEM((width, share), F32),
-            pltpu.SemaphoreType.DMA((4,)),
+            pltpu.VMEM((count, quarter + 8, tile), BF16),
+            pltpu.SemaphoreType.DMA((5,)),
         ],
+        [HBM, VMEM],
     )
     start_own = jnp.stack([start, swap_x(start)])
     start_near = swap_core(start_own)
-    tiles_own = jnp.stack([flat_tiles, swap_x(flat_tiles)])
-    tiles_near = swap_core(tiles_own)
     moved = lax.all_to_all(moved, ("blk", "rep"), split_axis=0, concat_axis=0, tiled=True)
     chosen, places = call(
         choose_kernel,
@@ -444,7 +555,12 @@
         [place],
         [],
         [moved, start_own, start_near],
-    )
+        [pltpu.VMEM((blocks, 2 * width, tile), BF16), pltpu.SemaphoreType.DMA((blocks,))],
+        [HBM, VMEM],
+    )
+    flat_tiles, moved = lax.optimization_barrier((flat_tiles, moved))
+    tiles_own = jnp.stack([flat_tiles, swap_x(flat_tiles)])
+    tiles_near = swap_core(tiles_own)
     columns_own = jnp.stack([moved, swap_x(moved)])
     columns_near = swap_core(columns_own)
     places = places[:, 0, 0 : 2 * held].reshape(blocks, group, 2 * held)
@@ -469,49 +585,60 @@
             [tiles_own, tiles_near, chosen, swap_core(chosen)],
             [
                 pltpu.VMEM((width, ROW_TILES * tile), F32),
-                pltpu.VMEM((2 * width, ROW_TILES * tile), BF16),
+                pltpu.VMEM((2 * width if first else width, ROW_TILES * tile), BF16),
                 packed,
                 work,
                 spread,
-            ],
+                pltpu.VMEM((width, 2 * width), F32),
+            ]
+            + ([pltpu.SemaphoreType.DMA((blocks, 3))] if first else []),
+            [HBM] if first else None,
         )
         picked = across(results[0])
         left_raw = results[-1]
-        outs = [shape((blocks, packed_rows, tile), BF16)]
+        total = pltpu.VMEM((width, count * tile), F32)
+        gram_scratch = pltpu.VMEM((width, 2 * width), F32)
+        quarters = pltpu.VMEM((group, count, quarter, tile), BF16)
+        other = swap_core(picked)
         if last:
-            outs = [
-                shape((blocks, width // 2, 2 * width), F32),
-                shape((width, count * tile), F32),
-                shape((width, width), F32),
-            ]
-        results = call(
-            functools.partial(right_kernel, last),
-            outs,
+            break
+        (chosen,) = call(
+            right_kernel,
+            [shape((blocks, packed_rows, tile), BF16)],
             [cols_here, place],
             [],
-            [columns_own, columns_near, picked, swap_core(picked)],
-            ([] if last else [pltpu.VMEM((width, count * tile), F32)])
-            + [
-                pltpu.VMEM((2 * width, count * tile), BF16),
-                packed,
-                work,
-                spread,
-            ]
-            + [pltpu.VMEM((group, count, quarter, tile), BF16)]
+            [columns_own, columns_near, picked, other],
+            [total, pltpu.VMEM((width, count * tile), BF16), packed, work, spread, gram_scratch, quarters]
             + slot_scratch,
         )
-        chosen = results[0]
-    gram, right_total, left_scale = results
-    left, parts = call(
-        functools.partial(between_kernel, math.sqrt(total_rows)),
-        [shape(left_raw.shape, F32), shape((6 * width, share), BF16)],
-        [cols_here, place],
-        [],
-        [left_scale, left_raw, right_total],
-        [pltpu.VMEM((width, share), F32)] + slot_scratch,
+    (slots,) = call(
+        slots_kernel,
+        [shape(cols_here.shape, jnp.int32)],
+        [cols_here],
+        [],
+        [],
+        slot_scratch[1:],
+        [SMEM],
+    )
+    (gram,) = call(
+        last_right_kernel,
+        [shape((blocks, width // 2, 2 * width), F32)],
+        [slots, place],
+        [],
+        [columns_own, columns_near, picked, other],
+        [total, gram_scratch, quarters, pltpu.SemaphoreType.DMA((blocks,))],
+        [HBM],
+    )
+    left, parts, left_scale = call(
+        functools.partial(between_kernel, math.sqrt(total_rows), math.sqrt(total_cols)),
+        [shape(left_raw.shape, F32), shape((2 * width, share), BF16), shape((width, width), F32)],
+        [cols_here, slots, place],
+        [],
+        [columns_own, columns_near, picked, other, left_raw],
+        [pltpu.VMEM((width, share), F32), work, spread, total, gram_scratch, quarters],
     )
     (right,) = call(
-        functools.partial(finish_kernel, math.sqrt(total_cols)),
+        finish_kernel,
         [shape((width, share), F32)],
         [],
         [],

time: 113 us -> 113 us (level)
  starting transfers between devices: 21.4 us -> 19.8 us
  Pallas kernels: 22.2 us -> 23.6 us
    all_to_all x3, waiting for transfers between devices: 21.9 us -> 18.7 us  [across(): return lax.all_to_all(value, 'blk', split_axis=0, concat_axis=0, tiled=True)]
    ppermute x3, waiting for transfers between devices: 3.7 us -> 5.73 us  [swap_x(): return lax.ppermute(value, 'rep', [(i, i ^ 2) for i in range(group)])]
    ppermute x3, starting transfers between devices: 5.94 us -> 4.05 us  [swap_x(): return lax.ppermute(value, 'rep', [(i, i ^ 2) for i in range(group)])]
    all_to_all x1, waiting for transfers between devices: 8.6 us -> 10.5 us  [local(): lax.all_to_all(moved, ('blk', 'rep'), split_axis=0, concat_axis=0, tiled=...]
    pallas_call x8 -> x9, Pallas kernels: 22.2 us -> 23.6 us  [call(): pl.pallas_call(kernel, out_shape=outs, in_specs=[SMEM] * len(smem) + [HBM...]
  transfers between devices with their start and end apart: 14 -> 14, of which waited for: 10 -> 11; matrix products, arithmetic and copies ran while one was open for 0% -> 0% of each run, Pallas kernels for 6% -> 9%
where the time goes in v5:
time: 113 us; the launch traced here: 112 us
  waiting for transfers between devices  38.9 us (34%)
  blocking collectives  28.6 us (25%)
  Pallas kernels  23.6 us (21%)
  starting transfers between devices  19.8 us (18%)
    all_to_all x2, blocking collectives, across(): return lax.all_to_all(value, 'blk', split_axis=0, concat_axis=0, tiled=True)  28.6 us
    pallas_call x9, Pallas kernels, call(): pl.pallas_call(kernel, out_shape=outs, in_specs=[SMEM] * len(smem) + [HBM...  23.6 us
    all_to_all x3, waiting for transfers between devices, across(): return lax.all_to_all(value, 'blk', split_axis=0, concat_axis=0, tiled=True)  18.7 us
    all_to_all x3, starting transfers between devices, across(): return lax.all_to_all(value, 'blk', split_axis=0, concat_axis=0, tiled=True)  10.6 us
    all_to_all x1, waiting for transfers between devices, local(): lax.all_to_all(moved, ('blk', 'rep'), split_axis=0, concat_axis=0, tiled=...  10.5 us
    ppermute x3, waiting for transfers between devices, swap_x(): return lax.ppermute(value, 'rep', [(i, i ^ 2) for i in range(group)])  5.73 us
    all_to_all x1, starting transfers between devices, local(): lax.all_to_all(moved, ('blk', 'rep'), split_axis=0, concat_axis=0, tiled=...  4.92 us
    ppermute x3, starting transfers between devices, swap_x(): return lax.ppermute(value, 'rep', [(i, i ^ 2) for i in range(group)])  4.05 us
  transfers between devices with their start and end apart: 14, of which 11 were waited for; matrix products, arithmetic and copies ran while one was open for 0% of the time, Pallas kernels for 9%

profile of v5, /device:TPU:0, one launch (start us, length us, event | category | flops | bytes accessed | tf_op | source)
XLA Modules:
  0.0 112.2 jit_solution(17563302130861535051)
XLA Ops:
  0.6 1.8 %shard_map.59 = (bf16[32,40,128]{2,1,0:T(8,128)(2,1)}, bf16[64,2048]{1,0:T(8,128)(2,1)S(1)}) custom-call(s32[1,8]{1,0:T(1,128)} %rows_hbm.1, s32[1,8]{1,0:T(1,128)} %cols_hbm.1, bf16[32,32,128]{2,1,0:T(8,128)(2,1)} %bitcast.22, f32[64,2048]{1,0:T(8,128)} %bitcast.25), custom_call_target="tpu_custom_call" | custom-call | tf_op jit(solution)/shard_map/pallas_call | solution.py:497
  2.4 3.0 %collective-permute-start = (bf16[64,2048]{1,0:T(8,128)(2,1)S(1)}, bf16[64,2048]{1,0:T(8,128)(2,1)S(1)}, u32[]{:S(2)}, u32[]{:S(2)}) collective-permute-start(bf16[64,2048]{1,0:T(8,128)(2,1)S(1)} %get-tuple-element.14), channel_id=1, source_target_pairs={{0,2},{1,3},{2,0},{3,1},{4,6},{5,7},{6,4},{7,5},{8,10},{9,11},{10,... | collective-permute-start | bytes 786440 | tf_op jit(solution)/shard_map/ppermute | solution.py:528
  5.4 4.9 %all-to-all-start = ((bf16[32,40,128]{2,1,0:T(8,128)(2,1)}), bf16[32,40,128]{2,1,0:T(8,128)(2,1)S(1)}, u32[]{:S(2)}, u32[]{:S(2)}) async-start(bf16[32,40,128]{2,1,0:T(8,128)(2,1)} %get-tuple-element.13), calls=%async_computation | async-start | bytes 655360 | tf_op jit(solution)/shard_map/all_to_all | solution.py:551
  10.3 1.4 %collective-permute-done = bf16[64,2048]{1,0:T(8,128)(2,1)S(1)} collective-permute-done((bf16[64,2048]{1,0:T(8,128)(2,1)S(1)}, bf16[64,2048]{1,0:T(8,128)(2,1)S(1)}, u32[]{:S(2)}, u32[]{:S(2)}) %collective-permute-start) | collective-permute-done | bytes 262176 | tf_op jit(solution)/shard_map/ppermute | solution.py:528
  11.9 10.5 %all-to-all-done.moved_ref = bf16[32,40,128]{2,1,0:T(8,128)(2,1)S(1)} async-done(((bf16[32,40,128]{2,1,0:T(8,128)(2,1)}), bf16[32,40,128]{2,1,0:T(8,128)(2,1)S(1)}, u32[]{:S(2)}, u32[]{:S(2)}) %all-to-all-start) | async-done | bytes 327712 | tf_op jit(solution)/shard_map/all_to_all | solution.py:551
  22.7 1.7 %shard_map.60 = (bf16[8,128,128]{2,1,0:T(8,128)(2,1)}, s32[32,8,128]{2,1,0:T(8,128)S(1)}) custom-call(s32[2]{0:T(128)S(1)} %pad_add_fusion.place_ref, bf16[32,40,128]{2,1,0:T(8,128)(2,1)S(1)} %all-to-all-done.moved_ref, bf16[2,64,2048]{2,1,0:T(8,128)(2,1)S(1)} %pad_maximum_fusion.1.own_ref, bf16[2,64,2048]{2,1,0:T(8,128)(2,1)S(1)} %collective-permute-done.1.near_ref), custom_call_target="tpu_custom_call" | custom-call | tf_op jit(solution)/shard_map/pallas_call | solution.py:497
  24.3 3.6 %all-to-all-start.1 = ((bf16[8,128,128]{2,1,0:T(8,128)(2,1)}), bf16[8,128,128]{2,1,0:T(8,128)(2,1)S(1)}, u32[]{:S(2)}, u32[]{:S(2)}) async-start(bf16[8,128,128]{2,1,0:T(8,128)(2,1)} %get-tuple-element.18), calls=%async_computation.1 | async-start | bytes 524288 | tf_op jit(solution)/shard_map/all_to_all | solution.py:525
  28.0 2.1 %collective-permute-done.4 = bf16[8,128,128]{2,1,0:T(8,128)(2,1)S(1)} collective-permute-done((bf16[8,128,128]{2,1,0:T(8,128)(2,1)S(1)}, bf16[8,128,128]{2,1,0:T(8,128)(2,1)S(1)}, u32[]{:S(2)}, u32[]{:S(2)}) %collective-permute-start.4) | collective-permute-done | bytes 262176 | tf_op jit(solution)/shard_map/ppermute | solution.py:528
  30.2 7.1 %all-to-all-done.1.own_ref = bf16[8,128,128]{2,1,0:T(8,128)(2,1)S(1)} async-done(((bf16[8,128,128]{2,1,0:T(8,128)(2,1)}), bf16[8,128,128]{2,1,0:T(8,128)(2,1)S(1)}, u32[]{:S(2)}, u32[]{:S(2)}) %all-to-all-start.1) | async-done | bytes 262176 | tf_op jit(solution)/shard_map/all_to_all | solution.py:525
  38.9 2.8 %shard_map.62 = bf16[8,160,128]{2,1,0:T(8,128)(2,1)} custom-call(s32[4,8]{1,0:T(4,128)S(1)} %bitcast.20, s32[2]{0:T(128)S(1)} %pad_add_fusion.place_ref, bf16[2,8,128,128]{3,2,1,0:T(8,128)(2,1)S(1)} %pad_maximum_fusion.2.tiles_own, bf16[2,8,128,128]{3,2,1,0:T(8,128)(2,1)S(1)} %collective-permute-done.5.tiles_near, ...), custom_call_target="tpu_custom_call" | custom-call | tf_op jit(solution)/shard_map/pallas_call | solution.py:497
  41.6 3.6 %all-to-all-start.2 = ((bf16[8,160,128]{2,1,0:T(8,128)(2,1)}), bf16[8,160,128]{2,1,0:T(8,128)(2,1)S(1)}, u32[]{:S(2)}, u32[]{:S(2)}) async-start(bf16[8,160,128]{2,1,0:T(8,128)(2,1)} %shard_map.62), calls=%async_computation.2 | async-start | bytes 655360 | tf_op jit(solution)/shard_map/all_to_all | solution.py:525
  45.2 2.2 %collective-permute-done.2 = bf16[32,40,128]{2,1,0:T(8,128)(2,1)S(1)} collective-permute-done((bf16[32,40,128]{2,1,0:T(8,128)(2,1)S(1)}, bf16[32,40,128]{2,1,0:T(8,128)(2,1)S(1)}, u32[]{:S(2)}, u32[]{:S(2)}) %collective-permute-start.2) | collective-permute-done | bytes 327712 | tf_op jit(solution)/shard_map/ppermute | solution.py:528
  47.6 8.3 %all-to-all-done.2.own_ref = bf16[8,160,128]{2,1,0:T(8,128)(2,1)S(1)} async-done(((bf16[8,160,128]{2,1,0:T(8,128)(2,1)}), bf16[8,160,128]{2,1,0:T(8,128)(2,1)S(1)}, u32[]{:S(2)}, u32[]{:S(2)}) %all-to-all-start.2) | async-done | bytes 327712 | tf_op jit(solution)/shard_map/all_to_all | solution.py:525
  56.1 1.4 %collective-permute-done.7.other_ref = bf16[8,160,128]{2,1,0:T(8,128)(2,1)S(1)} collective-permute-done((bf16[8,160,128]{2,1,0:T(8,128)(2,1)S(1)}, bf16[8,160,128]{2,1,0:T(8,128)(2,1)S(1)}, u32[]{:S(2)}, u32[]{:S(2)}) %collective-permute-start.7) | collective-permute-done | bytes 327712 | tf_op jit(solution)/shard_map/ppermute | solution.py:531
  57.5 3.2 %shard_map.63 = bf16[8,160,128]{2,1,0:T(8,128)(2,1)S(1)} custom-call(s32[8,4]{1,0:T(8,128)S(1)} %copy.9.cols_ref, s32[2]{0:T(128)S(1)} %pad_add_fusion.place_ref, bf16[2,32,40,128]{3,2,1,0:T(8,128)(2,1)S(1)} %pad_maximum_fusion.tiles_own, bf16[2,32,40,128]{3,2,1,0:T(8,128)(2,1)S(1)} %collective-permute-done.3.tiles_near, ...), custom_call_target="tpu_custom_call" | custom-call | tf_op jit(solution)/shard_map/pallas_call | solution.py:497
  60.7 14.6 %all_to_all.30.own_ref = bf16[8,160,128]{2,1,0:T(8,128)(2,1)S(1)} all-to-all(bf16[8,160,128]{2,1,0:T(8,128)(2,1)S(1)} %shard_map.63), channel_id=1, replica_groups=mesh['blk'=8,'rep'=4] {'blk'}, dimensions={0} | all-to-all | bytes 655360 | tf_op jit(solution)/shard_map/all_to_all | solution.py:525
  75.3 1.6 %collective-permute-done.8.other_ref = bf16[8,160,128]{2,1,0:T(8,128)(2,1)S(1)} collective-permute-done((bf16[8,160,128]{2,1,0:T(8,128)(2,1)S(1)}, bf16[8,160,128]{2,1,0:T(8,128)(2,1)S(1)}, u32[]{:S(2)}, u32[]{:S(2)}) %collective-permute-start.8) | collective-permute-done | bytes 327712 | tf_op jit(solution)/shard_map/ppermute | solution.py:531
  76.9 3.1 %shard_map.64 = (bf16[8,160,128]{2,1,0:T(8,128)(2,1)S(1)}, f32[64,2048]{1,0:T(8,128)S(1)}) custom-call(s32[4,8]{1,0:T(4,128)S(1)} %bitcast.21, s32[2]{0:T(128)S(1)} %pad_add_fusion.place_ref, bf16[2,8,128,128]{3,2,1,0:T(8,128)(2,1)S(1)} %pad_maximum_fusion.2.tiles_own, bf16[2,8,128,128]{3,2,1,0:T(8,128)(2,1)S(1)} %collective-permute-done.5.tiles_near, ...), custom_call_target="tpu_custom_call" | custom-call | tf_op jit(solution)/shard_map/pallas_call | solution.py:497
  80.0 14.0 %all_to_all.31.own_ref = bf16[8,160,128]{2,1,0:T(8,128)(2,1)S(1)} all-to-all(bf16[8,160,128]{2,1,0:T(8,128)(2,1)S(1)} %get-tuple-element.19), channel_id=1, replica_groups=mesh['blk'=8,'rep'=4] {'blk'}, dimensions={0} | all-to-all | bytes 655360 | tf_op jit(solution)/shard_map/all_to_all | solution.py:525
  95.7 2.3 %shard_map.66 = f32[8,32,128]{2,1,0:T(8,128)} custom-call(s32[8,4]{1,0:T(8,128)S(1)} %shard_map.61.slots_ref, s32[2]{0:T(128)S(1)} %pad_add_fusion.place_ref, bf16[2,32,40,128]{3,2,1,0:T(8,128)(2,1)S(1)} %pad_maximum_fusion.tiles_own, bf16[2,32,40,128]{3,2,1,0:T(8,128)(2,1)S(1)} %collective-permute-done.3.tiles_near, ...), custom_call_target="tpu_custom_call" | custom-call | tf_op jit(solution)/shard_map/pallas_call | solution.py:497
  98.0 3.4 %all-to-all-start.5 = ((f32[8,32,128]{2,1,0:T(8,128)}), f32[8,32,128]{2,1,0:T(8,128)S(1)}, u32[]{:S(2)}, u32[]{:S(2)}) async-start(f32[8,32,128]{2,1,0:T(8,128)} %shard_map.66), calls=%async_computation.5 | async-start | bytes 262144 | tf_op jit(solution)/shard_map/all_to_all | solution.py:525
  101.4 4.3 %shard_map.65 = (f32[64,2048]{1,0:T(8,128)}, bf16[128,2048]{1,0:T(8,128)(2,1)S(1)}, f32[64,64]{1,0:T(8,128)S(1)}) custom-call(s32[8,4]{1,0:T(8,128)S(1)} %copy.9.cols_ref, s32[8,4]{1,0:T(8,128)S(1)} %shard_map.61.slots_ref, s32[2]{0:T(128)S(1)} %pad_add_fusion.place_ref, bf16[2,32,40,128]{3,2,1,0:T(8,128)(2,1)S(1)} %pad_maximum_fusion.tiles_own, ...), custom_call_target="tpu_custom_call" | custom-call | tf_op jit(solution)/shard_map/pallas_call | solution.py:497
  105.7 3.3 %all-to-all-done.5.gram_ref = f32[8,32,128]{2,1,0:T(8,128)S(1)} async-done(((f32[8,32,128]{2,1,0:T(8,128)}), f32[8,32,128]{2,1,0:T(8,128)S(1)}, u32[]{:S(2)}, u32[]{:S(2)}) %all-to-all-start.5) | async-done | bytes 131104 | tf_op jit(solution)/shard_map/all_to_all | solution.py:525
  109.0 3.2 %shard_map.67 = f32[64,2048]{1,0:T(8,128)} custom-call(f32[8,32,128]{2,1,0:T(8,128)S(1)} %all-to-all-done.5.gram_ref, f32[64,64]{1,0:T(8,128)S(1)} %get-tuple-element.22.scale_ref, bf16[128,2048]{1,0:T(8,128)(2,1)S(1)} %get-tuple-element.23.parts_ref), custom_call_target="tpu_custom_call" | custom-call | tf_op jit(solution)/shard_map/pallas_call | solution.py:497
  (26 shorter events, 4.1 us)
Async XLA Ops:
  2.4 9.3 %collective-permute-start = (bf16[64,2048]{1,0:T(8,128)(2,1)S(1)}, bf16[64,2048]{1,0:T(8,128)(2,1)S(1)}, u32[]{:S(2)}, u32[]{:S(2)}) collective-permute-start(bf16[64,2048]{1,0:T(8,128)(2,1)S(1)} %get-tuple-element.14), channel_id=1, source_target_pairs={{0,2},{1,3},{2,0},{3,1},{4,6},{5,7},{6,4},{7,5},{8,10},{9,11},{10,... | collective-permute-start | bytes 786440 | tf_op jit(solution)/shard_map/ppermute | solution.py:528
  5.4 16.9 %all-to-all-start = ((bf16[32,40,128]{2,1,0:T(8,128)(2,1)}), bf16[32,40,128]{2,1,0:T(8,128)(2,1)S(1)}, u32[]{:S(2)}, u32[]{:S(2)}) async-start(bf16[32,40,128]{2,1,0:T(8,128)(2,1)} %get-tuple-element.13), calls=%async_computation | async-start | bytes 655360 | tf_op jit(solution)/shard_map/all_to_all | solution.py:551
  11.7 10.6 %copy-start = (bf16[1,8,128,128]{3,2,1,0:T(8,128)(2,1)S(1)}, bf16[1,8,128,128]{3,2,1,0:T(8,128)(2,1)}, u32[]{:S(2)}) copy-start(bf16[1,8,128,128]{3,2,1,0:T(8,128)(2,1)} %param.4) | copy-start | bytes 786436
  11.8 10.9 %collective-permute-start.1 = (bf16[2,64,2048]{2,1,0:T(8,128)(2,1)S(1)}, bf16[2,64,2048]{2,1,0:T(8,128)(2,1)S(1)}, u32[]{:S(2)}, u32[]{:S(2)}) collective-permute-start(bf16[2,64,2048]{2,1,0:T(8,128)(2,1)S(1)} %pad_maximum_fusion.1.own_ref), channel_id=1, source_target_pairs={{0,1},{1,0},{2,3},{3,2},{4,5},{5,4},{6,7},{7,6},{8,9},{9,8},{10,11... | collective-permute-start | bytes 1572872 | tf_op jit(solution)/shard_map/ppermute | solution.py:531
  22.3 7.8 %collective-permute-start.4 = (bf16[8,128,128]{2,1,0:T(8,128)(2,1)S(1)}, bf16[8,128,128]{2,1,0:T(8,128)(2,1)S(1)}, u32[]{:S(2)}, u32[]{:S(2)}) collective-permute-start(bf16[8,128,128]{2,1,0:T(8,128)(2,1)S(1)} %bitcast.23), channel_id=1, source_target_pairs={{0,2},{1,3},{2,0},{3,1},{4,6},{5,7},{6,4},{7,5},{8,10},{9,11},{10,... | collective-permute-start | bytes 786440 | tf_op jit(solution)/shard_map/ppermute | solution.py:528
  24.3 13.0 %all-to-all-start.1 = ((bf16[8,128,128]{2,1,0:T(8,128)(2,1)}), bf16[8,128,128]{2,1,0:T(8,128)(2,1)S(1)}, u32[]{:S(2)}, u32[]{:S(2)}) async-start(bf16[8,128,128]{2,1,0:T(8,128)(2,1)} %get-tuple-element.18), calls=%async_computation.1 | async-start | bytes 524288 | tf_op jit(solution)/shard_map/all_to_all | solution.py:525
  30.2 8.0 %collective-permute-start.5 = (bf16[2,8,128,128]{3,2,1,0:T(8,128)(2,1)S(1)}, bf16[2,8,128,128]{3,2,1,0:T(8,128)(2,1)S(1)}, u32[]{:S(2)}, u32[]{:S(2)}) collective-permute-start(bf16[2,8,128,128]{3,2,1,0:T(8,128)(2,1)S(1)} %pad_maximum_fusion.2.tiles_own), channel_id=1, source_target_pairs={{0,1},{1,0},{2,3},{3,2},{4,5},{5,4},{6,7},{7,6},{8,9},{9,8},{10,11... | collective-permute-start | bytes 1572872 | tf_op jit(solution)/shard_map/ppermute | solution.py:531
  37.3 1.5 %collective-permute-start.6 = (bf16[8,128,128]{2,1,0:T(8,128)(2,1)S(1)}, bf16[8,128,128]{2,1,0:T(8,128)(2,1)S(1)}, u32[]{:S(2)}, u32[]{:S(2)}) collective-permute-start(bf16[8,128,128]{2,1,0:T(8,128)(2,1)S(1)} %all-to-all-done.1.own_ref), channel_id=1, source_target_pairs={{0,1},{1,0},{2,3},{3,2},{4,5},{5,4},{6,7},{7,6},{8,9},{9,8},{10,11... | collective-permute-start | bytes 786440 | tf_op jit(solution)/shard_map/ppermute | solution.py:531
  37.3 10.1 %collective-permute-start.2 = (bf16[32,40,128]{2,1,0:T(8,128)(2,1)S(1)}, bf16[32,40,128]{2,1,0:T(8,128)(2,1)S(1)}, u32[]{:S(2)}, u32[]{:S(2)}) collective-permute-start(bf16[32,40,128]{2,1,0:T(8,128)(2,1)S(1)} %all-to-all-done.moved_ref), channel_id=1, source_target_pairs={{0,2},{1,3},{2,0},{3,1},{4,6},{5,7},{6,4},{7,5},{8,10},{9,11},{10,... | collective-permute-start | bytes 983048 | tf_op jit(solution)/shard_map/ppermute | solution.py:528
  41.6 14.2 %all-to-all-start.2 = ((bf16[8,160,128]{2,1,0:T(8,128)(2,1)}), bf16[8,160,128]{2,1,0:T(8,128)(2,1)S(1)}, u32[]{:S(2)}, u32[]{:S(2)}) async-start(bf16[8,160,128]{2,1,0:T(8,128)(2,1)} %shard_map.62), calls=%async_computation.2 | async-start | bytes 655360 | tf_op jit(solution)/shard_map/all_to_all | solution.py:525
  47.5 8.6 %collective-permute-start.3 = (bf16[2,32,40,128]{3,2,1,0:T(8,128)(2,1)S(1)}, bf16[2,32,40,128]{3,2,1,0:T(8,128)(2,1)S(1)}, u32[]{:S(2)}, u32[]{:S(2)}) collective-permute-start(bf16[2,32,40,128]{3,2,1,0:T(8,128)(2,1)S(1)} %pad_maximum_fusion.tiles_own), channel_id=1, source_target_pairs={{0,1},{1,0},{2,3},{3,2},{4,5},{5,4},{6,7},{7,6},{8,9},{9,8},{10,11... | collective-permute-start | bytes 1966088 | tf_op jit(solution)/shard_map/ppermute | solution.py:531
  55.9 1.6 %collective-permute-start.7 = (bf16[8,160,128]{2,1,0:T(8,128)(2,1)S(1)}, bf16[8,160,128]{2,1,0:T(8,128)(2,1)S(1)}, u32[]{:S(2)}, u32[]{:S(2)}) collective-permute-start(bf16[8,160,128]{2,1,0:T(8,128)(2,1)S(1)} %all-to-all-done.2.own_ref), channel_id=1, source_target_pairs={{0,1},{1,0},{2,3},{3,2},{4,5},{5,4},{6,7},{7,6},{8,9},{9,8},{10,11... | collective-permute-start | bytes 983048 | tf_op jit(solution)/shard_map/ppermute | solution.py:531
  75.3 1.6 %collective-permute-start.8 = (bf16[8,160,128]{2,1,0:T(8,128)(2,1)S(1)}, bf16[8,160,128]{2,1,0:T(8,128)(2,1)S(1)}, u32[]{:S(2)}, u32[]{:S(2)}) collective-permute-start(bf16[8,160,128]{2,1,0:T(8,128)(2,1)S(1)} %all_to_all.30.own_ref), channel_id=1, source_target_pairs={{0,1},{1,0},{2,3},{3,2},{4,5},{5,4},{6,7},{7,6},{8,9},{9,8},{10,11... | collective-permute-start | bytes 983048 | tf_op jit(solution)/shard_map/ppermute | solution.py:531
  94.0 1.6 %collective-permute-start.9 = (bf16[8,160,128]{2,1,0:T(8,128)(2,1)S(1)}, bf16[8,160,128]{2,1,0:T(8,128)(2,1)S(1)}, u32[]{:S(2)}, u32[]{:S(2)}) collective-permute-start(bf16[8,160,128]{2,1,0:T(8,128)(2,1)S(1)} %all_to_all.31.own_ref), channel_id=1, source_target_pairs={{0,1},{1,0},{2,3},{3,2},{4,5},{5,4},{6,7},{7,6},{8,9},{9,8},{10,11... | collective-permute-start | bytes 983048 | tf_op jit(solution)/shard_map/ppermute | solution.py:531
  98.0 11.0 %all-to-all-start.5 = ((f32[8,32,128]{2,1,0:T(8,128)}), f32[8,32,128]{2,1,0:T(8,128)S(1)}, u32[]{:S(2)}, u32[]{:S(2)}) async-start(f32[8,32,128]{2,1,0:T(8,128)} %shard_map.66), calls=%async_computation.5 | async-start | bytes 262144 | tf_op jit(solution)/shard_map/all_to_all | solution.py:525

commit v6 on v5

--- a/solution.py
+++ b/solution.py
@@ -121,7 +121,9 @@
         lax.fori_loop(0, count // step, several, 0)
 
 
-def beside(steps, tasks):
+def beside(steps, ready, tasks):
+    next(steps, None)
+    ready()
     if max(count for _, count in tasks) > 8:
         run(steps)
         for body, count in tasks:
@@ -130,9 +132,9 @@
     tasks = [functools.partial(body, i) for body, count in tasks for i in range(count)]
     panels = 8
     for n in range(panels):
-        next(steps, None)
         for task in tasks[len(tasks) * n // panels : len(tasks) * (n + 1) // panels]:
             task()
+        next(steps, None)
     run(steps)
 
 
@@ -160,7 +162,7 @@
 
 
 def pack_kernel(
-    rows_hbm, cols_hbm, tiles_hbm, start_hbm, out_hbm, start_out, rows_ref, cols_ref, tiles_ref, start_ref, out_ref, sems
+    rows_hbm, cols_hbm, tiles_hbm, start_hbm, out_ref, start_out, rows_ref, cols_ref, tiles_ref, start_ref, sems
 ):
     pairs = ((rows_hbm, rows_ref), (cols_hbm, cols_ref), (tiles_hbm, tiles_ref), (start_hbm, start_ref))
     copies = [pltpu.make_async_copy(source, to, sems.at[n]) for n, (source, to) in enumerate(pairs)]
@@ -181,15 +183,12 @@
         out_ref[i] = jnp.concatenate([tiles_ref[i], places], axis=0)
 
     each(count, pack, 32)
-    packed = pltpu.make_async_copy(out_ref, out_hbm, sems.at[4])
-    packed.start()
     copies[3].wait()
     start_out[...] = start_ref[...].astype(BF16)
-    packed.wait()
-
-
-def choose_kernel(place_ref, moved_ref, own_ref, near_ref, out_hbm, places_ref, out_ref, sems):
-    rep, block = place_ref[0], place_ref[1]
+
+
+def choose_kernel(moved_ref, own_ref, near_ref, out_hbm, places_ref, out_ref, sems):
+    rep, block = lax.axis_index("rep"), lax.axis_index("blk")
     core = lax.rem(rep, 2)
     blocks, _, tile = out_ref.shape
     width, share = own_ref.shape[1:]
@@ -234,11 +233,14 @@
     each(blocks, look)
 
 
-def left_kernel(first, last, rows_ref, place_ref, tiles_own, tiles_near, own_ref, other_ref, out_ref, *rest):
+def left_kernel(first, last, rows_vmem, tiles_own, tiles_near, own_ref, other_ref, out_ref, *rest):
     if last:
         raw_ref, *rest = rest
-    total, stacked, packed, work, spread, raw_gram, *sems = rest
-    core = lax.rem(place_ref[0], 2)
+    total, stacked, packed, work, spread, raw_gram, rows_ref, rows_sem, *rest = rest
+    rows = pltpu.make_async_copy(rows_vmem, rows_ref, rows_sem.at[0])
+    rows.start()
+    this = lax.axis_index("rep")
+    core = lax.rem(this, 2)
     pieces, _, tile = own_ref.shape
     width = total.shape[0]
     half = width // 2
@@ -247,23 +249,34 @@
     steps = eliminate(work, spread) if not first else iter(())
     total[...] = jnp.zeros_like(total)
 
+    early = first and pieces <= 8
+    if first:
+        sems, *rest = rest
+    if early:
+        (products,) = rest
     tasks = []
     for far in range(2):
         for source, stored, near in ((own_ref, tiles_own, 0), (other_ref, tiles_near, 1)):
-            rep = lax.bitwise_xor(place_ref[0], 2 * far + near)
-
-            def add(p, source=source, stored=stored, far=far, rep=rep):
+            rep = lax.bitwise_xor(this, 2 * far + near)
+
+            def multiply(p, source=source, stored=stored, far=far, rep=rep):
                 chosen = source[p, pl.ds(pl.multiple_of(lax.div(rep, 2) * width, width), width), :]
-                product = dot(chosen, stored[far, p], NT)
+                return dot(chosen, stored[far, p], NT)
+
+            def add(p, rep=rep, multiply=multiply, kept=2 * far + near):
+                product = products[kept, p] if early else multiply(p)
                 at = pl.multiple_of(rows_ref[rep, p] * tile, tile)
                 total[:, pl.ds(at, tile)] += product
 
             tasks.append((add, pieces))
+            if early:
+                for p in range(pieces):
+                    products[2 * far + near, p] = multiply(p)
     chunk = 4 * tile
     if not first:
         raw_gram[...] = jnp.zeros_like(raw_gram)
         tasks.append((add_gram(total, raw_gram, chunk), total.shape[1] // chunk))
-    beside(steps, tasks)
+    beside(steps, rows.wait, tasks)
     mine = pl.ds(pl.multiple_of(core * half, half), half)
     if first:
         stacked[...] = jnp.concatenate(two_parts(total[...]), axis=0)
@@ -275,14 +288,14 @@
                     pltpu.make_async_copy(
                         stacked.at[pl.ds(0, width), pl.ds(at, tile)],
                         out_ref.at[p, pl.ds(x * width, width), :],
-                        sems[0].at[p, x],
+                        sems.at[p, x],
                     )
                 )
                 copies[-1].start()
         pack_gram(gram_of_parts(stacked[...]), packed)
         for p in range(pieces):
             copies.append(
-                pltpu.make_async_copy(packed.at[mine, :], out_ref.at[p, pl.ds(2 * width, half), :], sems[0].at[p, 2])
+                pltpu.make_async_copy(packed.at[mine, :], out_ref.at[p, pl.ds(2 * width, half), :], sems.at[p, 2])
             )
             copies[-1].start()
         for copy in copies:
@@ -321,15 +334,15 @@
     find_slots(cols_ref, slots_ref, first_at)
 
 
-def place_quarters(place_ref, tiles_own, tiles_near, quarters):
+def place_quarters(tiles_own, tiles_near, quarters):
     quarter = quarters.shape[2]
     for far in range(2):
         for near, source in enumerate((tiles_own, tiles_near)):
-            quarters[lax.bitwise_xor(place_ref[0], 2 * far + near)] = source[far, :, 0:quarter, :]
-
-
-def right_tasks(place_ref, slots_ref, quarters, own_ref, other_ref, total, raw_gram):
-    core = lax.rem(place_ref[0], 2)
+            quarters[lax.bitwise_xor(lax.axis_index("rep"), 2 * far + near)] = source[far, :, 0:quarter, :]
+
+
+def right_tasks(slots_ref, quarters, own_ref, other_ref, total, raw_gram):
+    core = lax.rem(lax.axis_index("rep"), 2)
     blocks, _, tile = own_ref.shape
     width = total.shape[0]
     total[...] = jnp.zeros_like(total)
@@ -351,8 +364,7 @@
 
 
 def right_kernel(
-    cols_ref,
-    place_ref,
+    cols_vmem,
     tiles_own,
     tiles_near,
     own_ref,
@@ -365,19 +377,26 @@
     spread,
     raw_gram,
     quarters,
+    cols_ref,
+    cols_sem,
     slots_ref,
     first_at,
 ):
-    find_slots(cols_ref, slots_ref, first_at)
-    core = lax.rem(place_ref[0], 2)
+    cols = pltpu.make_async_copy(cols_vmem, cols_ref, cols_sem.at[0])
+    cols.start()
+    core = lax.rem(lax.axis_index("rep"), 2)
     blocks, _, tile = own_ref.shape
     width = total.shape[0]
     half = width // 2
-    place_quarters(place_ref, tiles_own, tiles_near, quarters)
+    place_quarters(tiles_own, tiles_near, quarters)
     gather_gram(work, own_ref, other_ref, core)
-    beside(
-        eliminate(work, spread), right_tasks(place_ref, slots_ref, quarters, own_ref, other_ref, total, raw_gram)
-    )
+
+    def ready():
+        cols.wait()
+        find_slots(cols_ref, slots_ref, first_at)
+
+    tasks = right_tasks(slots_ref, quarters, own_ref, other_ref, total, raw_gram)
+    beside(eliminate(work, spread), ready, tasks)
     scale = work[:, 0:width]
     pack_gram(scaled_gram(scale, raw_gram), packed)
     scale_parts = two_parts(scale)
@@ -400,10 +419,13 @@
 
 
 def last_right_kernel(
-    slots_ref, place_ref, tiles_own, tiles_near, own_ref, other_ref, gram_hbm, total, raw_gram, quarters, sems
+    slots_vmem, tiles_own, tiles_near, own_ref, other_ref, gram_hbm, total, raw_gram, quarters, slots_ref, sems
 ):
-    place_quarters(place_ref, tiles_own, tiles_near, quarters)
-    beside(iter(()), right_tasks(place_ref, slots_ref, quarters, own_ref, other_ref, total, raw_gram))
+    slots = pltpu.make_async_copy(slots_vmem, slots_ref, sems.at[gram_hbm.shape[0]])
+    slots.start()
+    place_quarters(tiles_own, tiles_near, quarters)
+    tasks = right_tasks(slots_ref, quarters, own_ref, other_ref, total, raw_gram)
+    beside(iter(()), slots.wait, tasks)
     width = total.shape[0]
     half = width // 2
     lane = lax.broadcasted_iota(jnp.int32, (half, 2 * width), 1)
@@ -423,7 +445,6 @@
     right_factor,
     cols_ref,
     slots_ref,
-    place_ref,
     tiles_own,
     tiles_near,
     own_ref,
@@ -439,10 +460,10 @@
     raw_gram,
     quarters,
 ):
-    place_quarters(place_ref, tiles_own, tiles_near, quarters)
-    gather_gram(work, own_ref, other_ref, lax.rem(place_ref[0], 2))
-    products = right_tasks(place_ref, slots_ref, quarters, own_ref, other_ref, total_ref, raw_gram)[:-1]
-    beside(eliminate(work, spread), products)
+    place_quarters(tiles_own, tiles_near, quarters)
+    gather_gram(work, own_ref, other_ref, lax.rem(lax.axis_index("rep"), 2))
+    products = right_tasks(slots_ref, quarters, own_ref, other_ref, total_ref, raw_gram)[:-1]
+    beside(eliminate(work, spread), lambda: None, products)
     scale_ref[...] = work[:, 0 : scale_ref.shape[1]]
     left_out[...] = exact_dot(scale_ref[...] * left_factor, left_ref[...])
     width, tile = share.shape[0], total_ref.shape[1] // (slots_ref.shape[0] * 4)
@@ -453,7 +474,7 @@
         for rep in range(4):
             col = cols_ref[b, rep]
 
-            @pl.when(lax.div(col, shares) == place_ref[0])
+            @pl.when(lax.div(col, shares) == lax.axis_index("rep"))
             def _():
                 to = pl.multiple_of(lax.rem(col, shares) * tile, tile)
                 at = pl.multiple_of(slots_ref[b, rep] * tile, tile)
@@ -508,7 +529,6 @@
     blocks = lax.axis_size("blk")
     group = lax.axis_size("rep")
     block = lax.axis_index("blk")
-    rep = lax.axis_index("rep").astype(jnp.int32)
     tile = tiles.shape[-1]
     share, width = start_right.shape
     flat_tiles = tiles.reshape(-1, tile, tile)
@@ -517,7 +537,6 @@
     total_rows = ROW_TILES * tile * blocks
     total_cols = share * group * blocks
     count = blocks * group
-    place = jnp.stack([rep, block.astype(jnp.int32)])
     packed_rows = 2 * width + width // 2
     shape = jax.ShapeDtypeStruct
 
@@ -541,10 +560,8 @@
             pltpu.SMEM(tile_cols.shape, jnp.int32),
             pltpu.VMEM((count, quarter, tile), BF16),
             pltpu.VMEM((width, share), F32),
-            pltpu.VMEM((count, quarter + 8, tile), BF16),
-            pltpu.SemaphoreType.DMA((5,)),
+            pltpu.SemaphoreType.DMA((4,)),
         ],
-        [HBM, VMEM],
     )
     start_own = jnp.stack([start, swap_x(start)])
     start_near = swap_core(start_own)
@@ -552,7 +569,7 @@
     chosen, places = call(
         choose_kernel,
         [shape((blocks, 2 * width, tile), BF16), shape((count, 8, tile), jnp.int32)],
-        [place],
+        [],
         [],
         [moved, start_own, start_near],
         [pltpu.VMEM((blocks, 2 * width, tile), BF16), pltpu.SemaphoreType.DMA((blocks,))],
@@ -580,9 +597,9 @@
         results = call(
             functools.partial(left_kernel, first, last),
             outs,
-            [rows_all, place],
             [],
-            [tiles_own, tiles_near, chosen, swap_core(chosen)],
+            [],
+            [rows_all, tiles_own, tiles_near, chosen, swap_core(chosen)],
             [
                 pltpu.VMEM((width, ROW_TILES * tile), F32),
                 pltpu.VMEM((2 * width if first else width, ROW_TILES * tile), BF16),
@@ -590,8 +607,11 @@
                 work,
                 spread,
                 pltpu.VMEM((width, 2 * width), F32),
+                pltpu.SMEM(rows_all.shape, jnp.int32),
+                pltpu.SemaphoreType.DMA((1,)),
             ]
-            + ([pltpu.SemaphoreType.DMA((blocks, 3))] if first else []),
+            + ([pltpu.SemaphoreType.DMA((blocks, 3))] if first else [])
+            + ([pltpu.VMEM((group, blocks, width, tile), F32)] if first and blocks <= 8 else []),
             [HBM] if first else None,
         )
         picked = across(results[0])
@@ -605,10 +625,11 @@
         (chosen,) = call(
             right_kernel,
             [shape((blocks, packed_rows, tile), BF16)],
-            [cols_here, place],
             [],
-            [columns_own, columns_near, picked, other],
+            [],
+            [cols_here, columns_own, columns_near, picked, other],
             [total, pltpu.VMEM((width, count * tile), BF16), packed, work, spread, gram_scratch, quarters]
+            + [pltpu.SMEM(cols_here.shape, jnp.int32), pltpu.SemaphoreType.DMA((1,))]
             + slot_scratch,
         )
     (slots,) = call(
@@ -623,16 +644,16 @@
     (gram,) = call(
         last_right_kernel,
         [shape((blocks, width // 2, 2 * width), F32)],
-        [slots, place],
-        [],
-        [columns_own, columns_near, picked, other],
-        [total, gram_scratch, quarters, pltpu.SemaphoreType.DMA((blocks,))],
+        [],
+        [],
+        [slots, columns_own, columns_near, picked, other],
+        [total, gram_scratch, quarters, pltpu.SMEM(slots.shape, jnp.int32), pltpu.SemaphoreType.DMA((blocks + 1,))],
         [HBM],
     )
     left, parts, left_scale = call(
         functools.partial(between_kernel, math.sqrt(total_rows), math.sqrt(total_cols)),
         [shape(left_raw.shape, F32), shape((2 * width, share), BF16), shape((width, width), F32)],
-        [cols_here, slots, place],
+        [cols_here, slots],
         [],
         [columns_own, columns_near, picked, other, left_raw],
         [pltpu.VMEM((width, share), F32), work, spread, total, gram_scratch, quarters],

time: 113 us -> 111 us (0.982)
  Pallas kernels: 23.6 us -> 22.1 us
    pallas_call x9, Pallas kernels: 23.6 us -> 22.1 us  [call(): pl.pallas_call(kernel, out_shape=outs, in_specs=[SMEM] * len(smem) + [HBM...]
  transfers between devices with their start and end apart: 14 -> 14, of which waited for: 11 -> 11; matrix products, arithmetic and copies ran while one was open for 0% -> 0% of each run, Pallas kernels for 9% -> 8%
where the time goes in v6:
time: 111 us
  waiting for transfers between devices  38.9 us (35%)
  blocking collectives  28.6 us (26%)
  Pallas kernels  22.1 us (20%)
  starting transfers between devices  19.8 us (18%)
    all_to_all x2, blocking collectives, across(): return lax.all_to_all(value, 'blk', split_axis=0, concat_axis=0, tiled=True)  28.6 us
    pallas_call x9, Pallas kernels, call(): pl.pallas_call(kernel, out_shape=outs, in_specs=[SMEM] * len(smem) + [HBM...  22.1 us
    all_to_all x3, waiting for transfers between devices, across(): return lax.all_to_all(value, 'blk', split_axis=0, concat_axis=0, tiled=True)  17.7 us
    all_to_all x3, starting transfers between devices, across(): return lax.all_to_all(value, 'blk', split_axis=0, concat_axis=0, tiled=True)  10.6 us
    all_to_all x1, waiting for transfers between devices, local(): lax.all_to_all(moved, ('blk', 'rep'), split_axis=0, concat_axis=0, tiled=...  10.5 us
    ppermute x3, waiting for transfers between devices, swap_x(): return lax.ppermute(value, 'rep', [(i, i ^ 2) for i in range(group)])  6.69 us
    all_to_all x1, starting transfers between devices, local(): lax.all_to_all(moved, ('blk', 'rep'), split_axis=0, concat_axis=0, tiled=...  4.92 us
    ppermute x3, starting transfers between devices, swap_x(): return lax.ppermute(value, 'rep', [(i, i ^ 2) for i in range(group)])  4.05 us
  transfers between devices with their start and end apart: 14, of which 11 were waited for; matrix products, arithmetic and copies ran while one was open for 0% of the time, Pallas kernels for 8%

profile of v6, /device:TPU:0, one launch (start us, length us, event | category | flops | bytes accessed | tf_op | source)
XLA Modules:
  0.0 110.6 jit_solution(15428343504707932649)
XLA Ops:
  0.6 1.9 %shard_map.59 = (bf16[32,40,128]{2,1,0:T(8,128)(2,1)}, bf16[64,2048]{1,0:T(8,128)(2,1)S(1)}) custom-call(s32[1,8]{1,0:T(1,128)} %rows_hbm.1, s32[1,8]{1,0:T(1,128)} %cols_hbm.1, bf16[32,32,128]{2,1,0:T(8,128)(2,1)} %bitcast.20, f32[64,2048]{1,0:T(8,128)} %bitcast.23), custom_call_target="tpu_custom_call" | custom-call | tf_op jit(solution)/shard_map/pallas_call | solution.py:518
  2.5 3.0 %collective-permute-start = (bf16[64,2048]{1,0:T(8,128)(2,1)S(1)}, bf16[64,2048]{1,0:T(8,128)(2,1)S(1)}, u32[]{:S(2)}, u32[]{:S(2)}) collective-permute-start(bf16[64,2048]{1,0:T(8,128)(2,1)S(1)} %get-tuple-element.14), channel_id=1, source_target_pairs={{0,2},{1,3},{2,0},{3,1},{4,6},{5,7},{6,4},{7,5},{8,10},{9,11},{10,... | collective-permute-start | bytes 786440 | tf_op jit(solution)/shard_map/ppermute | solution.py:547
  5.5 4.9 %all-to-all-start = ((bf16[32,40,128]{2,1,0:T(8,128)(2,1)}), bf16[32,40,128]{2,1,0:T(8,128)(2,1)S(1)}, u32[]{:S(2)}, u32[]{:S(2)}) async-start(bf16[32,40,128]{2,1,0:T(8,128)(2,1)} %get-tuple-element.13), calls=%async_computation | async-start | bytes 655360 | tf_op jit(solution)/shard_map/all_to_all | solution.py:568
  10.5 1.4 %collective-permute-done = bf16[64,2048]{1,0:T(8,128)(2,1)S(1)} collective-permute-done((bf16[64,2048]{1,0:T(8,128)(2,1)S(1)}, bf16[64,2048]{1,0:T(8,128)(2,1)S(1)}, u32[]{:S(2)}, u32[]{:S(2)}) %collective-permute-start) | collective-permute-done | bytes 262176 | tf_op jit(solution)/shard_map/ppermute | solution.py:547
  12.0 10.5 %all-to-all-done.moved_ref = bf16[32,40,128]{2,1,0:T(8,128)(2,1)S(1)} async-done(((bf16[32,40,128]{2,1,0:T(8,128)(2,1)}), bf16[32,40,128]{2,1,0:T(8,128)(2,1)S(1)}, u32[]{:S(2)}, u32[]{:S(2)}) %all-to-all-start) | async-done | bytes 327712 | tf_op jit(solution)/shard_map/all_to_all | solution.py:568
  23.9 3.6 %all-to-all-start.1 = ((bf16[8,128,128]{2,1,0:T(8,128)(2,1)}), bf16[8,128,128]{2,1,0:T(8,128)(2,1)S(1)}, u32[]{:S(2)}, u32[]{:S(2)}) async-start(bf16[8,128,128]{2,1,0:T(8,128)(2,1)} %get-tuple-element.18), calls=%async_computation.1 | async-start | bytes 524288 | tf_op jit(solution)/shard_map/all_to_all | solution.py:544
  27.5 2.7 %collective-permute-done.4 = bf16[8,128,128]{2,1,0:T(8,128)(2,1)S(1)} collective-permute-done((bf16[8,128,128]{2,1,0:T(8,128)(2,1)S(1)}, bf16[8,128,128]{2,1,0:T(8,128)(2,1)S(1)}, u32[]{:S(2)}, u32[]{:S(2)}) %collective-permute-start.4) | collective-permute-done | bytes 262176 | tf_op jit(solution)/shard_map/ppermute | solution.py:547
  30.3 6.5 %all-to-all-done.1.own_ref = bf16[8,128,128]{2,1,0:T(8,128)(2,1)S(1)} async-done(((bf16[8,128,128]{2,1,0:T(8,128)(2,1)}), bf16[8,128,128]{2,1,0:T(8,128)(2,1)S(1)}, u32[]{:S(2)}, u32[]{:S(2)}) %all-to-all-start.1) | async-done | bytes 262176 | tf_op jit(solution)/shard_map/all_to_all | solution.py:544
  38.4 2.4 %shard_map.62 = bf16[8,160,128]{2,1,0:T(8,128)(2,1)} custom-call(s32[4,8]{1,0:T(4,128)S(1)} %bitcast.18, bf16[2,8,128,128]{3,2,1,0:T(8,128)(2,1)S(1)} %pad_maximum_fusion.2.tiles_own, bf16[2,8,128,128]{3,2,1,0:T(8,128)(2,1)S(1)} %collective-permute-done.5.tiles_near, bf16[8,128,128]{2,1,0:T(8,128)(2,1)S(1)} %all-to-all-done.1.own_ref, ...), custom_call_target="tpu_custom_call" | custom-call | tf_op jit(solution)/shard_map/pallas_call | solution.py:518
  40.8 3.6 %all-to-all-start.2 = ((bf16[8,160,128]{2,1,0:T(8,128)(2,1)}), bf16[8,160,128]{2,1,0:T(8,128)(2,1)S(1)}, u32[]{:S(2)}, u32[]{:S(2)}) async-start(bf16[8,160,128]{2,1,0:T(8,128)(2,1)} %shard_map.62), calls=%async_computation.2 | async-start | bytes 655360 | tf_op jit(solution)/shard_map/all_to_all | solution.py:544
  44.4 2.6 %collective-permute-done.2 = bf16[32,40,128]{2,1,0:T(8,128)(2,1)S(1)} collective-permute-done((bf16[32,40,128]{2,1,0:T(8,128)(2,1)S(1)}, bf16[32,40,128]{2,1,0:T(8,128)(2,1)S(1)}, u32[]{:S(2)}, u32[]{:S(2)}) %collective-permute-start.2) | collective-permute-done | bytes 327712 | tf_op jit(solution)/shard_map/ppermute | solution.py:547
  47.1 7.9 %all-to-all-done.2.own_ref = bf16[8,160,128]{2,1,0:T(8,128)(2,1)S(1)} async-done(((bf16[8,160,128]{2,1,0:T(8,128)(2,1)}), bf16[8,160,128]{2,1,0:T(8,128)(2,1)S(1)}, u32[]{:S(2)}, u32[]{:S(2)}) %all-to-all-start.2) | async-done | bytes 327712 | tf_op jit(solution)/shard_map/all_to_all | solution.py:544
  55.3 1.4 %collective-permute-done.7.other_ref = bf16[8,160,128]{2,1,0:T(8,128)(2,1)S(1)} collective-permute-done((bf16[8,160,128]{2,1,0:T(8,128)(2,1)S(1)}, bf16[8,160,128]{2,1,0:T(8,128)(2,1)S(1)}, u32[]{:S(2)}, u32[]{:S(2)}) %collective-permute-start.7) | collective-permute-done | bytes 327712 | tf_op jit(solution)/shard_map/ppermute | solution.py:550
  56.7 2.9 %shard_map.63 = bf16[8,160,128]{2,1,0:T(8,128)(2,1)S(1)} custom-call(s32[8,4]{1,0:T(8,128)S(1)} %copy.9.cols_ref.cols_vmem, bf16[2,32,40,128]{3,2,1,0:T(8,128)(2,1)S(1)} %pad_maximum_fusion.tiles_own, bf16[2,32,40,128]{3,2,1,0:T(8,128)(2,1)S(1)} %collective-permute-done.3.tiles_near, bf16[8,160,128]{2,1,0:T(8,128)(2,1)S(1)} %all-to-all-done.2.own_ref, ...), custom_call_target="tpu_custom_call" | custom-call | tf_op jit(solution)/shard_map/pallas_call | solution.py:518
  59.6 14.6 %all_to_all.30.own_ref = bf16[8,160,128]{2,1,0:T(8,128)(2,1)S(1)} all-to-all(bf16[8,160,128]{2,1,0:T(8,128)(2,1)S(1)} %shard_map.63), channel_id=1, replica_groups=mesh['blk'=8,'rep'=4] {'blk'}, dimensions={0} | all-to-all | bytes 655360 | tf_op jit(solution)/shard_map/all_to_all | solution.py:544
  74.2 1.6 %collective-permute-done.8.other_ref = bf16[8,160,128]{2,1,0:T(8,128)(2,1)S(1)} collective-permute-done((bf16[8,160,128]{2,1,0:T(8,128)(2,1)S(1)}, bf16[8,160,128]{2,1,0:T(8,128)(2,1)S(1)}, u32[]{:S(2)}, u32[]{:S(2)}) %collective-permute-start.8) | collective-permute-done | bytes 327712 | tf_op jit(solution)/shard_map/ppermute | solution.py:550
  75.9 2.7 %shard_map.64 = (bf16[8,160,128]{2,1,0:T(8,128)(2,1)S(1)}, f32[64,2048]{1,0:T(8,128)S(1)}) custom-call(s32[4,8]{1,0:T(4,128)S(1)} %bitcast.19, bf16[2,8,128,128]{3,2,1,0:T(8,128)(2,1)S(1)} %pad_maximum_fusion.2.tiles_own, bf16[2,8,128,128]{3,2,1,0:T(8,128)(2,1)S(1)} %collective-permute-done.5.tiles_near, bf16[8,160,128]{2,1,0:T(8,128)(2,1)S(1)} %all_to_all.30.own_ref, ...), custom_call_target="tpu_custom_call" | custom-call | tf_op jit(solution)/shard_map/pallas_call | solution.py:518
  78.6 14.0 %all_to_all.31.own_ref = bf16[8,160,128]{2,1,0:T(8,128)(2,1)S(1)} all-to-all(bf16[8,160,128]{2,1,0:T(8,128)(2,1)S(1)} %get-tuple-element.19), channel_id=1, replica_groups=mesh['blk'=8,'rep'=4] {'blk'}, dimensions={0} | all-to-all | bytes 655360 | tf_op jit(solution)/shard_map/all_to_all | solution.py:544
  92.6 1.3 %shard_map.61.slots_ref.slots_vmem = s32[8,4]{1,0:T(8,128)S(1)} custom-call(s32[8,4]{1,0:T(8,128)S(1)} %copy.9.cols_ref.cols_vmem), custom_call_target="tpu_custom_call" | custom-call | tf_op jit(solution)/shard_map/pallas_call | solution.py:518
  94.2 2.3 %shard_map.66 = f32[8,32,128]{2,1,0:T(8,128)} custom-call(s32[8,4]{1,0:T(8,128)S(1)} %shard_map.61.slots_ref.slots_vmem, bf16[2,32,40,128]{3,2,1,0:T(8,128)(2,1)S(1)} %pad_maximum_fusion.tiles_own, bf16[2,32,40,128]{3,2,1,0:T(8,128)(2,1)S(1)} %collective-permute-done.3.tiles_near, bf16[8,160,128]{2,1,0:T(8,128)(2,1)S(1)} %all_to_all.31.own_ref, ...), custom_call_target="tpu_custom_call" | custom-call | tf_op jit(solution)/shard_map/pallas_call | solution.py:518
  96.5 3.4 %all-to-all-start.5 = ((f32[8,32,128]{2,1,0:T(8,128)}), f32[8,32,128]{2,1,0:T(8,128)S(1)}, u32[]{:S(2)}, u32[]{:S(2)}) async-start(f32[8,32,128]{2,1,0:T(8,128)} %shard_map.66), calls=%async_computation.5 | async-start | bytes 262144 | tf_op jit(solution)/shard_map/all_to_all | solution.py:544
  99.9 4.3 %shard_map.65 = (f32[64,2048]{1,0:T(8,128)}, bf16[128,2048]{1,0:T(8,128)(2,1)S(1)}, f32[64,64]{1,0:T(8,128)S(1)}) custom-call(s32[8,4]{1,0:T(8,128)S(1)} %copy.9.cols_ref.cols_vmem, s32[8,4]{1,0:T(8,128)S(1)} %shard_map.61.slots_ref.slots_vmem, bf16[2,32,40,128]{3,2,1,0:T(8,128)(2,1)S(1)} %pad_maximum_fusion.tiles_own, ...), custom_call_target="tpu_custom_call" | custom-call | tf_op jit(solution)/shard_map/pallas_call | solution.py:518
  104.2 3.3 %all-to-all-done.5.gram_ref = f32[8,32,128]{2,1,0:T(8,128)S(1)} async-done(((f32[8,32,128]{2,1,0:T(8,128)}), f32[8,32,128]{2,1,0:T(8,128)S(1)}, u32[]{:S(2)}, u32[]{:S(2)}) %all-to-all-start.5) | async-done | bytes 131104 | tf_op jit(solution)/shard_map/all_to_all | solution.py:544
  107.5 3.2 %shard_map.67 = f32[64,2048]{1,0:T(8,128)} custom-call(f32[8,32,128]{2,1,0:T(8,128)S(1)} %all-to-all-done.5.gram_ref, f32[64,64]{1,0:T(8,128)S(1)} %get-tuple-element.22.scale_ref, bf16[128,2048]{1,0:T(8,128)(2,1)S(1)} %get-tuple-element.23.parts_ref), custom_call_target="tpu_custom_call" | custom-call | tf_op jit(solution)/shard_map/pallas_call | solution.py:518
  (25 shorter events, 3.9 us)
Async XLA Ops:
  2.5 9.3 %collective-permute-start = (bf16[64,2048]{1,0:T(8,128)(2,1)S(1)}, bf16[64,2048]{1,0:T(8,128)(2,1)S(1)}, u32[]{:S(2)}, u32[]{:S(2)}) collective-permute-start(bf16[64,2048]{1,0:T(8,128)(2,1)S(1)} %get-tuple-element.14), channel_id=1, source_target_pairs={{0,2},{1,3},{2,0},{3,1},{4,6},{5,7},{6,4},{7,5},{8,10},{9,11},{10,... | collective-permute-start | bytes 786440 | tf_op jit(solution)/shard_map/ppermute | solution.py:547
  5.5 16.9 %all-to-all-start = ((bf16[32,40,128]{2,1,0:T(8,128)(2,1)}), bf16[32,40,128]{2,1,0:T(8,128)(2,1)S(1)}, u32[]{:S(2)}, u32[]{:S(2)}) async-start(bf16[32,40,128]{2,1,0:T(8,128)(2,1)} %get-tuple-element.13), calls=%async_computation | async-start | bytes 655360 | tf_op jit(solution)/shard_map/all_to_all | solution.py:568
  11.8 10.6 %copy-start = (bf16[1,8,128,128]{3,2,1,0:T(8,128)(2,1)S(1)}, bf16[1,8,128,128]{3,2,1,0:T(8,128)(2,1)}, u32[]{:S(2)}) copy-start(bf16[1,8,128,128]{3,2,1,0:T(8,128)(2,1)} %param.4) | copy-start | bytes 786436
  11.9 10.8 %collective-permute-start.1 = (bf16[2,64,2048]{2,1,0:T(8,128)(2,1)S(1)}, bf16[2,64,2048]{2,1,0:T(8,128)(2,1)S(1)}, u32[]{:S(2)}, u32[]{:S(2)}) collective-permute-start(bf16[2,64,2048]{2,1,0:T(8,128)(2,1)S(1)} %pad_maximum_fusion.1.own_ref), channel_id=1, source_target_pairs={{0,1},{1,0},{2,3},{3,2},{4,5},{5,4},{6,7},{7,6},{8,9},{9,8},{10,11... | collective-permute-start | bytes 1572872 | tf_op jit(solution)/shard_map/ppermute | solution.py:550
  22.5 7.8 %collective-permute-start.4 = (bf16[8,128,128]{2,1,0:T(8,128)(2,1)S(1)}, bf16[8,128,128]{2,1,0:T(8,128)(2,1)S(1)}, u32[]{:S(2)}, u32[]{:S(2)}) collective-permute-start(bf16[8,128,128]{2,1,0:T(8,128)(2,1)S(1)} %bitcast.21), channel_id=1, source_target_pairs={{0,2},{1,3},{2,0},{3,1},{4,6},{5,7},{6,4},{7,5},{8,10},{9,11},{10,... | collective-permute-start | bytes 786440 | tf_op jit(solution)/shard_map/ppermute | solution.py:547
  23.9 13.0 %all-to-all-start.1 = ((bf16[8,128,128]{2,1,0:T(8,128)(2,1)}), bf16[8,128,128]{2,1,0:T(8,128)(2,1)S(1)}, u32[]{:S(2)}, u32[]{:S(2)}) async-start(bf16[8,128,128]{2,1,0:T(8,128)(2,1)} %get-tuple-element.18), calls=%async_computation.1 | async-start | bytes 524288 | tf_op jit(solution)/shard_map/all_to_all | solution.py:544
  30.3 7.4 %collective-permute-start.5 = (bf16[2,8,128,128]{3,2,1,0:T(8,128)(2,1)S(1)}, bf16[2,8,128,128]{3,2,1,0:T(8,128)(2,1)S(1)}, u32[]{:S(2)}, u32[]{:S(2)}) collective-permute-start(bf16[2,8,128,128]{3,2,1,0:T(8,128)(2,1)S(1)} %pad_maximum_fusion.2.tiles_own), channel_id=1, source_target_pairs={{0,1},{1,0},{2,3},{3,2},{4,5},{5,4},{6,7},{7,6},{8,9},{9,8},{10,11... | collective-permute-start | bytes 1572872 | tf_op jit(solution)/shard_map/ppermute | solution.py:550
  36.8 1.5 %collective-permute-start.6 = (bf16[8,128,128]{2,1,0:T(8,128)(2,1)S(1)}, bf16[8,128,128]{2,1,0:T(8,128)(2,1)S(1)}, u32[]{:S(2)}, u32[]{:S(2)}) collective-permute-start(bf16[8,128,128]{2,1,0:T(8,128)(2,1)S(1)} %all-to-all-done.1.own_ref), channel_id=1, source_target_pairs={{0,1},{1,0},{2,3},{3,2},{4,5},{5,4},{6,7},{7,6},{8,9},{9,8},{10,11... | collective-permute-start | bytes 786440 | tf_op jit(solution)/shard_map/ppermute | solution.py:550
  36.8 10.1 %collective-permute-start.2 = (bf16[32,40,128]{2,1,0:T(8,128)(2,1)S(1)}, bf16[32,40,128]{2,1,0:T(8,128)(2,1)S(1)}, u32[]{:S(2)}, u32[]{:S(2)}) collective-permute-start(bf16[32,40,128]{2,1,0:T(8,128)(2,1)S(1)} %all-to-all-done.moved_ref), channel_id=1, source_target_pairs={{0,2},{1,3},{2,0},{3,1},{4,6},{5,7},{6,4},{7,5},{8,10},{9,11},{10,... | collective-permute-start | bytes 983048 | tf_op jit(solution)/shard_map/ppermute | solution.py:547
  40.8 14.2 %all-to-all-start.2 = ((bf16[8,160,128]{2,1,0:T(8,128)(2,1)}), bf16[8,160,128]{2,1,0:T(8,128)(2,1)S(1)}, u32[]{:S(2)}, u32[]{:S(2)}) async-start(bf16[8,160,128]{2,1,0:T(8,128)(2,1)} %shard_map.62), calls=%async_computation.2 | async-start | bytes 655360 | tf_op jit(solution)/shard_map/all_to_all | solution.py:544
  47.0 8.3 %collective-permute-start.3 = (bf16[2,32,40,128]{3,2,1,0:T(8,128)(2,1)S(1)}, bf16[2,32,40,128]{3,2,1,0:T(8,128)(2,1)S(1)}, u32[]{:S(2)}, u32[]{:S(2)}) collective-permute-start(bf16[2,32,40,128]{3,2,1,0:T(8,128)(2,1)S(1)} %pad_maximum_fusion.tiles_own), channel_id=1, source_target_pairs={{0,1},{1,0},{2,3},{3,2},{4,5},{5,4},{6,7},{7,6},{8,9},{9,8},{10,11... | collective-permute-start | bytes 1966088 | tf_op jit(solution)/shard_map/ppermute | solution.py:550
  55.0 1.6 %collective-permute-start.7 = (bf16[8,160,128]{2,1,0:T(8,128)(2,1)S(1)}, bf16[8,160,128]{2,1,0:T(8,128)(2,1)S(1)}, u32[]{:S(2)}, u32[]{:S(2)}) collective-permute-start(bf16[8,160,128]{2,1,0:T(8,128)(2,1)S(1)} %all-to-all-done.2.own_ref), channel_id=1, source_target_pairs={{0,1},{1,0},{2,3},{3,2},{4,5},{5,4},{6,7},{7,6},{8,9},{9,8},{10,11... | collective-permute-start | bytes 983048 | tf_op jit(solution)/shard_map/ppermute | solution.py:550
  74.2 1.6 %collective-permute-start.8 = (bf16[8,160,128]{2,1,0:T(8,128)(2,1)S(1)}, bf16[8,160,128]{2,1,0:T(8,128)(2,1)S(1)}, u32[]{:S(2)}, u32[]{:S(2)}) collective-permute-start(bf16[8,160,128]{2,1,0:T(8,128)(2,1)S(1)} %all_to_all.30.own_ref), channel_id=1, source_target_pairs={{0,1},{1,0},{2,3},{3,2},{4,5},{5,4},{6,7},{7,6},{8,9},{9,8},{10,11... | collective-permute-start | bytes 983048 | tf_op jit(solution)/shard_map/ppermute | solution.py:550
  92.6 1.6 %collective-permute-start.9 = (bf16[8,160,128]{2,1,0:T(8,128)(2,1)S(1)}, bf16[8,160,128]{2,1,0:T(8,128)(2,1)S(1)}, u32[]{:S(2)}, u32[]{:S(2)}) collective-permute-start(bf16[8,160,128]{2,1,0:T(8,128)(2,1)S(1)} %all_to_all.31.own_ref), channel_id=1, source_target_pairs={{0,1},{1,0},{2,3},{3,2},{4,5},{5,4},{6,7},{7,6},{8,9},{9,8},{10,11... | collective-permute-start | bytes 983048 | tf_op jit(solution)/shard_map/ppermute | solution.py:550
  96.5 11.0 %all-to-all-start.5 = ((f32[8,32,128]{2,1,0:T(8,128)}), f32[8,32,128]{2,1,0:T(8,128)S(1)}, u32[]{:S(2)}, u32[]{:S(2)}) async-start(f32[8,32,128]{2,1,0:T(8,128)} %shard_map.66), calls=%async_computation.5 | async-start | bytes 262144 | tf_op jit(solution)/shard_map/all_to_all | solution.py:544

commit v7 on v6

--- a/solution.py
+++ b/solution.py
@@ -187,7 +187,7 @@
     start_out[...] = start_ref[...].astype(BF16)
 
 
-def choose_kernel(moved_ref, own_ref, near_ref, out_hbm, places_ref, out_ref, sems):
+def choose_kernel(moved_ref, own_ref, near_ref, out_ref, places_ref):
     rep, block = lax.axis_index("rep"), lax.axis_index("blk")
     core = lax.rem(rep, 2)
     blocks, _, tile = out_ref.shape
@@ -210,11 +210,8 @@
             mine = own_ref[far, :, pl.ds(at, tile)]
             theirs = near_ref[far, :, pl.ds(at, tile)]
             out_ref[b, x * width : (x + 1) * width, :] = jnp.where(lax.rem(away, 2) == 0, mine, theirs)
-        pltpu.make_async_copy(out_ref.at[b], out_hbm.at[b], sems.at[b]).start()
 
     each(blocks, choose)
-    for b in range(blocks):
-        pltpu.make_async_copy(out_ref.at[b], out_hbm.at[b], sems.at[b]).wait()
 
 
 def find_slots(cols_ref, slots_ref, first_at):
@@ -572,8 +569,6 @@
         [],
         [],
         [moved, start_own, start_near],
-        [pltpu.VMEM((blocks, 2 * width, tile), BF16), pltpu.SemaphoreType.DMA((blocks,))],
-        [HBM, VMEM],
     )
     flat_tiles, moved = lax.optimization_barrier((flat_tiles, moved))
     tiles_own = jnp.stack([flat_tiles, swap_x(flat_tiles)])

time: 111 us -> 111 us (level)
  no operation moved by 1% of the time
where the time goes in v7:
time: 111 us; the launch traced here: 110 us
  waiting for transfers between devices  38.9 us (35%)
  blocking collectives  28.7 us (26%)
  Pallas kernels  21.9 us (20%)
  starting transfers between devices  19.8 us (18%)
    all_to_all x2, blocking collectives, across(): return lax.all_to_all(value, 'blk', split_axis=0, concat_axis=0, tiled=True)  28.7 us
    pallas_call x9, Pallas kernels, call(): pl.pallas_call(kernel, out_shape=outs, in_specs=[SMEM] * len(smem) + [HBM...  21.9 us
    all_to_all x3, waiting for transfers between devices, across(): return lax.all_to_all(value, 'blk', split_axis=0, concat_axis=0, tiled=True)  17.5 us
    all_to_all x3, starting transfers between devices, across(): return lax.all_to_all(value, 'blk', split_axis=0, concat_axis=0, tiled=True)  10.6 us
    all_to_all x1, waiting for transfers between devices, local(): lax.all_to_all(moved, ('blk', 'rep'), split_axis=0, concat_axis=0, tiled=...  10.5 us
    ppermute x3, waiting for transfers between devices, swap_x(): return lax.ppermute(value, 'rep', [(i, i ^ 2) for i in range(group)])  6.85 us
    all_to_all x1, starting transfers between devices, local(): lax.all_to_all(moved, ('blk', 'rep'), split_axis=0, concat_axis=0, tiled=...  4.92 us
    ppermute x3, starting transfers between devices, swap_x(): return lax.ppermute(value, 'rep', [(i, i ^ 2) for i in range(group)])  4.05 us
  transfers between devices with their start and end apart: 14, of which 11 were waited for; matrix products, arithmetic and copies ran while one was open for 0% of the time, Pallas kernels for 8%

profile of v7, /device:TPU:0, one launch (start us, length us, event | category | flops | bytes accessed | tf_op | source)
XLA Modules:
  0.0 110.4 jit_solution(8732564324283913629)
XLA Ops:
  0.6 1.9 %shard_map.59 = (bf16[32,40,128]{2,1,0:T(8,128)(2,1)}, bf16[64,2048]{1,0:T(8,128)(2,1)S(1)}) custom-call(s32[1,8]{1,0:T(1,128)} %rows_hbm.1, s32[1,8]{1,0:T(1,128)} %cols_hbm.1, bf16[32,32,128]{2,1,0:T(8,128)(2,1)} %bitcast.20, f32[64,2048]{1,0:T(8,128)} %bitcast.23), custom_call_target="tpu_custom_call" | custom-call | tf_op jit(solution)/shard_map/pallas_call | solution.py:515
  2.5 3.0 %collective-permute-start = (bf16[64,2048]{1,0:T(8,128)(2,1)S(1)}, bf16[64,2048]{1,0:T(8,128)(2,1)S(1)}, u32[]{:S(2)}, u32[]{:S(2)}) collective-permute-start(bf16[64,2048]{1,0:T(8,128)(2,1)S(1)} %get-tuple-element.14), channel_id=1, source_target_pairs={{0,2},{1,3},{2,0},{3,1},{4,6},{5,7},{6,4},{7,5},{8,10},{9,11},{10,... | collective-permute-start | bytes 786440 | tf_op jit(solution)/shard_map/ppermute | solution.py:544
  5.5 4.9 %all-to-all-start = ((bf16[32,40,128]{2,1,0:T(8,128)(2,1)}), bf16[32,40,128]{2,1,0:T(8,128)(2,1)S(1)}, u32[]{:S(2)}, u32[]{:S(2)}) async-start(bf16[32,40,128]{2,1,0:T(8,128)(2,1)} %get-tuple-element.13), calls=%async_computation | async-start | bytes 655360 | tf_op jit(solution)/shard_map/all_to_all | solution.py:565
  10.5 1.4 %collective-permute-done = bf16[64,2048]{1,0:T(8,128)(2,1)S(1)} collective-permute-done((bf16[64,2048]{1,0:T(8,128)(2,1)S(1)}, bf16[64,2048]{1,0:T(8,128)(2,1)S(1)}, u32[]{:S(2)}, u32[]{:S(2)}) %collective-permute-start) | collective-permute-done | bytes 262176 | tf_op jit(solution)/shard_map/ppermute | solution.py:544
  12.0 10.5 %all-to-all-done.moved_ref = bf16[32,40,128]{2,1,0:T(8,128)(2,1)S(1)} async-done(((bf16[32,40,128]{2,1,0:T(8,128)(2,1)}), bf16[32,40,128]{2,1,0:T(8,128)(2,1)S(1)}, u32[]{:S(2)}, u32[]{:S(2)}) %all-to-all-start) | async-done | bytes 327712 | tf_op jit(solution)/shard_map/all_to_all | solution.py:565
  23.7 3.6 %all-to-all-start.1 = ((bf16[8,128,128]{2,1,0:T(8,128)(2,1)}), bf16[8,128,128]{2,1,0:T(8,128)(2,1)S(1)}, u32[]{:S(2)}, u32[]{:S(2)}) async-start(bf16[8,128,128]{2,1,0:T(8,128)(2,1)} %get-tuple-element.18), calls=%async_computation.1 | async-start | bytes 524288 | tf_op jit(solution)/shard_map/all_to_all | solution.py:541
  27.3 2.9 %collective-permute-done.4 = bf16[8,128,128]{2,1,0:T(8,128)(2,1)S(1)} collective-permute-done((bf16[8,128,128]{2,1,0:T(8,128)(2,1)S(1)}, bf16[8,128,128]{2,1,0:T(8,128)(2,1)S(1)}, u32[]{:S(2)}, u32[]{:S(2)}) %collective-permute-start.4) | collective-permute-done | bytes 262176 | tf_op jit(solution)/shard_map/ppermute | solution.py:544
  30.3 6.3 %all-to-all-done.1.own_ref = bf16[8,128,128]{2,1,0:T(8,128)(2,1)S(1)} async-done(((bf16[8,128,128]{2,1,0:T(8,128)(2,1)}), bf16[8,128,128]{2,1,0:T(8,128)(2,1)S(1)}, u32[]{:S(2)}, u32[]{:S(2)}) %all-to-all-start.1) | async-done | bytes 262176 | tf_op jit(solution)/shard_map/all_to_all | solution.py:541
  38.2 2.4 %shard_map.62 = bf16[8,160,128]{2,1,0:T(8,128)(2,1)} custom-call(s32[4,8]{1,0:T(4,128)S(1)} %bitcast.18, bf16[2,8,128,128]{3,2,1,0:T(8,128)(2,1)S(1)} %pad_maximum_fusion.2.tiles_own, bf16[2,8,128,128]{3,2,1,0:T(8,128)(2,1)S(1)} %collective-permute-done.5.tiles_near, bf16[8,128,128]{2,1,0:T(8,128)(2,1)S(1)} %all-to-all-done.1.own_ref, ...), custom_call_target="tpu_custom_call" | custom-call | tf_op jit(solution)/shard_map/pallas_call | solution.py:515
  40.6 3.6 %all-to-all-start.2 = ((bf16[8,160,128]{2,1,0:T(8,128)(2,1)}), bf16[8,160,128]{2,1,0:T(8,128)(2,1)S(1)}, u32[]{:S(2)}, u32[]{:S(2)}) async-start(bf16[8,160,128]{2,1,0:T(8,128)(2,1)} %shard_map.62), calls=%async_computation.2 | async-start | bytes 655360 | tf_op jit(solution)/shard_map/all_to_all | solution.py:541
  44.2 2.6 %collective-permute-done.2 = bf16[32,40,128]{2,1,0:T(8,128)(2,1)S(1)} collective-permute-done((bf16[32,40,128]{2,1,0:T(8,128)(2,1)S(1)}, bf16[32,40,128]{2,1,0:T(8,128)(2,1)S(1)}, u32[]{:S(2)}, u32[]{:S(2)}) %collective-permute-start.2) | collective-permute-done | bytes 327712 | tf_op jit(solution)/shard_map/ppermute | solution.py:544
  46.9 7.9 %all-to-all-done.2.own_ref = bf16[8,160,128]{2,1,0:T(8,128)(2,1)S(1)} async-done(((bf16[8,160,128]{2,1,0:T(8,128)(2,1)}), bf16[8,160,128]{2,1,0:T(8,128)(2,1)S(1)}, u32[]{:S(2)}, u32[]{:S(2)}) %all-to-all-start.2) | async-done | bytes 327712 | tf_op jit(solution)/shard_map/all_to_all | solution.py:541
  55.1 1.4 %collective-permute-done.7.other_ref = bf16[8,160,128]{2,1,0:T(8,128)(2,1)S(1)} collective-permute-done((bf16[8,160,128]{2,1,0:T(8,128)(2,1)S(1)}, bf16[8,160,128]{2,1,0:T(8,128)(2,1)S(1)}, u32[]{:S(2)}, u32[]{:S(2)}) %collective-permute-start.7) | collective-permute-done | bytes 327712 | tf_op jit(solution)/shard_map/ppermute | solution.py:547
  56.5 2.9 %shard_map.63 = bf16[8,160,128]{2,1,0:T(8,128)(2,1)S(1)} custom-call(s32[8,4]{1,0:T(8,128)S(1)} %copy.9.cols_ref.cols_vmem, bf16[2,32,40,128]{3,2,1,0:T(8,128)(2,1)S(1)} %pad_maximum_fusion.tiles_own, bf16[2,32,40,128]{3,2,1,0:T(8,128)(2,1)S(1)} %collective-permute-done.3.tiles_near, bf16[8,160,128]{2,1,0:T(8,128)(2,1)S(1)} %all-to-all-done.2.own_ref, ...), custom_call_target="tpu_custom_call" | custom-call | tf_op jit(solution)/shard_map/pallas_call | solution.py:515
  59.4 14.6 %all_to_all.30.own_ref = bf16[8,160,128]{2,1,0:T(8,128)(2,1)S(1)} all-to-all(bf16[8,160,128]{2,1,0:T(8,128)(2,1)S(1)} %shard_map.63), channel_id=1, replica_groups=mesh['blk'=8,'rep'=4] {'blk'}, dimensions={0} | all-to-all | bytes 655360 | tf_op jit(solution)/shard_map/all_to_all | solution.py:541
  74.1 1.6 %collective-permute-done.8.other_ref = bf16[8,160,128]{2,1,0:T(8,128)(2,1)S(1)} collective-permute-done((bf16[8,160,128]{2,1,0:T(8,128)(2,1)S(1)}, bf16[8,160,128]{2,1,0:T(8,128)(2,1)S(1)}, u32[]{:S(2)}, u32[]{:S(2)}) %collective-permute-start.8) | collective-permute-done | bytes 327712 | tf_op jit(solution)/shard_map/ppermute | solution.py:547
  75.7 2.7 %shard_map.64 = (bf16[8,160,128]{2,1,0:T(8,128)(2,1)S(1)}, f32[64,2048]{1,0:T(8,128)S(1)}) custom-call(s32[4,8]{1,0:T(4,128)S(1)} %bitcast.19, bf16[2,8,128,128]{3,2,1,0:T(8,128)(2,1)S(1)} %pad_maximum_fusion.2.tiles_own, bf16[2,8,128,128]{3,2,1,0:T(8,128)(2,1)S(1)} %collective-permute-done.5.tiles_near, bf16[8,160,128]{2,1,0:T(8,128)(2,1)S(1)} %all_to_all.30.own_ref, ...), custom_call_target="tpu_custom_call" | custom-call | tf_op jit(solution)/shard_map/pallas_call | solution.py:515
  78.4 14.0 %all_to_all.31.own_ref = bf16[8,160,128]{2,1,0:T(8,128)(2,1)S(1)} all-to-all(bf16[8,160,128]{2,1,0:T(8,128)(2,1)S(1)} %get-tuple-element.19), channel_id=1, replica_groups=mesh['blk'=8,'rep'=4] {'blk'}, dimensions={0} | all-to-all | bytes 655360 | tf_op jit(solution)/shard_map/all_to_all | solution.py:541
  92.4 1.3 %shard_map.61.slots_ref.slots_vmem = s32[8,4]{1,0:T(8,128)S(1)} custom-call(s32[8,4]{1,0:T(8,128)S(1)} %copy.9.cols_ref.cols_vmem), custom_call_target="tpu_custom_call" | custom-call | tf_op jit(solution)/shard_map/pallas_call | solution.py:515
  94.0 2.3 %shard_map.66 = f32[8,32,128]{2,1,0:T(8,128)} custom-call(s32[8,4]{1,0:T(8,128)S(1)} %shard_map.61.slots_ref.slots_vmem, bf16[2,32,40,128]{3,2,1,0:T(8,128)(2,1)S(1)} %pad_maximum_fusion.tiles_own, bf16[2,32,40,128]{3,2,1,0:T(8,128)(2,1)S(1)} %collective-permute-done.3.tiles_near, bf16[8,160,128]{2,1,0:T(8,128)(2,1)S(1)} %all_to_all.31.own_ref, ...), custom_call_target="tpu_custom_call" | custom-call | tf_op jit(solution)/shard_map/pallas_call | solution.py:515
  96.3 3.4 %all-to-all-start.5 = ((f32[8,32,128]{2,1,0:T(8,128)}), f32[8,32,128]{2,1,0:T(8,128)S(1)}, u32[]{:S(2)}, u32[]{:S(2)}) async-start(f32[8,32,128]{2,1,0:T(8,128)} %shard_map.66), calls=%async_computation.5 | async-start | bytes 262144 | tf_op jit(solution)/shard_map/all_to_all | solution.py:541
  99.7 4.3 %shard_map.65 = (f32[64,2048]{1,0:T(8,128)}, bf16[128,2048]{1,0:T(8,128)(2,1)S(1)}, f32[64,64]{1,0:T(8,128)S(1)}) custom-call(s32[8,4]{1,0:T(8,128)S(1)} %copy.9.cols_ref.cols_vmem, s32[8,4]{1,0:T(8,128)S(1)} %shard_map.61.slots_ref.slots_vmem, bf16[2,32,40,128]{3,2,1,0:T(8,128)(2,1)S(1)} %pad_maximum_fusion.tiles_own, ...), custom_call_target="tpu_custom_call" | custom-call | tf_op jit(solution)/shard_map/pallas_call | solution.py:515
  104.0 3.3 %all-to-all-done.5.gram_ref = f32[8,32,128]{2,1,0:T(8,128)S(1)} async-done(((f32[8,32,128]{2,1,0:T(8,128)}), f32[8,32,128]{2,1,0:T(8,128)S(1)}, u32[]{:S(2)}, u32[]{:S(2)}) %all-to-all-start.5) | async-done | bytes 131104 | tf_op jit(solution)/shard_map/all_to_all | solution.py:541
  107.3 3.2 %shard_map.67 = f32[64,2048]{1,0:T(8,128)} custom-call(f32[8,32,128]{2,1,0:T(8,128)S(1)} %all-to-all-done.5.gram_ref, f32[64,64]{1,0:T(8,128)S(1)} %get-tuple-element.22.scale_ref, bf16[128,2048]{1,0:T(8,128)(2,1)S(1)} %get-tuple-element.23.parts_ref), custom_call_target="tpu_custom_call" | custom-call | tf_op jit(solution)/shard_map/pallas_call | solution.py:515
  (25 shorter events, 3.7 us)
Async XLA Ops:
  2.5 9.3 %collective-permute-start = (bf16[64,2048]{1,0:T(8,128)(2,1)S(1)}, bf16[64,2048]{1,0:T(8,128)(2,1)S(1)}, u32[]{:S(2)}, u32[]{:S(2)}) collective-permute-start(bf16[64,2048]{1,0:T(8,128)(2,1)S(1)} %get-tuple-element.14), channel_id=1, source_target_pairs={{0,2},{1,3},{2,0},{3,1},{4,6},{5,7},{6,4},{7,5},{8,10},{9,11},{10,... | collective-permute-start | bytes 786440 | tf_op jit(solution)/shard_map/ppermute | solution.py:544
  5.5 16.9 %all-to-all-start = ((bf16[32,40,128]{2,1,0:T(8,128)(2,1)}), bf16[32,40,128]{2,1,0:T(8,128)(2,1)S(1)}, u32[]{:S(2)}, u32[]{:S(2)}) async-start(bf16[32,40,128]{2,1,0:T(8,128)(2,1)} %get-tuple-element.13), calls=%async_computation | async-start | bytes 655360 | tf_op jit(solution)/shard_map/all_to_all | solution.py:565
  11.8 10.6 %copy-start = (bf16[1,8,128,128]{3,2,1,0:T(8,128)(2,1)S(1)}, bf16[1,8,128,128]{3,2,1,0:T(8,128)(2,1)}, u32[]{:S(2)}) copy-start(bf16[1,8,128,128]{3,2,1,0:T(8,128)(2,1)} %param.4) | copy-start | bytes 786436
  11.9 10.8 %collective-permute-start.1 = (bf16[2,64,2048]{2,1,0:T(8,128)(2,1)S(1)}, bf16[2,64,2048]{2,1,0:T(8,128)(2,1)S(1)}, u32[]{:S(2)}, u32[]{:S(2)}) collective-permute-start(bf16[2,64,2048]{2,1,0:T(8,128)(2,1)S(1)} %pad_maximum_fusion.1.own_ref), channel_id=1, source_target_pairs={{0,1},{1,0},{2,3},{3,2},{4,5},{5,4},{6,7},{7,6},{8,9},{9,8},{10,11... | collective-permute-start | bytes 1572872 | tf_op jit(solution)/shard_map/ppermute | solution.py:547
  22.5 7.8 %collective-permute-start.4 = (bf16[8,128,128]{2,1,0:T(8,128)(2,1)S(1)}, bf16[8,128,128]{2,1,0:T(8,128)(2,1)S(1)}, u32[]{:S(2)}, u32[]{:S(2)}) collective-permute-start(bf16[8,128,128]{2,1,0:T(8,128)(2,1)S(1)} %bitcast.21), channel_id=1, source_target_pairs={{0,2},{1,3},{2,0},{3,1},{4,6},{5,7},{6,4},{7,5},{8,10},{9,11},{10,... | collective-permute-start | bytes 786440 | tf_op jit(solution)/shard_map/ppermute | solution.py:544
  23.7 13.0 %all-to-all-start.1 = ((bf16[8,128,128]{2,1,0:T(8,128)(2,1)}), bf16[8,128,128]{2,1,0:T(8,128)(2,1)S(1)}, u32[]{:S(2)}, u32[]{:S(2)}) async-start(bf16[8,128,128]{2,1,0:T(8,128)(2,1)} %get-tuple-element.18), calls=%async_computation.1 | async-start | bytes 524288 | tf_op jit(solution)/shard_map/all_to_all | solution.py:541
  30.3 7.2 %collective-permute-start.5 = (bf16[2,8,128,128]{3,2,1,0:T(8,128)(2,1)S(1)}, bf16[2,8,128,128]{3,2,1,0:T(8,128)(2,1)S(1)}, u32[]{:S(2)}, u32[]{:S(2)}) collective-permute-start(bf16[2,8,128,128]{3,2,1,0:T(8,128)(2,1)S(1)} %pad_maximum_fusion.2.tiles_own), channel_id=1, source_target_pairs={{0,1},{1,0},{2,3},{3,2},{4,5},{5,4},{6,7},{7,6},{8,9},{9,8},{10,11... | collective-permute-start | bytes 1572872 | tf_op jit(solution)/shard_map/ppermute | solution.py:547
  36.7 1.5 %collective-permute-start.6 = (bf16[8,128,128]{2,1,0:T(8,128)(2,1)S(1)}, bf16[8,128,128]{2,1,0:T(8,128)(2,1)S(1)}, u32[]{:S(2)}, u32[]{:S(2)}) collective-permute-start(bf16[8,128,128]{2,1,0:T(8,128)(2,1)S(1)} %all-to-all-done.1.own_ref), channel_id=1, source_target_pairs={{0,1},{1,0},{2,3},{3,2},{4,5},{5,4},{6,7},{7,6},{8,9},{9,8},{10,11... | collective-permute-start | bytes 786440 | tf_op jit(solution)/shard_map/ppermute | solution.py:547
  36.7 10.1 %collective-permute-start.2 = (bf16[32,40,128]{2,1,0:T(8,128)(2,1)S(1)}, bf16[32,40,128]{2,1,0:T(8,128)(2,1)S(1)}, u32[]{:S(2)}, u32[]{:S(2)}) collective-permute-start(bf16[32,40,128]{2,1,0:T(8,128)(2,1)S(1)} %all-to-all-done.moved_ref), channel_id=1, source_target_pairs={{0,2},{1,3},{2,0},{3,1},{4,6},{5,7},{6,4},{7,5},{8,10},{9,11},{10,... | collective-permute-start | bytes 983048 | tf_op jit(solution)/shard_map/ppermute | solution.py:544
  40.6 14.2 %all-to-all-start.2 = ((bf16[8,160,128]{2,1,0:T(8,128)(2,1)}), bf16[8,160,128]{2,1,0:T(8,128)(2,1)S(1)}, u32[]{:S(2)}, u32[]{:S(2)}) async-start(bf16[8,160,128]{2,1,0:T(8,128)(2,1)} %shard_map.62), calls=%async_computation.2 | async-start | bytes 655360 | tf_op jit(solution)/shard_map/all_to_all | solution.py:541
  46.9 8.3 %collective-permute-start.3 = (bf16[2,32,40,128]{3,2,1,0:T(8,128)(2,1)S(1)}, bf16[2,32,40,128]{3,2,1,0:T(8,128)(2,1)S(1)}, u32[]{:S(2)}, u32[]{:S(2)}) collective-permute-start(bf16[2,32,40,128]{3,2,1,0:T(8,128)(2,1)S(1)} %pad_maximum_fusion.tiles_own), channel_id=1, source_target_pairs={{0,1},{1,0},{2,3},{3,2},{4,5},{5,4},{6,7},{7,6},{8,9},{9,8},{10,11... | collective-permute-start | bytes 1966088 | tf_op jit(solution)/shard_map/ppermute | solution.py:547
  54.9 1.6 %collective-permute-start.7 = (bf16[8,160,128]{2,1,0:T(8,128)(2,1)S(1)}, bf16[8,160,128]{2,1,0:T(8,128)(2,1)S(1)}, u32[]{:S(2)}, u32[]{:S(2)}) collective-permute-start(bf16[8,160,128]{2,1,0:T(8,128)(2,1)S(1)} %all-to-all-done.2.own_ref), channel_id=1, source_target_pairs={{0,1},{1,0},{2,3},{3,2},{4,5},{5,4},{6,7},{7,6},{8,9},{9,8},{10,11... | collective-permute-start | bytes 983048 | tf_op jit(solution)/shard_map/ppermute | solution.py:547
  74.1 1.6 %collective-permute-start.8 = (bf16[8,160,128]{2,1,0:T(8,128)(2,1)S(1)}, bf16[8,160,128]{2,1,0:T(8,128)(2,1)S(1)}, u32[]{:S(2)}, u32[]{:S(2)}) collective-permute-start(bf16[8,160,128]{2,1,0:T(8,128)(2,1)S(1)} %all_to_all.30.own_ref), channel_id=1, source_target_pairs={{0,1},{1,0},{2,3},{3,2},{4,5},{5,4},{6,7},{7,6},{8,9},{9,8},{10,11... | collective-permute-start | bytes 983048 | tf_op jit(solution)/shard_map/ppermute | solution.py:547
  92.4 1.6 %collective-permute-start.9 = (bf16[8,160,128]{2,1,0:T(8,128)(2,1)S(1)}, bf16[8,160,128]{2,1,0:T(8,128)(2,1)S(1)}, u32[]{:S(2)}, u32[]{:S(2)}) collective-permute-start(bf16[8,160,128]{2,1,0:T(8,128)(2,1)S(1)} %all_to_all.31.own_ref), channel_id=1, source_target_pairs={{0,1},{1,0},{2,3},{3,2},{4,5},{5,4},{6,7},{7,6},{8,9},{9,8},{10,11... | collective-permute-start | bytes 983048 | tf_op jit(solution)/shard_map/ppermute | solution.py:547
  96.3 11.0 %all-to-all-start.5 = ((f32[8,32,128]{2,1,0:T(8,128)}), f32[8,32,128]{2,1,0:T(8,128)S(1)}, u32[]{:S(2)}, u32[]{:S(2)}) async-start(f32[8,32,128]{2,1,0:T(8,128)} %shard_map.66), calls=%async_computation.5 | async-start | bytes 262144 | tf_op jit(solution)/shard_map/all_to_all | solution.py:541

commit v8 on v7

--- a/solution.py
+++ b/solution.py
@@ -494,9 +494,9 @@
     run(eliminate(work, spread))
     high, low = two_parts(work[:, 0:width])
     scale = jnp.concatenate([high, high], axis=1)
-    chunk = right.shape[1] // 4
+    chunk = right.shape[1] // 8
     copies = []
-    for n in range(4):
+    for n in range(8):
         at = pl.ds(n * chunk, chunk)
         right[:, at] = dot(scale, parts_ref[:, at], NN) + dot(low, parts_ref[0:width, at], NN)
         copies.append(pltpu.make_async_copy(right.at[:, at], right_hbm.at[:, at], sems.at[n]))
@@ -659,7 +659,7 @@
         [],
         [],
         [across(gram), left_scale, parts],
-        [work, spread, pltpu.VMEM((width, share), F32), pltpu.SemaphoreType.DMA((4,))],
+        [work, spread, pltpu.VMEM((width, share), F32), pltpu.SemaphoreType.DMA((8,))],
         [HBM],
     )
     return (left.T, right.T)

time: 111 us -> 111 us (level)
  no operation moved by 1% of the time
where the time goes in v8:
time: 111 us; the launch traced here: 110 us
  waiting for transfers between devices  38.9 us (35%)
  blocking collectives  28.7 us (26%)
  Pallas kernels  22 us (20%)
  starting transfers between devices  19.8 us (18%)
    all_to_all x2, blocking collectives, across(): return lax.all_to_all(value, 'blk', split_axis=0, concat_axis=0, tiled=True)  28.7 us
    pallas_call x9, Pallas kernels, call(): pl.pallas_call(kernel, out_shape=outs, in_specs=[SMEM] * len(smem) + [HBM...  22 us
    all_to_all x3, waiting for transfers between devices, across(): return lax.all_to_all(value, 'blk', split_axis=0, concat_axis=0, tiled=True)  17.5 us
    all_to_all x3, starting transfers between devices, across(): return lax.all_to_all(value, 'blk', split_axis=0, concat_axis=0, tiled=True)  10.6 us
    all_to_all x1, waiting for transfers between devices, local(): lax.all_to_all(moved, ('blk', 'rep'), split_axis=0, concat_axis=0, tiled=...  10.5 us
    ppermute x3, waiting for transfers between devices, swap_x(): return lax.ppermute(value, 'rep', [(i, i ^ 2) for i in range(group)])  6.85 us
    all_to_all x1, starting transfers between devices, local(): lax.all_to_all(moved, ('blk', 'rep'), split_axis=0, concat_axis=0, tiled=...  4.92 us
    ppermute x3, starting transfers between devices, swap_x(): return lax.ppermute(value, 'rep', [(i, i ^ 2) for i in range(group)])  4.05 us
  transfers between devices with their start and end apart: 14, of which 11 were waited for; matrix products, arithmetic and copies ran while one was open for 0% of the time, Pallas kernels for 8%

profile of v8, /device:TPU:0, one launch (start us, length us, event | category | flops | bytes accessed | tf_op | source)
XLA Modules:
  0.0 110.5 jit_solution(7495948448812481042)
XLA Ops:
  0.6 1.9 %shard_map.59 = (bf16[32,40,128]{2,1,0:T(8,128)(2,1)}, bf16[64,2048]{1,0:T(8,128)(2,1)S(1)}) custom-call(s32[1,8]{1,0:T(1,128)} %rows_hbm.1, s32[1,8]{1,0:T(1,128)} %cols_hbm.1, bf16[32,32,128]{2,1,0:T(8,128)(2,1)} %bitcast.20, f32[64,2048]{1,0:T(8,128)} %bitcast.23), custom_call_target="tpu_custom_call" | custom-call | tf_op jit(solution)/shard_map/pallas_call | solution.py:515
  2.5 3.0 %collective-permute-start = (bf16[64,2048]{1,0:T(8,128)(2,1)S(1)}, bf16[64,2048]{1,0:T(8,128)(2,1)S(1)}, u32[]{:S(2)}, u32[]{:S(2)}) collective-permute-start(bf16[64,2048]{1,0:T(8,128)(2,1)S(1)} %get-tuple-element.14), channel_id=1, source_target_pairs={{0,2},{1,3},{2,0},{3,1},{4,6},{5,7},{6,4},{7,5},{8,10},{9,11},{10,... | collective-permute-start | bytes 786440 | tf_op jit(solution)/shard_map/ppermute | solution.py:544
  5.5 4.9 %all-to-all-start = ((bf16[32,40,128]{2,1,0:T(8,128)(2,1)}), bf16[32,40,128]{2,1,0:T(8,128)(2,1)S(1)}, u32[]{:S(2)}, u32[]{:S(2)}) async-start(bf16[32,40,128]{2,1,0:T(8,128)(2,1)} %get-tuple-element.13), calls=%async_computation | async-start | bytes 655360 | tf_op jit(solution)/shard_map/all_to_all | solution.py:565
  10.5 1.4 %collective-permute-done = bf16[64,2048]{1,0:T(8,128)(2,1)S(1)} collective-permute-done((bf16[64,2048]{1,0:T(8,128)(2,1)S(1)}, bf16[64,2048]{1,0:T(8,128)(2,1)S(1)}, u32[]{:S(2)}, u32[]{:S(2)}) %collective-permute-start) | collective-permute-done | bytes 262176 | tf_op jit(solution)/shard_map/ppermute | solution.py:544
  12.0 10.5 %all-to-all-done.moved_ref = bf16[32,40,128]{2,1,0:T(8,128)(2,1)S(1)} async-done(((bf16[32,40,128]{2,1,0:T(8,128)(2,1)}), bf16[32,40,128]{2,1,0:T(8,128)(2,1)S(1)}, u32[]{:S(2)}, u32[]{:S(2)}) %all-to-all-start) | async-done | bytes 327712 | tf_op jit(solution)/shard_map/all_to_all | solution.py:565
  23.7 3.6 %all-to-all-start.1 = ((bf16[8,128,128]{2,1,0:T(8,128)(2,1)}), bf16[8,128,128]{2,1,0:T(8,128)(2,1)S(1)}, u32[]{:S(2)}, u32[]{:S(2)}) async-start(bf16[8,128,128]{2,1,0:T(8,128)(2,1)} %get-tuple-element.18), calls=%async_computation.1 | async-start | bytes 524288 | tf_op jit(solution)/shard_map/all_to_all | solution.py:541
  27.3 2.9 %collective-permute-done.4 = bf16[8,128,128]{2,1,0:T(8,128)(2,1)S(1)} collective-permute-done((bf16[8,128,128]{2,1,0:T(8,128)(2,1)S(1)}, bf16[8,128,128]{2,1,0:T(8,128)(2,1)S(1)}, u32[]{:S(2)}, u32[]{:S(2)}) %collective-permute-start.4) | collective-permute-done | bytes 262176 | tf_op jit(solution)/shard_map/ppermute | solution.py:544
  30.3 6.3 %all-to-all-done.1.own_ref = bf16[8,128,128]{2,1,0:T(8,128)(2,1)S(1)} async-done(((bf16[8,128,128]{2,1,0:T(8,128)(2,1)}), bf16[8,128,128]{2,1,0:T(8,128)(2,1)S(1)}, u32[]{:S(2)}, u32[]{:S(2)}) %all-to-all-start.1) | async-done | bytes 262176 | tf_op jit(solution)/shard_map/all_to_all | solution.py:541
  38.2 2.4 %shard_map.62 = bf16[8,160,128]{2,1,0:T(8,128)(2,1)} custom-call(s32[4,8]{1,0:T(4,128)S(1)} %bitcast.18, bf16[2,8,128,128]{3,2,1,0:T(8,128)(2,1)S(1)} %pad_maximum_fusion.2.tiles_own, bf16[2,8,128,128]{3,2,1,0:T(8,128)(2,1)S(1)} %collective-permute-done.5.tiles_near, bf16[8,128,128]{2,1,0:T(8,128)(2,1)S(1)} %all-to-all-done.1.own_ref, ...), custom_call_target="tpu_custom_call" | custom-call | tf_op jit(solution)/shard_map/pallas_call | solution.py:515
  40.6 3.6 %all-to-all-start.2 = ((bf16[8,160,128]{2,1,0:T(8,128)(2,1)}), bf16[8,160,128]{2,1,0:T(8,128)(2,1)S(1)}, u32[]{:S(2)}, u32[]{:S(2)}) async-start(bf16[8,160,128]{2,1,0:T(8,128)(2,1)} %shard_map.62), calls=%async_computation.2 | async-start | bytes 655360 | tf_op jit(solution)/shard_map/all_to_all | solution.py:541
  44.2 2.6 %collective-permute-done.2 = bf16[32,40,128]{2,1,0:T(8,128)(2,1)S(1)} collective-permute-done((bf16[32,40,128]{2,1,0:T(8,128)(2,1)S(1)}, bf16[32,40,128]{2,1,0:T(8,128)(2,1)S(1)}, u32[]{:S(2)}, u32[]{:S(2)}) %collective-permute-start.2) | collective-permute-done | bytes 327712 | tf_op jit(solution)/shard_map/ppermute | solution.py:544
  46.9 7.9 %all-to-all-done.2.own_ref = bf16[8,160,128]{2,1,0:T(8,128)(2,1)S(1)} async-done(((bf16[8,160,128]{2,1,0:T(8,128)(2,1)}), bf16[8,160,128]{2,1,0:T(8,128)(2,1)S(1)}, u32[]{:S(2)}, u32[]{:S(2)}) %all-to-all-start.2) | async-done | bytes 327712 | tf_op jit(solution)/shard_map/all_to_all | solution.py:541
  55.1 1.4 %collective-permute-done.7.other_ref = bf16[8,160,128]{2,1,0:T(8,128)(2,1)S(1)} collective-permute-done((bf16[8,160,128]{2,1,0:T(8,128)(2,1)S(1)}, bf16[8,160,128]{2,1,0:T(8,128)(2,1)S(1)}, u32[]{:S(2)}, u32[]{:S(2)}) %collective-permute-start.7) | collective-permute-done | bytes 327712 | tf_op jit(solution)/shard_map/ppermute | solution.py:547
  56.5 2.9 %shard_map.63 = bf16[8,160,128]{2,1,0:T(8,128)(2,1)S(1)} custom-call(s32[8,4]{1,0:T(8,128)S(1)} %copy.9.cols_ref.cols_vmem, bf16[2,32,40,128]{3,2,1,0:T(8,128)(2,1)S(1)} %pad_maximum_fusion.tiles_own, bf16[2,32,40,128]{3,2,1,0:T(8,128)(2,1)S(1)} %collective-permute-done.3.tiles_near, bf16[8,160,128]{2,1,0:T(8,128)(2,1)S(1)} %all-to-all-done.2.own_ref, ...), custom_call_target="tpu_custom_call" | custom-call | tf_op jit(solution)/shard_map/pallas_call | solution.py:515
  59.4 14.6 %all_to_all.30.own_ref = bf16[8,160,128]{2,1,0:T(8,128)(2,1)S(1)} all-to-all(bf16[8,160,128]{2,1,0:T(8,128)(2,1)S(1)} %shard_map.63), channel_id=1, replica_groups=mesh['blk'=8,'rep'=4] {'blk'}, dimensions={0} | all-to-all | bytes 655360 | tf_op jit(solution)/shard_map/all_to_all | solution.py:541
  74.1 1.6 %collective-permute-done.8.other_ref = bf16[8,160,128]{2,1,0:T(8,128)(2,1)S(1)} collective-permute-done((bf16[8,160,128]{2,1,0:T(8,128)(2,1)S(1)}, bf16[8,160,128]{2,1,0:T(8,128)(2,1)S(1)}, u32[]{:S(2)}, u32[]{:S(2)}) %collective-permute-start.8) | collective-permute-done | bytes 327712 | tf_op jit(solution)/shard_map/ppermute | solution.py:547
  75.7 2.7 %shard_map.64 = (bf16[8,160,128]{2,1,0:T(8,128)(2,1)S(1)}, f32[64,2048]{1,0:T(8,128)S(1)}) custom-call(s32[4,8]{1,0:T(4,128)S(1)} %bitcast.19, bf16[2,8,128,128]{3,2,1,0:T(8,128)(2,1)S(1)} %pad_maximum_fusion.2.tiles_own, bf16[2,8,128,128]{3,2,1,0:T(8,128)(2,1)S(1)} %collective-permute-done.5.tiles_near, bf16[8,160,128]{2,1,0:T(8,128)(2,1)S(1)} %all_to_all.30.own_ref, ...), custom_call_target="tpu_custom_call" | custom-call | tf_op jit(solution)/shard_map/pallas_call | solution.py:515
  78.4 14.0 %all_to_all.31.own_ref = bf16[8,160,128]{2,1,0:T(8,128)(2,1)S(1)} all-to-all(bf16[8,160,128]{2,1,0:T(8,128)(2,1)S(1)} %get-tuple-element.19), channel_id=1, replica_groups=mesh['blk'=8,'rep'=4] {'blk'}, dimensions={0} | all-to-all | bytes 655360 | tf_op jit(solution)/shard_map/all_to_all | solution.py:541
  92.4 1.3 %shard_map.61.slots_ref.slots_vmem = s32[8,4]{1,0:T(8,128)S(1)} custom-call(s32[8,4]{1,0:T(8,128)S(1)} %copy.9.cols_ref.cols_vmem), custom_call_target="tpu_custom_call" | custom-call | tf_op jit(solution)/shard_map/pallas_call | solution.py:515
  94.0 2.3 %shard_map.66 = f32[8,32,128]{2,1,0:T(8,128)} custom-call(s32[8,4]{1,0:T(8,128)S(1)} %shard_map.61.slots_ref.slots_vmem, bf16[2,32,40,128]{3,2,1,0:T(8,128)(2,1)S(1)} %pad_maximum_fusion.tiles_own, bf16[2,32,40,128]{3,2,1,0:T(8,128)(2,1)S(1)} %collective-permute-done.3.tiles_near, bf16[8,160,128]{2,1,0:T(8,128)(2,1)S(1)} %all_to_all.31.own_ref, ...), custom_call_target="tpu_custom_call" | custom-call | tf_op jit(solution)/shard_map/pallas_call | solution.py:515
  96.3 3.4 %all-to-all-start.5 = ((f32[8,32,128]{2,1,0:T(8,128)}), f32[8,32,128]{2,1,0:T(8,128)S(1)}, u32[]{:S(2)}, u32[]{:S(2)}) async-start(f32[8,32,128]{2,1,0:T(8,128)} %shard_map.66), calls=%async_computation.5 | async-start | bytes 262144 | tf_op jit(solution)/shard_map/all_to_all | solution.py:541
  99.7 4.3 %shard_map.65 = (f32[64,2048]{1,0:T(8,128)}, bf16[128,2048]{1,0:T(8,128)(2,1)S(1)}, f32[64,64]{1,0:T(8,128)S(1)}) custom-call(s32[8,4]{1,0:T(8,128)S(1)} %copy.9.cols_ref.cols_vmem, s32[8,4]{1,0:T(8,128)S(1)} %shard_map.61.slots_ref.slots_vmem, bf16[2,32,40,128]{3,2,1,0:T(8,128)(2,1)S(1)} %pad_maximum_fusion.tiles_own, ...), custom_call_target="tpu_custom_call" | custom-call | tf_op jit(solution)/shard_map/pallas_call | solution.py:515
  104.0 3.3 %all-to-all-done.5.gram_ref = f32[8,32,128]{2,1,0:T(8,128)S(1)} async-done(((f32[8,32,128]{2,1,0:T(8,128)}), f32[8,32,128]{2,1,0:T(8,128)S(1)}, u32[]{:S(2)}, u32[]{:S(2)}) %all-to-all-start.5) | async-done | bytes 131104 | tf_op jit(solution)/shard_map/all_to_all | solution.py:541
  107.3 3.2 %shard_map.67 = f32[64,2048]{1,0:T(8,128)} custom-call(f32[8,32,128]{2,1,0:T(8,128)S(1)} %all-to-all-done.5.gram_ref, f32[64,64]{1,0:T(8,128)S(1)} %get-tuple-element.22.scale_ref, bf16[128,2048]{1,0:T(8,128)(2,1)S(1)} %get-tuple-element.23.parts_ref), custom_call_target="tpu_custom_call" | custom-call | tf_op jit(solution)/shard_map/pallas_call | solution.py:515
  (25 shorter events, 3.7 us)
Async XLA Ops:
  2.5 9.3 %collective-permute-start = (bf16[64,2048]{1,0:T(8,128)(2,1)S(1)}, bf16[64,2048]{1,0:T(8,128)(2,1)S(1)}, u32[]{:S(2)}, u32[]{:S(2)}) collective-permute-start(bf16[64,2048]{1,0:T(8,128)(2,1)S(1)} %get-tuple-element.14), channel_id=1, source_target_pairs={{0,2},{1,3},{2,0},{3,1},{4,6},{5,7},{6,4},{7,5},{8,10},{9,11},{10,... | collective-permute-start | bytes 786440 | tf_op jit(solution)/shard_map/ppermute | solution.py:544
  5.5 16.9 %all-to-all-start = ((bf16[32,40,128]{2,1,0:T(8,128)(2,1)}), bf16[32,40,128]{2,1,0:T(8,128)(2,1)S(1)}, u32[]{:S(2)}, u32[]{:S(2)}) async-start(bf16[32,40,128]{2,1,0:T(8,128)(2,1)} %get-tuple-element.13), calls=%async_computation | async-start | bytes 655360 | tf_op jit(solution)/shard_map/all_to_all | solution.py:565
  11.8 10.6 %copy-start = (bf16[1,8,128,128]{3,2,1,0:T(8,128)(2,1)S(1)}, bf16[1,8,128,128]{3,2,1,0:T(8,128)(2,1)}, u32[]{:S(2)}) copy-start(bf16[1,8,128,128]{3,2,1,0:T(8,128)(2,1)} %param.4) | copy-start | bytes 786436
  11.9 10.8 %collective-permute-start.1 = (bf16[2,64,2048]{2,1,0:T(8,128)(2,1)S(1)}, bf16[2,64,2048]{2,1,0:T(8,128)(2,1)S(1)}, u32[]{:S(2)}, u32[]{:S(2)}) collective-permute-start(bf16[2,64,2048]{2,1,0:T(8,128)(2,1)S(1)} %pad_maximum_fusion.1.own_ref), channel_id=1, source_target_pairs={{0,1},{1,0},{2,3},{3,2},{4,5},{5,4},{6,7},{7,6},{8,9},{9,8},{10,11... | collective-permute-start | bytes 1572872 | tf_op jit(solution)/shard_map/ppermute | solution.py:547
  22.5 7.8 %collective-permute-start.4 = (bf16[8,128,128]{2,1,0:T(8,128)(2,1)S(1)}, bf16[8,128,128]{2,1,0:T(8,128)(2,1)S(1)}, u32[]{:S(2)}, u32[]{:S(2)}) collective-permute-start(bf16[8,128,128]{2,1,0:T(8,128)(2,1)S(1)} %bitcast.21), channel_id=1, source_target_pairs={{0,2},{1,3},{2,0},{3,1},{4,6},{5,7},{6,4},{7,5},{8,10},{9,11},{10,... | collective-permute-start | bytes 786440 | tf_op jit(solution)/shard_map/ppermute | solution.py:544
  23.7 13.0 %all-to-all-start.1 = ((bf16[8,128,128]{2,1,0:T(8,128)(2,1)}), bf16[8,128,128]{2,1,0:T(8,128)(2,1)S(1)}, u32[]{:S(2)}, u32[]{:S(2)}) async-start(bf16[8,128,128]{2,1,0:T(8,128)(2,1)} %get-tuple-element.18), calls=%async_computation.1 | async-start | bytes 524288 | tf_op jit(solution)/shard_map/all_to_all | solution.py:541
  30.3 7.2 %collective-permute-start.5 = (bf16[2,8,128,128]{3,2,1,0:T(8,128)(2,1)S(1)}, bf16[2,8,128,128]{3,2,1,0:T(8,128)(2,1)S(1)}, u32[]{:S(2)}, u32[]{:S(2)}) collective-permute-start(bf16[2,8,128,128]{3,2,1,0:T(8,128)(2,1)S(1)} %pad_maximum_fusion.2.tiles_own), channel_id=1, source_target_pairs={{0,1},{1,0},{2,3},{3,2},{4,5},{5,4},{6,7},{7,6},{8,9},{9,8},{10,11... | collective-permute-start | bytes 1572872 | tf_op jit(solution)/shard_map/ppermute | solution.py:547
  36.7 1.5 %collective-permute-start.6 = (bf16[8,128,128]{2,1,0:T(8,128)(2,1)S(1)}, bf16[8,128,128]{2,1,0:T(8,128)(2,1)S(1)}, u32[]{:S(2)}, u32[]{:S(2)}) collective-permute-start(bf16[8,128,128]{2,1,0:T(8,128)(2,1)S(1)} %all-to-all-done.1.own_ref), channel_id=1, source_target_pairs={{0,1},{1,0},{2,3},{3,2},{4,5},{5,4},{6,7},{7,6},{8,9},{9,8},{10,11... | collective-permute-start | bytes 786440 | tf_op jit(solution)/shard_map/ppermute | solution.py:547
  36.7 10.1 %collective-permute-start.2 = (bf16[32,40,128]{2,1,0:T(8,128)(2,1)S(1)}, bf16[32,40,128]{2,1,0:T(8,128)(2,1)S(1)}, u32[]{:S(2)}, u32[]{:S(2)}) collective-permute-start(bf16[32,40,128]{2,1,0:T(8,128)(2,1)S(1)} %all-to-all-done.moved_ref), channel_id=1, source_target_pairs={{0,2},{1,3},{2,0},{3,1},{4,6},{5,7},{6,4},{7,5},{8,10},{9,11},{10,... | collective-permute-start | bytes 983048 | tf_op jit(solution)/shard_map/ppermute | solution.py:544
  40.6 14.2 %all-to-all-start.2 = ((bf16[8,160,128]{2,1,0:T(8,128)(2,1)}), bf16[8,160,128]{2,1,0:T(8,128)(2,1)S(1)}, u32[]{:S(2)}, u32[]{:S(2)}) async-start(bf16[8,160,128]{2,1,0:T(8,128)(2,1)} %shard_map.62), calls=%async_computation.2 | async-start | bytes 655360 | tf_op jit(solution)/shard_map/all_to_all | solution.py:541
  46.9 8.3 %collective-permute-start.3 = (bf16[2,32,40,128]{3,2,1,0:T(8,128)(2,1)S(1)}, bf16[2,32,40,128]{3,2,1,0:T(8,128)(2,1)S(1)}, u32[]{:S(2)}, u32[]{:S(2)}) collective-permute-start(bf16[2,32,40,128]{3,2,1,0:T(8,128)(2,1)S(1)} %pad_maximum_fusion.tiles_own), channel_id=1, source_target_pairs={{0,1},{1,0},{2,3},{3,2},{4,5},{5,4},{6,7},{7,6},{8,9},{9,8},{10,11... | collective-permute-start | bytes 1966088 | tf_op jit(solution)/shard_map/ppermute | solution.py:547
  54.9 1.6 %collective-permute-start.7 = (bf16[8,160,128]{2,1,0:T(8,128)(2,1)S(1)}, bf16[8,160,128]{2,1,0:T(8,128)(2,1)S(1)}, u32[]{:S(2)}, u32[]{:S(2)}) collective-permute-start(bf16[8,160,128]{2,1,0:T(8,128)(2,1)S(1)} %all-to-all-done.2.own_ref), channel_id=1, source_target_pairs={{0,1},{1,0},{2,3},{3,2},{4,5},{5,4},{6,7},{7,6},{8,9},{9,8},{10,11... | collective-permute-start | bytes 983048 | tf_op jit(solution)/shard_map/ppermute | solution.py:547
  74.1 1.6 %collective-permute-start.8 = (bf16[8,160,128]{2,1,0:T(8,128)(2,1)S(1)}, bf16[8,160,128]{2,1,0:T(8,128)(2,1)S(1)}, u32[]{:S(2)}, u32[]{:S(2)}) collective-permute-start(bf16[8,160,128]{2,1,0:T(8,128)(2,1)S(1)} %all_to_all.30.own_ref), channel_id=1, source_target_pairs={{0,1},{1,0},{2,3},{3,2},{4,5},{5,4},{6,7},{7,6},{8,9},{9,8},{10,11... | collective-permute-start | bytes 983048 | tf_op jit(solution)/shard_map/ppermute | solution.py:547
  92.4 1.6 %collective-permute-start.9 = (bf16[8,160,128]{2,1,0:T(8,128)(2,1)S(1)}, bf16[8,160,128]{2,1,0:T(8,128)(2,1)S(1)}, u32[]{:S(2)}, u32[]{:S(2)}) collective-permute-start(bf16[8,160,128]{2,1,0:T(8,128)(2,1)S(1)} %all_to_all.31.own_ref), channel_id=1, source_target_pairs={{0,1},{1,0},{2,3},{3,2},{4,5},{5,4},{6,7},{7,6},{8,9},{9,8},{10,11... | collective-permute-start | bytes 983048 | tf_op jit(solution)/shard_map/ppermute | solution.py:547
  96.3 11.0 %all-to-all-start.5 = ((f32[8,32,128]{2,1,0:T(8,128)}), f32[8,32,128]{2,1,0:T(8,128)S(1)}, u32[]{:S(2)}, u32[]{:S(2)}) async-start(f32[8,32,128]{2,1,0:T(8,128)} %shard_map.66), calls=%async_computation.5 | async-start | bytes 262144 | tf_op jit(solution)/shard_map/all_to_all | solution.py:541
